TPU v7x, 32 devices: a whole 2x2x4 slice. The times are simulated.
32 devices in a mesh: dp: 8 (over z, x), seq: 4 (over y, core).
Axes of the slice: x: 2, y: 2, z: 4, core: 2. Of those that a mesh axis runs over, the one named last changes fastest.
Arguments:
- doc_tokens: bfloat16 [32, 1024, 768], P('dp', 'seq'), may hold values from -6 to 6
- queries: bfloat16 [512, 32, 768], P(('dp', 'seq')), may hold values from -6 to 6
- doc_cot: bfloat16 [32, 1024, 768], P('dp', 'seq'), may hold values from -6 to 6
- query_cot: bfloat16 [512, 32, 768], P(('dp', 'seq')), may hold values from -6 to 6
- q_weight: bfloat16 [768, 768], P(('dp', 'seq')), may hold values from -0.0546875 to 0.0546875
- kv_weight: bfloat16 [768, 1536], P(('dp', 'seq')), may hold values from -0.21875 to 0.21875
- out_weight: bfloat16 [768, 768], P(('dp', 'seq')), may hold values from -1.5 to 1.5
- up_weight: bfloat16 [768, 3072], P(('dp', 'seq')), may hold values from -0.21875 to 0.21875
- down_weight: bfloat16 [3072, 768], P(('dp', 'seq')), may hold values from -0.109375 to 0.109375
- attn_gain: float32 [768], replicated, may hold values from 0.5 to 1.5
- ff_gain: float32 [768], replicated, may hold values from 0.5 to 1.5
- rel_bias: float32 [32, 12], replicated, may hold values from -4 to 4
- doc_buckets: int32 [1024, 1024], P('seq'), may hold values from 0 to 31
- query_buckets: int32 [32, 32], replicated, may hold values from 0 to 31
- topk_mask: int32 [512, 1024], P(('dp', 'seq')), may hold values 0 or 1
- positives: int32 [512, 4], P(('dp', 'seq')), may hold values from 0 to 1023
- pos_count: int32 [512], P(('dp', 'seq')), may hold values from 1 to 4
Outputs:
- doc_out: bfloat16 [32, 1024, 768], P('dp', 'seq')
- query_out: bfloat16 [512, 32, 768], P(('dp', 'seq'))
- doc_dx: float32 [32, 1024, 768], P('dp', 'seq')
- query_dx: float32 [512, 32, 768], P(('dp', 'seq'))
- grad_q_weight: float32 [768, 768], P(('dp', 'seq'))
- grad_kv_weight: float32 [768, 1536], P(('dp', 'seq'))
- grad_out_weight: float32 [768, 768], P(('dp', 'seq'))
- grad_up_weight: float32 [768, 3072], P(('dp', 'seq'))
- grad_down_weight: float32 [3072, 768], P(('dp', 'seq'))
- grad_attn_gain: float32 [768], replicated
- grad_ff_gain: float32 [768], replicated
- grad_rel_bias: float32 [32, 12], replicated
- retrieved_fraction: float32 [], replicated
All inputs are finite; a program needn't handle non-finite values. No bound on the sum of `topk_mask` on one device may be relied on, other than what follows from the above.
Results may differ from a plain program's by a relative error of at most 0.014.
The roundings to bfloat16 on the way count: a program that leaves them out, or rounds other values in their place, can miss the bound.
Values may be sent and summed in bfloat16 or wider, within the bound.
A program may use at most 256 MiB of HBM per device.

v0:
```python
import math

import jax
import jax.numpy as jnp
from jax import lax
from jax.sharding import PartitionSpec as P

EPSILON = 1e-06
BFLOAT = jnp.bfloat16
SINGLE = jnp.float32
PRECISE = lax.Precision.HIGHEST


def normed(values, gain):
    return values * lax.rsqrt(jnp.mean(values * values, axis=-1, keepdims=True) + EPSILON) * gain


def smooth(values):
    return jax.nn.gelu(values, approximate=True)


def split_rows(buckets):
    block_rows = math.gcd(buckets.shape[0], 32)
    return (
        block_rows,
        buckets.reshape(buckets.shape[0] // block_rows, block_rows, buckets.shape[1]),
    )


def lookup(buckets, bias_table):
    block_rows, bucket_blocks = split_rows(buckets)
    labels = jnp.arange(bias_table.shape[0], dtype=jnp.int32)

    def part_bias(bucket_block):
        onehot = (bucket_block[:, :, None] == labels).astype(SINGLE)
        return jnp.einsum("ijb,bh->hij", onehot, bias_table, precision=PRECISE)

    pieces = lax.map(part_bias, bucket_blocks)
    return jnp.transpose(pieces, (1, 0, 2, 3)).reshape(
        bias_table.shape[1], buckets.shape[0], buckets.shape[1]
    )


def bucket_sums(buckets, grad_terms, bucket_count):
    block_rows, bucket_blocks = split_rows(buckets)
    head_count = grad_terms.shape[0]
    grad_blocks = grad_terms.reshape(
        head_count, bucket_blocks.shape[0], block_rows, buckets.shape[1]
    )
    grad_blocks = jnp.transpose(grad_blocks, (1, 0, 2, 3))
    labels = jnp.arange(bucket_count, dtype=jnp.int32)

    def part_sum(running, inputs_pair):
        bucket_block, grad_block = inputs_pair
        onehot = (bucket_block[:, :, None] == labels).astype(SINGLE)
        return (running + jnp.einsum("hij,ijb->bh", grad_block, onehot, precision=PRECISE), None)

    summed, _ = lax.scan(
        part_sum, jnp.zeros((bucket_count, head_count), SINGLE), (bucket_blocks, grad_blocks)
    )
    return summed


def on_device(
    doc_tokens,
    queries,
    doc_cot,
    query_cot,
    q_weight,
    kv_weight,
    out_weight,
    up_weight,
    down_weight,
    attn_gain,
    ff_gain,
    rel_bias,
    doc_buckets,
    query_buckets,
    topk_mask,
    positives,
    pos_count,
):
    n_docs, shard_rows, model_width = doc_tokens.shape
    n_query, query_len, _ = queries.shape
    bucket_count, head_count = rel_bias.shape
    head_dim = model_width // head_count
    doc_len = doc_buckets.shape[1]
    doc_rows = n_docs * shard_rows
    query_total = n_query * query_len
    shards = (q_weight, kv_weight, out_weight, up_weight, down_weight)
    w_query, w_keyval, w_out, w_up, w_down = (
        lax.all_gather(shards[0], ("dp", "seq"), axis=0, tiled=True),
        lax.all_gather(shards[1], ("dp", "seq"), axis=0, tiled=True),
        lax.all_gather(shards[2], ("dp", "seq"), axis=0, tiled=True),
        lax.all_gather(shards[3], ("dp", "seq"), axis=0, tiled=True),
        lax.all_gather(shards[4], ("dp", "seq"), axis=0, tiled=True),
    )
    tokens = jnp.concatenate(
        [doc_tokens.reshape(doc_rows, model_width), queries.reshape(query_total, model_width)], 0
    ).astype(SINGLE)
    first_norm = normed(tokens, attn_gain).astype(BFLOAT)
    query_rows = jnp.dot(first_norm, w_query, preferred_element_type=SINGLE).astype(BFLOAT)
    keyval_rows = jnp.dot(first_norm, w_keyval, preferred_element_type=SINGLE).astype(BFLOAT)
    doc_terms = lookup(doc_buckets, rel_bias)
    query_terms = lookup(query_buckets, rel_bias)
    doc_query = query_rows[:doc_rows].reshape(n_docs, shard_rows, head_count, head_dim)
    doc_keyval = keyval_rows[:doc_rows].reshape(n_docs, shard_rows, 2 * model_width)

    def doc_forward(running, inputs_pair):
        query_block, keyval_block = inputs_pair
        gathered = lax.all_gather(keyval_block, "seq", axis=0, tiled=True)
        key_rows = gathered[:, :model_width].reshape(doc_len, head_count, head_dim)
        value_rows = gathered[:, model_width:].reshape(doc_len, head_count, head_dim)
        scores = (
            jnp.einsum("ihd,jhd->hij", query_block, key_rows, preferred_element_type=SINGLE)
            + doc_terms
        )
        row_max = jnp.max(scores, axis=-1, keepdims=True)
        shifted = jnp.exp(scores - row_max)
        row_sum = jnp.sum(shifted, axis=-1, keepdims=True)
        soft_low = (shifted / row_sum).astype(BFLOAT)
        mixture = jnp.einsum("hij,jhd->ihd", soft_low, value_rows, preferred_element_type=SINGLE)
        return (
            running,
            (mixture.reshape(shard_rows, model_width).astype(BFLOAT), row_max, row_sum),
        )

    _, (doc_mixture, doc_max, doc_sum) = lax.scan(
        doc_forward, jnp.zeros((), SINGLE), (doc_query, doc_keyval)
    )
    q_heads = query_rows[doc_rows:].reshape(n_query, query_len, head_count, head_dim)
    q_pairs = keyval_rows[doc_rows:].reshape(n_query, query_len, 2, head_count, head_dim)
    q_keys = q_pairs[:, :, 0]
    q_values = q_pairs[:, :, 1]
    q_scores = (
        jnp.einsum("bihd,bjhd->bhij", q_heads, q_keys, preferred_element_type=SINGLE) + query_terms
    )
    q_shifted = jnp.exp(q_scores - jnp.max(q_scores, axis=-1, keepdims=True))
    q_soft = q_shifted / jnp.sum(q_shifted, axis=-1, keepdims=True)
    q_soft_low = q_soft.astype(BFLOAT)
    q_mixture = jnp.einsum("bhij,bjhd->bihd", q_soft_low, q_values, preferred_element_type=SINGLE)
    mixture = jnp.concatenate(
        [
            doc_mixture.reshape(doc_rows, model_width),
            q_mixture.reshape(query_total, model_width).astype(BFLOAT),
        ],
        0,
    )
    residual = tokens + jnp.dot(mixture, w_out, preferred_element_type=SINGLE)
    second = normed(residual, ff_gain).astype(BFLOAT)
    pre_act = jnp.dot(second, w_up, preferred_element_type=SINGLE)
    hidden = smooth(pre_act).astype(BFLOAT)
    outputs = (residual + jnp.dot(hidden, w_down, preferred_element_type=SINGLE)).astype(BFLOAT)
    doc_out = outputs[:doc_rows].reshape(doc_tokens.shape)
    query_out = outputs[doc_rows:].reshape(queries.shape)
    b_query, b_keyval, b_out, b_up, b_down = (
        lax.all_gather(shards[0], ("dp", "seq"), axis=0, tiled=True),
        lax.all_gather(shards[1], ("dp", "seq"), axis=0, tiled=True),
        lax.all_gather(shards[2], ("dp", "seq"), axis=0, tiled=True),
        lax.all_gather(shards[3], ("dp", "seq"), axis=0, tiled=True),
        lax.all_gather(shards[4], ("dp", "seq"), axis=0, tiled=True),
    )
    cotangent = jnp.concatenate(
        [doc_cot.reshape(doc_rows, model_width), query_cot.reshape(query_total, model_width)], 0
    )
    grad_down = jnp.einsum("tf,td->fd", hidden, cotangent, preferred_element_type=SINGLE)
    grad_hidden = jnp.einsum("td,fd->tf", cotangent, b_down, preferred_element_type=SINGLE)
    _, gelu_back = jax.vjp(smooth, pre_act)
    grad_pre = gelu_back(grad_hidden)[0].astype(BFLOAT)
    grad_up = jnp.einsum("td,tf->df", second, grad_pre, preferred_element_type=SINGLE)
    grad_second = jnp.einsum("tf,df->td", grad_pre, b_up, preferred_element_type=SINGLE)
    _, norm_back_two = jax.vjp(normed, residual, ff_gain)
    grad_res_part, grad_ff = norm_back_two(grad_second)
    grad_residual = cotangent.astype(SINGLE) + grad_res_part
    grad_res_low = grad_residual.astype(BFLOAT)
    grad_out = jnp.einsum("td,te->de", mixture, grad_res_low, preferred_element_type=SINGLE)
    grad_mixture = jnp.einsum(
        "te,de->td", grad_res_low, b_out, preferred_element_type=SINGLE
    ).astype(BFLOAT)
    doc_grad_mix = grad_mixture[:doc_rows].reshape(n_docs, shard_rows, head_count, head_dim)

    def doc_backward(running, inputs_pack):
        query_block, keyval_block, row_max, row_sum, grad_block = inputs_pack
        gathered = lax.all_gather(keyval_block, "seq", axis=0, tiled=True)
        key_rows = gathered[:, :model_width].reshape(doc_len, head_count, head_dim)
        value_rows = gathered[:, model_width:].reshape(doc_len, head_count, head_dim)
        scores = (
            jnp.einsum("ihd,jhd->hij", query_block, key_rows, preferred_element_type=SINGLE)
            + doc_terms
        )
        soft = jnp.exp(scores - row_max) / row_sum
        grad_soft = jnp.einsum(
            "ihd,jhd->hij", grad_block, value_rows, preferred_element_type=SINGLE
        )
        correction = jnp.sum(soft * grad_soft, axis=-1, keepdims=True)
        grad_scores = soft * (grad_soft - correction)
        scores_low = grad_scores.astype(BFLOAT)
        grad_query = jnp.einsum("hij,jhd->ihd", scores_low, key_rows, preferred_element_type=SINGLE)
        soft_low = soft.astype(BFLOAT)
        grad_keys = jnp.einsum(
            "hij,ihd->jhd", scores_low, query_block, preferred_element_type=SINGLE
        )
        grad_values = jnp.einsum(
            "hij,ihd->jhd", soft_low, grad_block, preferred_element_type=SINGLE
        )
        terms = jnp.concatenate(
            [grad_keys.reshape(doc_len, model_width), grad_values.reshape(doc_len, model_width)], 1
        )
        own_rows = lax.psum_scatter(
            terms.astype(jnp.bfloat16), "seq", scatter_dimension=0, tiled=True
        ).astype(jnp.float32)
        grad_query = grad_query.reshape(shard_rows, model_width).astype(BFLOAT)
        return (running + scores_low.astype(SINGLE), (grad_query, own_rows.astype(BFLOAT)))

    bias_running = jnp.zeros((head_count, shard_rows, doc_len), SINGLE)
    bias_running, (doc_grad_query, doc_grad_keyval) = lax.scan(
        doc_backward, bias_running, (doc_query, doc_keyval, doc_max, doc_sum, doc_grad_mix)
    )
    q_grad_mix = grad_mixture[doc_rows:].reshape(n_query, query_len, head_count, head_dim)
    q_grad_soft = jnp.einsum("bihd,bjhd->bhij", q_grad_mix, q_values, preferred_element_type=SINGLE)
    q_grad_scores = q_soft * (q_grad_soft - jnp.sum(q_soft * q_grad_soft, axis=-1, keepdims=True))
    q_scores_low = q_grad_scores.astype(BFLOAT)
    q_grad_heads = jnp.einsum(
        "bhij,bjhd->bihd", q_scores_low, q_keys, preferred_element_type=SINGLE
    )
    q_grad_keys = jnp.einsum(
        "bhij,bihd->bjhd", q_scores_low, q_heads, preferred_element_type=SINGLE
    )
    q_grad_values = jnp.einsum(
        "bhij,bihd->bjhd", q_soft_low, q_grad_mix, preferred_element_type=SINGLE
    )
    q_grad_pairs = jnp.stack([q_grad_keys, q_grad_values], 2).reshape(query_total, 2 * model_width)
    grad_query_rows = jnp.concatenate(
        [
            doc_grad_query.reshape(doc_rows, model_width),
            q_grad_heads.reshape(query_total, model_width).astype(BFLOAT),
        ],
        0,
    )
    grad_keyval_rows = jnp.concatenate(
        [doc_grad_keyval.reshape(doc_rows, 2 * model_width), q_grad_pairs.astype(BFLOAT)], 0
    )
    grad_wq = jnp.einsum("td,te->de", first_norm, grad_query_rows, preferred_element_type=SINGLE)
    grad_wkv = jnp.einsum("td,te->de", first_norm, grad_keyval_rows, preferred_element_type=SINGLE)
    grad_first = jnp.einsum("te,de->td", grad_query_rows, b_query, preferred_element_type=SINGLE)
    grad_first = grad_first + jnp.einsum(
        "te,de->td", grad_keyval_rows, b_keyval, preferred_element_type=SINGLE
    )
    _, norm_back_one = jax.vjp(normed, tokens, attn_gain)
    grad_tok_part, grad_attn = norm_back_one(grad_first)
    grad_tokens = grad_residual + grad_tok_part
    doc_dx = grad_tokens[:doc_rows].reshape(doc_tokens.shape)
    query_dx = grad_tokens[doc_rows:].reshape(queries.shape)
    grad_shards = (
        lax.psum_scatter(grad_wq, ("dp", "seq"), scatter_dimension=0, tiled=True),
        lax.psum_scatter(grad_wkv, ("dp", "seq"), scatter_dimension=0, tiled=True),
        lax.psum_scatter(grad_out, ("dp", "seq"), scatter_dimension=0, tiled=True),
        lax.psum_scatter(grad_up, ("dp", "seq"), scatter_dimension=0, tiled=True),
        lax.psum_scatter(grad_down, ("dp", "seq"), scatter_dimension=0, tiled=True),
    )
    bias_local = bucket_sums(doc_buckets, bias_running, bucket_count)
    bias_local = bias_local + bucket_sums(
        query_buckets, jnp.sum(q_scores_low.astype(SINGLE), axis=0), bucket_count
    )
    matches = positives[:, :, None] == jnp.arange(doc_len, dtype=jnp.int32)[None, None, :]
    counted = jnp.arange(positives.shape[1], dtype=jnp.int32)[None, :] < pos_count[:, None]
    retrieved = jnp.sum(
        jnp.where(matches & counted[:, :, None], topk_mask[:, None, :].astype(SINGLE), 0.0)
    )
    gain_pair = jnp.stack([grad_attn, grad_ff])
    gain_total, bias_total, retrieved_total = lax.psum(
        (gain_pair, bias_local, retrieved), ("dp", "seq")
    )
    slots = float(n_query * lax.axis_size("dp") * lax.axis_size("seq") * positives.shape[1])
    fraction = retrieved_total / slots
    return (
        doc_out,
        query_out,
        doc_dx,
        query_dx,
        grad_shards[0],
        grad_shards[1],
        grad_shards[2],
        grad_shards[3],
        grad_shards[4],
        gain_total[0],
        gain_total[1],
        bias_total,
        fraction,
    )


def solution(mesh):
    return jax.shard_map(
        on_device,
        mesh=mesh,
        in_specs=(
            P("dp", "seq", None),
            P(("dp", "seq"), None, None),
            P("dp", "seq", None),
            P(("dp", "seq"), None, None),
            P(("dp", "seq"), None),
            P(("dp", "seq"), None),
            P(("dp", "seq"), None),
            P(("dp", "seq"), None),
            P(("dp", "seq"), None),
            P(),
            P(),
            P(),
            P("seq", None),
            P(),
            P(("dp", "seq"), None),
            P(("dp", "seq"), None),
            P(("dp", "seq")),
        ),
        out_specs=(
            P("dp", "seq", None),
            P(("dp", "seq"), None, None),
            P("dp", "seq", None),
            P(("dp", "seq"), None, None),
            P(("dp", "seq"), None),
            P(("dp", "seq"), None),
            P(("dp", "seq"), None),
            P(("dp", "seq"), None),
            P(("dp", "seq"), None),
            P(),
            P(),
            P(),
            P(),
        ),
        check_vma=False,
    )
```

profile of v0, /device:TPU:0, one launch (start us, length us, event | category | flops | bytes accessed | tf_op | source)
XLA Modules:
  0.0 1664.1 jit_solution(1797888600750470563)
XLA Ops:
  8.7 36.1 %while.60 = (s32[]{:T(128)}, f32[8,12,32,1024]{3,1,2,0:T(8,128)}, s32[8,32,1024]{2,1,0:T(8,128)}, f32[32,12]{0,1:T(8,128)}, s32[]{:T(128)}) while((s32[]{:T(128)}, f32[8,12,32,1024]{3,1,2,0:T(8,128)}, s32[8,32,1024]{2,1,0:T(8,128)}, f32[32,12]{0,1:T(8,128)}, s32[]{:T(128)}) %tuple.156), condition=%wide.region_2.3_spmd.clone, body=%wide.region_1.2_spmd.clone.sunk | while | flops 152043520 | bytes 2498637 | solution.py:38
  44.8 17.8 %copy.99 = f32[12,8,32,1024]{3,2,1,0:T(8,128)} copy(f32[12,8,32,1024]{3,0,2,1:T(8,128)} %bitcast.218) | data formatting | bytes 25165824 | tf_op jit(solution)/shard_map/transpose | solution.py:39
  63.1 4.6 all-gather.17.cloned.1.call-done
  67.7 4.9 convolution_convert_fusion.4
  78.0 48.9 %all-gather.15.cloned.1.call-done = bf16[768,1536]{1,0:T(8,128)(2,1)} async-done(((bf16[24,1536]{1,0:T(8,128)(2,1)}), bf16[768,1536]{1,0:T(8,128)(2,1)}) %all-gather.15.cloned.1.call-update) | async-done | bytes 2359312 | tf_op jit(solution)/shard_map/all_gather | solution.py:93
  126.9 6.3 convolution_convert_fusion.2
  139.7 188.2 %while.59 = (s32[]{:T(128)}, bf16[4,256,768]{2,1,0:T(8,128)(2,1)}, f32[4,12,256,1]{2,1,3,0:T(8,128)S(1)}, f32[4,12,256,1]{2,1,3,0:T(8,128)S(1)}, bf16[4,256,1536...) while((s32[]{:T(128)}, bf16[4,256,768]{2,1,0:T(8,128)(2,1)}, ...), condition=%wide.region_6.7_spmd, body=%wide.region_3.6_spmd.sunk | while | flops 827516928 | bytes 75624584 | solution.py:128
  141.9 28.7 %all-gather.25.cloned.1.call-done = bf16[1,1024,1536]{1,2,0:T(8,128)(2,1)} async-done(((bf16[1,256,1536]{1,2,0:T(8,128)(2,1)}), bf16[1,1024,1536]{1,2,0:T(8,128)(2,1)}) %all-gather.25.cloned.1.call-update) | async-done | bytes 3145744 | tf_op jit(solution)/shard_map/while/body/eval_jaxpr/all_gather | solution.py:111
  172.7 6.7 fusion.153
  188.2 29.6 %all-gather.25.cloned.1.call-done = bf16[1,1024,1536]{1,2,0:T(8,128)(2,1)} async-done(((bf16[1,256,1536]{1,2,0:T(8,128)(2,1)}), bf16[1,1024,1536]{1,2,0:T(8,128)(2,1)}) %all-gather.25.cloned.1.call-update) | async-done | bytes 3145744 | tf_op jit(solution)/shard_map/while/body/eval_jaxpr/all_gather | solution.py:111
  220.0 6.7 fusion.153
  235.5 29.6 %all-gather.25.cloned.1.call-done = bf16[1,1024,1536]{1,2,0:T(8,128)(2,1)} async-done(((bf16[1,256,1536]{1,2,0:T(8,128)(2,1)}), bf16[1,1024,1536]{1,2,0:T(8,128)(2,1)}) %all-gather.25.cloned.1.call-update) | async-done | bytes 3145744 | tf_op jit(solution)/shard_map/while/body/eval_jaxpr/all_gather | solution.py:111
  267.2 6.7 fusion.153
  282.7 29.6 %all-gather.25.cloned.1.call-done = bf16[1,1024,1536]{1,2,0:T(8,128)(2,1)} async-done(((bf16[1,256,1536]{1,2,0:T(8,128)(2,1)}), bf16[1,1024,1536]{1,2,0:T(8,128)(2,1)}) %all-gather.25.cloned.1.call-update) | async-done | bytes 3145744 | tf_op jit(solution)/shard_map/while/body/eval_jaxpr/all_gather | solution.py:111
  314.5 6.7 fusion.153
  336.4 6.2 reshape.237
  352.3 33.4 %all-gather.19.cloned.1.call-done = bf16[768,768]{1,0:T(8,128)(2,1)} async-done(((bf16[24,768]{1,0:T(8,128)(2,1)}), bf16[768,768]{1,0:T(8,128)(2,1)}) %all-gather.19.cloned.1.call-update) | async-done | bytes 1179664 | tf_op jit(solution)/shard_map/all_gather | solution.py:94
  385.7 6.8 multiply_reduce_fusion.3
  392.5 58.7 %all-gather.21.cloned.1.call-done = bf16[768,3072]{1,0:T(8,128)(2,1)} async-done(((bf16[24,3072]{1,0:T(8,128)(2,1)}), bf16[768,3072]{1,0:T(8,128)(2,1)}) %all-gather.21.cloned.1.call-update) | async-done | bytes 4718608 | tf_op jit(solution)/shard_map/all_gather | solution.py:95
  451.2 14.9 fusion.97
  466.1 50.4 %all-gather.23.cloned.1.call-done = bf16[3072,768]{1,0:T(8,128)(2,1)} async-done(((bf16[96,768]{1,0:T(8,128)(2,1)}), bf16[3072,768]{1,0:T(8,128)(2,1)}) %all-gather.23.cloned.1.call-update) | async-done | bytes 4718608 | tf_op jit(solution)/shard_map/all_gather | solution.py:96
  516.6 21.9 %fusion.49 = bf16[1536,3072]{1,0:T(8,128)(2,1)} fusion(f32[1536,3072]{1,0:T(8,128)} %fusion.97, bf16[3072,768]{1,0:T(8,128)(2,1)} %all-gather.23.cloned.1.call-done, bf16[512,768]{1,0:T(8,128)(2,1)S(1)} %bitcast.251, bf16[1024,768]{1,0:T(8,128)(2,1)S(1)} %bitcast.248), kind=kOutput, calls=%fused_computation.67 | convolution fusion | flops 7346847744 | bytes 35389440 | tf_op jit(solution)/shard_map/td,fd->tf/dot_general | solution.py:167
  538.4 11.2 multiply_reduce_fusion.1
  557.5 4.4 convolution_convert_fusion.3
  568.1 482.6 %while.61 = (s32[]{:T(128)}, f32[12,256,1024]{2,1,0:T(8,128)}, bf16[4,256,768]{2,1,0:T(8,128)(2,1)}, bf16[4,256,1536]{2,1,0:T(8,128)(2,1)}, bf16[4,256,12,64]{1,...) while((s32[]{:T(128)}, f32[12,256,1024]{2,1,0:T(8,128)}, ...), condition=%wide.region_14.15_spmd.clone, body=%wide.region_11.14_spmd.clone.sunk | while | flops 2059072512 | bytes 266305856 | solution.py:216
  570.7 28.3 %all-gather.27.cloned.1.call-done = bf16[1,1024,1536]{1,2,0:T(8,128)(2,1)} async-done(((bf16[1,256,1536]{1,2,0:T(8,128)(2,1)}), bf16[1,1024,1536]{1,2,0:T(8,128)(2,1)}) %all-gather.27.cloned.1.call-update) | async-done | bytes 3145744 | tf_op jit(solution)/shard_map/while/body/eval_jaxpr/all_gather | solution.py:184
  605.1 15.1 multiply_reduce_fusion.6
  620.3 5.9 fusion.168
  626.2 14.1 select_add_fusion.2
  645.0 4.8 convolution_convert_fusion.11
  650.8 32.3 %reduce-scatter.17.cloned.1.call-done = bf16[256,1536]{0,1:T(8,128)(2,1)} async-done(((bf16[1024,1536]{0,1:T(8,128)(2,1)}), bf16[256,1536]{0,1:T(8,128)(2,1)}) %reduce-scatter.17.cloned.1.call-update) | async-done | bytes 786448 | tf_op jit(solution)/shard_map/while/body/eval_jaxpr/reduce_scatter | solution.py:209
  687.6 29.5 %all-gather.27.cloned.1.call-done = bf16[1,1024,1536]{1,2,0:T(8,128)(2,1)} async-done(((bf16[1,256,1536]{1,2,0:T(8,128)(2,1)}), bf16[1,1024,1536]{1,2,0:T(8,128)(2,1)}) %all-gather.27.cloned.1.call-update) | async-done | bytes 3145744 | tf_op jit(solution)/shard_map/while/body/eval_jaxpr/all_gather | solution.py:184
  723.3 15.1 multiply_reduce_fusion.6
  738.5 5.9 fusion.168
  744.4 17.7 %select_add_fusion.2 = (f32[12,256,1024]{2,1,0:T(8,128)}, bf16[12,256,1024]{2,1,0:T(8,128)(2,1)S(1)}) fusion(f32[12,256,1024]{2,1,0:T(8,128)} %get-tuple-element.645, pred[]{:T(512)S(6)} %compare.6, f32[12,256,1024]{2,1,0:T(8,128)} %get-tuple-element.585, f32[12,256,1024]{2,1,0:T(8,128)} %copy-done.1, f32[12,256]{1,0:T(8,128)S(1)} %get-tuple-element.586), kind=kLoop, calls=%fused_computation.21.clone.1 | loop fusion | flops 18874368 | bytes 56635392 | tf_op jit(solution)/shard_map/while/body/eval_jaxpr/add | solution.py:213
  766.8 4.8 convolution_convert_fusion.11
  772.5 32.3 %reduce-scatter.17.cloned.1.call-done = bf16[256,1536]{0,1:T(8,128)(2,1)} async-done(((bf16[1024,1536]{0,1:T(8,128)(2,1)}), bf16[256,1536]{0,1:T(8,128)(2,1)}) %reduce-scatter.17.cloned.1.call-update) | async-done | bytes 786448 | tf_op jit(solution)/shard_map/while/body/eval_jaxpr/reduce_scatter | solution.py:209
  809.3 29.5 %all-gather.27.cloned.1.call-done = bf16[1,1024,1536]{1,2,0:T(8,128)(2,1)} async-done(((bf16[1,256,1536]{1,2,0:T(8,128)(2,1)}), bf16[1,1024,1536]{1,2,0:T(8,128)(2,1)}) %all-gather.27.cloned.1.call-update) | async-done | bytes 3145744 | tf_op jit(solution)/shard_map/while/body/eval_jaxpr/all_gather | solution.py:184
  845.0 15.1 multiply_reduce_fusion.6
  860.2 5.9 fusion.168
  866.1 17.7 %select_add_fusion.2 = (f32[12,256,1024]{2,1,0:T(8,128)}, bf16[12,256,1024]{2,1,0:T(8,128)(2,1)S(1)}) fusion(f32[12,256,1024]{2,1,0:T(8,128)} %get-tuple-element.645, pred[]{:T(512)S(6)} %compare.6, f32[12,256,1024]{2,1,0:T(8,128)} %get-tuple-element.585, f32[12,256,1024]{2,1,0:T(8,128)} %copy-done.1, f32[12,256]{1,0:T(8,128)S(1)} %get-tuple-element.586), kind=kLoop, calls=%fused_computation.21.clone.1 | loop fusion | flops 18874368 | bytes 56635392 | tf_op jit(solution)/shard_map/while/body/eval_jaxpr/add | solution.py:213
  888.5 4.8 convolution_convert_fusion.11
  894.2 32.3 %reduce-scatter.17.cloned.1.call-done = bf16[256,1536]{0,1:T(8,128)(2,1)} async-done(((bf16[1024,1536]{0,1:T(8,128)(2,1)}), bf16[256,1536]{0,1:T(8,128)(2,1)}) %reduce-scatter.17.cloned.1.call-update) | async-done | bytes 786448 | tf_op jit(solution)/shard_map/while/body/eval_jaxpr/reduce_scatter | solution.py:209
  931.1 29.5 %all-gather.27.cloned.1.call-done = bf16[1,1024,1536]{1,2,0:T(8,128)(2,1)} async-done(((bf16[1,256,1536]{1,2,0:T(8,128)(2,1)}), bf16[1,1024,1536]{1,2,0:T(8,128)(2,1)}) %all-gather.27.cloned.1.call-update) | async-done | bytes 3145744 | tf_op jit(solution)/shard_map/while/body/eval_jaxpr/all_gather | solution.py:184
  966.8 15.1 multiply_reduce_fusion.6
  981.9 5.9 fusion.168
  987.8 17.7 %select_add_fusion.2 = (f32[12,256,1024]{2,1,0:T(8,128)}, bf16[12,256,1024]{2,1,0:T(8,128)(2,1)S(1)}) fusion(f32[12,256,1024]{2,1,0:T(8,128)} %get-tuple-element.645, pred[]{:T(512)S(6)} %compare.6, f32[12,256,1024]{2,1,0:T(8,128)} %get-tuple-element.585, f32[12,256,1024]{2,1,0:T(8,128)} %copy-done.1, f32[12,256]{1,0:T(8,128)S(1)} %get-tuple-element.586), kind=kLoop, calls=%fused_computation.21.clone.1 | loop fusion | flops 18874368 | bytes 56635392 | tf_op jit(solution)/shard_map/while/body/eval_jaxpr/add | solution.py:213
  1010.2 4.8 convolution_convert_fusion.11
  1016.0 32.3 %reduce-scatter.17.cloned.1.call-done = bf16[256,1536]{0,1:T(8,128)(2,1)} async-done(((bf16[1024,1536]{0,1:T(8,128)(2,1)}), bf16[256,1536]{0,1:T(8,128)(2,1)}) %reduce-scatter.17.cloned.1.call-update) | async-done | bytes 786448 | tf_op jit(solution)/shard_map/while/body/eval_jaxpr/reduce_scatter | solution.py:209
  1069.4 5.6 fusion.64
  1084.1 6.5 convert_element_type.140
  1090.6 8.6 fusion.58
  1100.3 16.7 %fusion.81 = f32[3072,768]{1,0:T(8,128)} fusion(bf16[512,768]{1,0:T(8,128)(2,1)S(1)} %bitcast.253, bf16[1024,768]{1,0:T(8,128)(2,1)} %bitcast.247, f32[1536,3072]{1,0:T(8,128)} %fusion.97), kind=kOutput, calls=%fused_computation.134 | convolution fusion | flops 7294943232 | bytes 30670848 | tf_op jit(solution)/shard_map/tf,td->fd/dot_general | solution.py:166
  1117.7 14.8 fusion.96
  1134.2 17.5 %add_convert_fusion = bf16[1536,768]{1,0:T(8,128)(2,1)S(1)} fusion(f32[1536,768]{1,0:T(8,128)} %get-tuple-element.406, bf16[3072,768]{1,0:T(8,128)(2,1)} %all-gather.23.cloned.1.call-done, f32[1536,3072]{1,0:T(8,128)} %fusion.97), kind=kOutput, calls=%fused_computation.88 | convolution fusion | flops 7292583936 | bytes 30670848 | tf_op jit(solution)/shard_map/dot_general | solution.py:153
  1166.7 18.1 %copy.121 = f32[12,256,1024]{2,0,1:T(8,128)} copy(f32[12,256,1024]{2,1,0:T(8,128)} %get-tuple-element.196) | data formatting | bytes 25165824 | tf_op jit(solution)/shard_map/while | solution.py:216
  1184.8 39.5 %while.62 = (s32[]{:T(128)}, f32[32,12]{0,1:T(8,128)S(1)}, s32[8,32,1024]{2,1,0:T(8,128)}, f32[8,12,32,1024]{3,1,2,0:T(8,128)}, s32[]{:T(128)}, /*index=5*/s32[]{:T(128)}) while((s32[]{:T(128)}, f32[32,12]{0,1:T(8,128)S(1)}, s32[8,32,1024]{2,1,0:T(8,128)}, f32[8,12,32,1024]{3,1,2,0:T(8,128)}, s32[]{:T(128)}, ...), condition=%wide.region_26.27_spmd.clone, body=%wide.region_25.26_spmd.clone.sunk | while | flops 152044288 | bytes 2493535 | solution.py:58
  1185.7 4.0 fusion.170
  1190.7 4.0 fusion.170
  1220.3 4.0 fusion.170
  1224.8 40.0 %all-reduce = (f32[2,768]{1,0:T(2,128)S(1)}, f32[32,12]{0,1:T(8,128)}, f32[]{:T(128)}) all-reduce(f32[2,768]{1,0:T(2,128)S(1)} %pad_maximum_fusion.15, f32[32,12]{0,1:T(8,128)S(1)} %fusion.78, f32[]{:T(128)} %select_reduce_fusion), channel_id=1, replica_groups=mesh['dp'=8,'seq'=4] {'dp','seq'}, use_global_device_ids=true, to_apply=%region_24.25 | all-reduce | flops 1921 | bytes 15368 | tf_op jit(solution)/shard_map/psum | solution.py:271
  1266.0 106.7 %reduce-scatter.9.cloned.1.call-done = f32[24,1536]{1,0:T(8,128)} async-done(((f32[768,1536]{1,0:T(8,128)}), f32[24,1536]{1,0:T(8,128)}) %reduce-scatter.9.cloned.1.call-update) | async-done | bytes 147472 | tf_op jit(solution)/shard_map/reduce_scatter | solution.py:256
  1372.7 142.2 %reduce-scatter.15.cloned.1.call-done = f32[96,768]{1,0:T(8,128)} async-done(((f32[3072,768]{1,0:T(8,128)}), f32[96,768]{1,0:T(8,128)}) %reduce-scatter.15.cloned.1.call-update) | async-done | bytes 294928 | tf_op jit(solution)/shard_map/reduce_scatter | solution.py:259
  1514.9 141.0 %reduce-scatter.13.cloned.1.call-done = f32[24,3072]{1,0:T(8,128)} async-done(((f32[768,3072]{1,0:T(8,128)}), f32[24,3072]{1,0:T(8,128)}) %reduce-scatter.13.cloned.1.call-update) | async-done | bytes 294928 | tf_op jit(solution)/shard_map/reduce_scatter | solution.py:258
  (339 shorter events, 265.1 us)
Async XLA Ops:
  7.2 60.6 %all-gather.17.cloned.1.call-start = ((), (), s32[]{:S(2)}) async-start(), calls=%async_computation.7 | async-start | bytes 1216512 | tf_op jit(solution)/shard_map/all_gather | solution.py:92
  7.9 119.0 %all-gather.15.cloned.1.call-start = ((), (), s32[]{:S(2)}) async-start(), calls=%async_computation.6 | async-start | bytes 2433024 | tf_op jit(solution)/shard_map/all_gather | solution.py:93
  44.7 17.8 %copy-start.11 = (bf16[4,256,768]{2,1,0:T(8,128)(2,1)S(1)}, bf16[4,256,768]{2,1,0:T(8,128)(2,1)}, u32[]{:S(2)}) copy-start(bf16[4,256,768]{2,1,0:T(8,128)(2,1)} %param.25) | copy-start | bytes 4718596
  44.7 17.8 %copy-start.15 = (bf16[16,32,768]{2,1,0:T(8,128)(2,1)S(1)}, bf16[16,32,768]{2,1,0:T(8,128)(2,1)}, u32[]{:S(2)}) copy-start(bf16[16,32,768]{2,1,0:T(8,128)(2,1)} %param.26) | copy-start | bytes 2359300
  44.7 23.0 %copy-start.43 = (f32[768]{0:T(1024)S(1)}, f32[768]{0:T(1024)}, u32[]{:S(2)}) copy-start(f32[768]{0:T(1024)} %param.34) | copy-start | bytes 9220
  63.1 4.7 copy-start.31
  63.1 63.8 %copy-start.36 = (f32[1536]{0:T(1024)}, f32[1536]{0:T(1024)S(1)}, u32[]{:S(2)}) copy-start(f32[1536]{0:T(1024)S(1)} %fusion.86) | copy-start | bytes 18436
  139.7 190.5 %copy-start.30 = (f32[32,12]{0,1:T(8,128)S(1)}, f32[32,12]{0,1:T(8,128)}, u32[]{:S(2)}) copy-start(f32[32,12]{0,1:T(8,128)} %get-tuple-element.720) | copy-start | bytes 4612
  139.7 190.5 %copy-start.33 = (s32[32,32]{1,0:T(8,128)S(1)}, s32[32,32]{1,0:T(8,128)}, u32[]{:S(2)}) copy-start(s32[32,32]{1,0:T(8,128)} %param.38) | copy-start | bytes 12292
  139.7 191.8 %slice-start.4 = ((bf16[1536,768]{1,0:T(8,128)(2,1)}), bf16[512,768]{1,0:T(8,128)(2,1)S(1)}, s32[]{:S(2)}) async-start(bf16[1536,768]{1,0:T(8,128)(2,1)} %copy-done.14), calls=%async_computation.23 | async-start | bytes 1572864 | tf_op jit(solution)/shard_map/slice | solution.py:131
  139.7 30.9 %all-gather.25.cloned.1.call-start = ((), (), s32[]{:S(2)}) async-start(), calls=%async_computation.16 | async-start | bytes 3932160 | tf_op jit(solution)/shard_map/while/body/eval_jaxpr/all_gather | solution.py:111
  186.1 31.7 %all-gather.25.cloned.1.call-start = ((), (), s32[]{:S(2)}) async-start(), calls=%async_computation.16 | async-start | bytes 3932160 | tf_op jit(solution)/shard_map/while/body/eval_jaxpr/all_gather | solution.py:111
  233.4 31.7 %all-gather.25.cloned.1.call-start = ((), (), s32[]{:S(2)}) async-start(), calls=%async_computation.16 | async-start | bytes 3932160 | tf_op jit(solution)/shard_map/while/body/eval_jaxpr/all_gather | solution.py:111
  280.6 31.7 %all-gather.25.cloned.1.call-start = ((), (), s32[]{:S(2)}) async-start(), calls=%async_computation.16 | async-start | bytes 3932160 | tf_op jit(solution)/shard_map/while/body/eval_jaxpr/all_gather | solution.py:111
  327.9 57.9 %all-gather.19.cloned.1.call-start = ((), (), s32[]{:S(2)}) async-start(), calls=%async_computation.8 | async-start | bytes 1216512 | tf_op jit(solution)/shard_map/all_gather | solution.py:94
  328.6 122.6 %all-gather.21.cloned.1.call-start = ((), (), s32[]{:S(2)}) async-start(), calls=%async_computation.9 | async-start | bytes 4866048 | tf_op jit(solution)/shard_map/all_gather | solution.py:95
  329.4 187.2 %all-gather.23.cloned.1.call-start = ((), (), s32[]{:S(2)}) async-start(), calls=%async_computation.10 | async-start | bytes 4866048 | tf_op jit(solution)/shard_map/all_gather | solution.py:96
  333.0 12.7 copy-start.4
  349.6 36.2 %copy-start.16 = (bf16[16,32,768]{2,1,0:T(8,128)(2,1)S(1)}, bf16[16,32,768]{2,1,0:T(8,128)(2,1)}, u32[]{:S(2)}) copy-start(bf16[16,32,768]{2,1,0:T(8,128)(2,1)} %param.26) | copy-start | bytes 2359300
  385.7 65.5 %copy-start.41 = (f32[768]{0:T(1024)S(1)}, f32[768]{0:T(1024)}, u32[]{:S(2)}) copy-start(f32[768]{0:T(1024)} %param.35) | copy-start | bytes 9220
  392.5 157.1 %copy-start.38 = (f32[1536]{0:T(1024)}, f32[1536]{0:T(1024)S(1)}, u32[]{:S(2)}) copy-start(f32[1536]{0:T(1024)S(1)} %fusion.87) | copy-start | bytes 18436
  451.2 65.3 %copy-start.23 = (bf16[4,256,768]{2,1,0:T(8,128)(2,1)S(1)}, bf16[4,256,768]{2,1,0:T(8,128)(2,1)}, u32[]{:S(2)}) copy-start(bf16[4,256,768]{2,1,0:T(8,128)(2,1)} %param.27) | copy-start | bytes 4718596
  451.2 65.3 %copy-start.26 = (bf16[16,32,768]{2,1,0:T(8,128)(2,1)S(1)}, bf16[16,32,768]{2,1,0:T(8,128)(2,1)}, u32[]{:S(2)}) copy-start(bf16[16,32,768]{2,1,0:T(8,128)(2,1)} %param.28) | copy-start | bytes 2359300
  451.2 87.2 %slice-start.2 = ((s8[4718592]{0:T(1024)(128)(4,1)}), s8[524288]{0:T(1024)(128)(4,1)S(1)}, s32[]{:S(2)}) async-start(s8[4718592]{0:T(1024)(128)(4,1)} %bitcast.229), calls=%async_computation.21 | async-start | bytes 1048576
  516.5 21.9 %slice-start.3 = ((s8[4718592]{0:T(1024)(128)(4,1)}), s8[4194304]{0:T(1024)(128)(4,1)S(1)}, s32[]{:S(2)}) async-start(s8[4718592]{0:T(1024)(128)(4,1)} %bitcast.229), calls=%async_computation.22 | async-start | bytes 8388608
  516.5 21.9 %copy-start.46 = (bf16[768,3072]{1,0:T(8,128)(2,1)S(1)}, bf16[768,3072]{1,0:T(8,128)(2,1)}, u32[]{:S(2)}) copy-start(bf16[768,3072]{1,0:T(8,128)(2,1)} %all-gather.21.cloned.1.call-done) | copy-start | bytes 14155780
  549.7 4.4 copy-start.21
  549.7 4.4 copy-start.25
  554.0 3.5 copy-start.50
  568.4 30.5 %all-gather.27.cloned.1.call-start = ((), (), s32[]{:S(2)}) async-start(), calls=%async_computation.17 | async-start | bytes 3932160 | tf_op jit(solution)/shard_map/while/body/eval_jaxpr/all_gather | solution.py:184
  570.6 112.5 %reduce-scatter.17.cloned.1.call-start = ((), (), s32[]{:S(2)}) async-start(), calls=%async_computation.18 | async-start | bytes 3932160 | tf_op jit(solution)/shard_map/while/body/eval_jaxpr/reduce_scatter | solution.py:209
  605.1 15.2 copy-start.1
  685.5 31.7 %all-gather.27.cloned.1.call-start = ((), (), s32[]{:S(2)}) async-start(), calls=%async_computation.17 | async-start | bytes 3932160 | tf_op jit(solution)/shard_map/while/body/eval_jaxpr/all_gather | solution.py:184
  687.6 117.3 %reduce-scatter.17.cloned.1.call-start = ((), (), s32[]{:S(2)}) async-start(), calls=%async_computation.18 | async-start | bytes 3932160 | tf_op jit(solution)/shard_map/while/body/eval_jaxpr/reduce_scatter | solution.py:209
  723.3 15.1 copy-start.1
  807.2 31.7 %all-gather.27.cloned.1.call-start = ((), (), s32[]{:S(2)}) async-start(), calls=%async_computation.17 | async-start | bytes 3932160 | tf_op jit(solution)/shard_map/while/body/eval_jaxpr/all_gather | solution.py:184
  809.3 117.3 %reduce-scatter.17.cloned.1.call-start = ((), (), s32[]{:S(2)}) async-start(), calls=%async_computation.18 | async-start | bytes 3932160 | tf_op jit(solution)/shard_map/while/body/eval_jaxpr/reduce_scatter | solution.py:209
  845.0 15.1 copy-start.1
  928.9 31.7 %all-gather.27.cloned.1.call-start = ((), (), s32[]{:S(2)}) async-start(), calls=%async_computation.17 | async-start | bytes 3932160 | tf_op jit(solution)/shard_map/while/body/eval_jaxpr/all_gather | solution.py:184
  931.0 117.3 %reduce-scatter.17.cloned.1.call-start = ((), (), s32[]{:S(2)}) async-start(), calls=%async_computation.18 | async-start | bytes 3932160 | tf_op jit(solution)/shard_map/while/body/eval_jaxpr/reduce_scatter | solution.py:209
  966.7 15.1 copy-start.1
  1050.6 6.9 copy-start.8
  1050.6 6.9 copy-start.29
  1050.6 215.4 %reduce-scatter.11.cloned.1.call-start = ((), (), s32[]{:S(2)}) async-start(), calls=%async_computation.13 | async-start | bytes 2433024 | tf_op jit(solution)/shard_map/reduce_scatter | solution.py:257
  1051.2 214.8 %reduce-scatter.7.cloned.1.call-start = ((), (), s32[]{:S(2)}) async-start(), calls=%async_computation.11 | async-start | bytes 2433024 | tf_op jit(solution)/shard_map/reduce_scatter | solution.py:255
  1057.5 3.5 copy-start.9
  1063.4 5.9 copy-start.12
  1063.4 5.9 copy-start.37
  1063.4 5.9 copy-start.44
  1075.0 297.7 %reduce-scatter.9.cloned.1.call-start = ((), (), s32[]{:S(2)}) async-start(), calls=%async_computation.12 | async-start | bytes 4866048 | tf_op jit(solution)/shard_map/reduce_scatter | solution.py:256
  1084.1 6.5 copy-start.17
  1099.2 415.7 %reduce-scatter.15.cloned.1.call-start = ((), (), s32[]{:S(2)}) async-start(), calls=%async_computation.15 | async-start | bytes 9732096 | tf_op jit(solution)/shard_map/reduce_scatter | solution.py:259
  1117.1 538.9 %reduce-scatter.13.cloned.1.call-start = ((), (), s32[]{:S(2)}) async-start(), calls=%async_computation.14 | async-start | bytes 9732096 | tf_op jit(solution)/shard_map/reduce_scatter | solution.py:258
  1134.2 19.7 %copy-start.22 = (bf16[512,1536]{1,0:T(8,128)(2,1)S(1)}, bf16[512,1536]{1,0:T(8,128)(2,1)}, u32[]{:S(2)}) copy-start(bf16[512,1536]{1,0:T(8,128)(2,1)} %convert_element_type.140) | copy-start | bytes 4718596
  1134.2 19.7 %copy-start.47 = (bf16[4,256,1536]{2,1,0:T(8,128)(2,1)S(1)}, bf16[4,256,1536]{2,1,0:T(8,128)(2,1)}, u32[]{:S(2)}) copy-start(bf16[4,256,1536]{2,1,0:T(8,128)(2,1)} %get-tuple-element.195) | copy-start | bytes 9437188
  1134.2 19.7 %copy-start.48 = (bf16[768,1536]{1,0:T(8,128)(2,1)S(1)}, bf16[768,1536]{1,0:T(8,128)(2,1)}, u32[]{:S(2)}) copy-start(bf16[768,1536]{1,0:T(8,128)(2,1)} %all-gather.15.cloned.1.call-done) | copy-start | bytes 7077892
  1151.7 9.3 slice-start
  1153.9 4.0 copy-start.20
  1153.9 4.0 copy-start.24
  1153.9 4.0 copy-start.49
  1153.9 7.1 slice-start.1
  1158.0 3.0 copy-start.32
  1163.4 3.1 copy-start.40
  1184.8 39.5 %copy-start.34 = (s32[32,32]{1,0:T(8,128)S(1)}, s32[32,32]{1,0:T(8,128)}, u32[]{:S(2)}) copy-start(s32[32,32]{1,0:T(8,128)} %param.38) | copy-start | bytes 12292
  (24 other events, 43.0 us)
Sparse Core Ops, SparseCore 0:
  10.9 56.7 all-gather.16
  70.6 56.2 all-gather.14
  142.7 27.8 all-gather.24
  188.8 28.9 all-gather.24
  236.1 28.9 all-gather.24
  283.3 28.9 all-gather.24
  331.6 54.0 all-gather.18
  388.6 62.5 all-gather.20
  454.1 62.3 all-gather.22
  571.2 27.7 all-gather.26
  645.1 37.9 reduce-scatter.16
  688.2 28.9 all-gather.26
  766.9 37.9 reduce-scatter.16
  809.9 28.9 all-gather.26
  888.6 37.9 reduce-scatter.16
  931.6 28.9 all-gather.26
  1010.3 37.9 reduce-scatter.16
  1057.0 99.0 reduce-scatter.10
  1162.8 97.9 reduce-scatter.6
  1266.7 105.9 reduce-scatter.8
  1380.2 134.6 reduce-scatter.14
  1521.4 134.5 reduce-scatter.12
where the time goes:
time: 1680 us; the launch traced here: 1660 us
  waiting for transfers between devices  954 us (57%)
  matrix products  381 us (23%)
  local copies, waits for them, and re-layouts  176 us (10%)
  other arithmetic  94.7 us (6%)
  blocking collectives  40 us (2%)
  between operations  16.8 us (1%)
    reduce_scatter x1, waiting for transfers between devices, on_device(): lax.psum_scatter(grad_down, ('dp', 'seq'), scatter_dimension=0, tiled=True)  142 us
    reduce_scatter x1, waiting for transfers between devices, on_device(): lax.psum_scatter(grad_up, ('dp', 'seq'), scatter_dimension=0, tiled=True)  141 us
    reduce_scatter x4, waiting for transfers between devices, doc_backward(): lax.psum_scatter(terms.astype(jnp.bfloat16), 'seq', scatter_dimension=0,...  129 us
    all_gather x4, waiting for transfers between devices, doc_forward(): gathered = lax.all_gather(keyval_block, 'seq', axis=0, tiled=True)  117 us
    all_gather x4, waiting for transfers between devices, doc_backward(): gathered = lax.all_gather(keyval_block, 'seq', axis=0, tiled=True)  117 us
    reduce_scatter x1, waiting for transfers between devices, on_device(): lax.psum_scatter(grad_wkv, ('dp', 'seq'), scatter_dimension=0, tiled=True)  107 us
    add x4, other arithmetic, doc_backward(): running + scores_low.astype(SINGLE)  67.1 us
    dot_general x4, matrix products, doc_backward(): jnp.einsum('ihd,jhd->hij', query_block, key_rows, preferred_element_type=...  60.5 us
  transfers between devices with their start and end apart: 22, of which 20 were waited for; matrix products, arithmetic and copies ran while one was open for 18% of the time, Pallas kernels for 0%

commit v1 on v0

v1 whole, which is shorter than its diff:
```python
import functools
import math

import jax
import jax.numpy as jnp
from jax import lax
from jax.experimental import pallas as pl
from jax.experimental.pallas import tpu as pltpu
from jax.sharding import PartitionSpec as P

EPSILON = 1e-06
BFLOAT = jnp.bfloat16
SINGLE = jnp.float32
FIXED = 8191.0
GELU_A = math.sqrt(2.0 / math.pi)
GELU_B = 0.044715
VMEM_LIMIT = 60 << 20


def nn(left, right):
    return jnp.dot(left, right, preferred_element_type=SINGLE)


def nt(left, right):
    return lax.dot_general(left, right, (((1,), (1,)), ((), ())), preferred_element_type=SINGLE)


def tn(left, right):
    return lax.dot_general(left, right, (((0,), (0,)), ((), ())), preferred_element_type=SINGLE)


def whole(shape):
    zeros = (0,) * len(shape)
    return pl.BlockSpec(shape, lambda *_: zeros, pipeline_mode=pl.Buffered(1))


def params():
    return pltpu.CompilerParams(vmem_limit_bytes=VMEM_LIMIT)


def cost(flops, moved):
    return pl.CostEstimate(flops=int(flops), bytes_accessed=int(moved), transcendentals=0)


def scale_of(values):
    return lax.rsqrt(jnp.mean(values * values, axis=-1, keepdims=True) + EPSILON)


def norm_back(values, scale, scaled_grad):
    dot = jnp.mean(values * scaled_grad, axis=-1, keepdims=True)
    return scale * (scaled_grad - values * (scale * scale * dot))


def first_lanes(shape, head_dim):
    return lax.broadcasted_iota(jnp.int32, shape, 1) < head_dim


def project_kernel(x_ref, gain_ref, wq_ref, wkv_ref, q_ref, kv_ref):
    values = x_ref[...].astype(SINGLE)
    normed = (values * scale_of(values) * gain_ref[...]).astype(BFLOAT)
    q_ref[...] = nn(normed, wq_ref[...]).astype(BFLOAT)
    kv_ref[...] = nn(normed, wkv_ref[...]).astype(BFLOAT)


def project(tokens, gain, w_query, w_keyval):
    rows, width = tokens.shape
    block = math.gcd(rows, 256)
    return pl.pallas_call(
        project_kernel,
        grid=(rows // block,),
        in_specs=[
            pl.BlockSpec((block, width), lambda i: (i, 0)),
            whole((1, width)),
            whole(w_query.shape),
            whole(w_keyval.shape),
        ],
        out_specs=[
            pl.BlockSpec((block, width), lambda i: (i, 0)),
            pl.BlockSpec((block, 2 * width), lambda i: (i, 0)),
        ],
        out_shape=[
            jax.ShapeDtypeStruct((rows, width), BFLOAT),
            jax.ShapeDtypeStruct((rows, 2 * width), BFLOAT),
        ],
        compiler_params=params(),
        cost_estimate=cost(6 * rows * width * width, 12 * rows * width),
    )(tokens, gain.reshape(1, width), w_query, w_keyval)


def doc_forward_kernel(q_ref, k_ref, v_ref, table_ref, bucket_ref, mix_ref, prob_ref):
    rows, width = q_ref.shape
    keys = k_ref.shape[0]
    heads = prob_ref.shape[0]
    head_dim = width // heads

    def pair(step, carry):
        lanes = pl.ds(pl.multiple_of(step * 2 * head_dim, 128), 2 * head_dim)
        q_pair = q_ref[:, lanes]
        k_pair = k_ref[:, lanes]
        v_pair = v_ref[:, lanes]
        wide = first_lanes(q_pair.shape, head_dim)
        tall = first_lanes(v_pair.shape, head_dim)
        table = jnp.broadcast_to(table_ref[pl.ds(step, 1), :], (rows, 128))
        packed = jnp.concatenate(
            [
                jnp.take_along_axis(
                    table,
                    bucket_ref[:, part * 128 : part * 128 + 128].astype(jnp.int32),
                    axis=1,
                    mode="promise_in_bounds",
                )
                for part in range(keys // 128)
            ],
            1,
        )
        total = None
        for side in range(2):
            mine = wide if side == 0 else ~wide
            mine_tall = tall if side == 0 else ~tall
            coded = (packed >> 16) if side == 0 else ((packed << 16) >> 16)
            scores = nt(jnp.where(mine, q_pair, 0), k_pair)
            scores = scores + coded.astype(SINGLE) * (1.0 / FIXED)
            shifted = jnp.exp(scores - jnp.max(scores, axis=-1, keepdims=True))
            inverse = 1.0 / jnp.sum(shifted, axis=-1, keepdims=True)
            soft = (shifted * inverse).astype(BFLOAT)
            prob_ref[2 * step + side] = soft
            term = nn(soft, jnp.where(mine_tall, v_pair, 0))
            total = term if total is None else total + term
        mix_ref[:, lanes] = total.astype(BFLOAT)
        return carry

    lax.fori_loop(0, heads // 2, pair, 0)


def doc_forward(q_rows, kv_rows, table, buckets, n_docs, rows, heads):
    width = q_rows.shape[1]
    keys = buckets.shape[1]
    block = math.gcd(rows, 256)
    steps = rows // block
    return pl.pallas_call(
        doc_forward_kernel,
        grid=(n_docs, steps),
        in_specs=[
            pl.BlockSpec((block, width), lambda d, i: (d * steps + i, 0)),
            pl.BlockSpec((keys, width), lambda d, i: (d, 0)),
            pl.BlockSpec((keys, width), lambda d, i: (d, 1)),
            whole(table.shape),
            pl.BlockSpec((block, keys), lambda d, i: (i, 0)),
        ],
        out_specs=[
            pl.BlockSpec((block, width), lambda d, i: (d * steps + i, 0)),
            pl.BlockSpec((heads, block, keys), lambda d, i: (0, d * steps + i, 0)),
        ],
        out_shape=[
            jax.ShapeDtypeStruct((n_docs * rows, width), BFLOAT),
            jax.ShapeDtypeStruct((heads, n_docs * rows, keys), BFLOAT),
        ],
        compiler_params=params(),
        cost_estimate=cost(30 * n_docs * rows * keys * width, 2 * heads * n_docs * rows * keys),
    )(q_rows, kv_rows, kv_rows, table, buckets)


def bucket_products(bucket_rows, grad_rows, labels):
    rows, keys = bucket_rows.shape
    numbers = bucket_rows.astype(jnp.int32)
    names = lax.broadcasted_iota(jnp.int32, (labels, keys), 0)
    parts = [
        jnp.where(jnp.broadcast_to(numbers[r : r + 1, :], (labels, keys)) == names, 1.0, 0.0).astype(
            BFLOAT
        )
        for r in range(rows)
    ]
    onehot = jnp.concatenate(parts, 0)
    return nt(onehot, grad_rows)


def attend_back(q_pair, k_pair, v_pair, da_pair, mix_pair, probs, head_dim):
    wide = first_lanes(q_pair.shape, head_dim)
    tall = first_lanes(k_pair.shape, head_dim)
    product = da_pair.astype(SINGLE) * mix_pair.astype(SINGLE)
    dq = dk = dv = None
    kept = []
    for side in range(2):
        mine = wide if side == 0 else ~wide
        mine_tall = tall if side == 0 else ~tall
        da_mine = jnp.where(mine, da_pair, 0)
        correction = jnp.sum(jnp.where(mine, product, 0.0), axis=-1, keepdims=True)
        grad_soft = nt(da_mine, v_pair)
        soft = probs[side]
        grad_scores = (soft.astype(SINGLE) * (grad_soft - correction)).astype(BFLOAT)
        kept.append(grad_scores)
        dq_term = nn(grad_scores, jnp.where(mine_tall, k_pair, 0))
        dk_term = tn(grad_scores, jnp.where(mine, q_pair, 0))
        dv_term = tn(soft, da_mine)
        dq = dq_term if dq is None else dq + dq_term
        dk = dk_term if dk is None else dk + dk_term
        dv = dv_term if dv is None else dv + dv_term
    return dq, dk, dv, kept


def doc_backward_kernel(
    labels,
    q_ref,
    k_ref,
    v_ref,
    da_ref,
    mix_ref,
    prob_ref,
    bucket_ref,
    dq_ref,
    dk_ref,
    dv_ref,
    sums_ref,
    dk_acc,
    dv_acc,
    ds_keep,
):
    rows, width = q_ref.shape
    heads = prob_ref.shape[0]
    keys = k_ref.shape[0]
    head_dim = width // heads
    doc, step_i = pl.program_id(0), pl.program_id(1)

    @pl.when(step_i == 0)
    def _():
        dk_acc[...] = jnp.zeros_like(dk_acc)
        dv_acc[...] = jnp.zeros_like(dv_acc)

    @pl.when((step_i == 0) & (doc == 0))
    def _():
        sums_ref[...] = jnp.zeros_like(sums_ref)

    def pair(step, carry):
        lanes = pl.ds(pl.multiple_of(step * 2 * head_dim, 128), 2 * head_dim)
        dq, dk, dv, kept = attend_back(
            q_ref[:, lanes],
            k_ref[:, lanes],
            v_ref[:, lanes],
            da_ref[:, lanes],
            mix_ref[:, lanes],
            [prob_ref[2 * step], prob_ref[2 * step + 1]],
            head_dim,
        )
        ds_keep[2 * step] = kept[0]
        ds_keep[2 * step + 1] = kept[1]
        dq_ref[:, lanes] = dq.astype(BFLOAT)
        dk_acc[:, lanes] += dk
        dv_acc[:, lanes] += dv
        return carry

    lax.fori_loop(0, heads // 2, pair, 0)

    def group(number, carry):
        span = pl.ds(pl.multiple_of(number * 16, 16), 16)
        sums_ref[...] += bucket_products(
            bucket_ref[span, :], ds_keep[:, span, :].reshape(heads * 16, keys), labels
        )
        return carry

    lax.fori_loop(0, rows // 16, group, 0)

    @pl.when(step_i == pl.num_programs(1) - 1)
    def _():
        dk_ref[...] = dk_acc[...].astype(BFLOAT)
        dv_ref[...] = dv_acc[...].astype(BFLOAT)


def doc_backward(q_rows, kv_rows, da_rows, mixture, probs, buckets, n_docs, rows, labels):
    width = q_rows.shape[1]
    heads = probs.shape[0]
    keys = buckets.shape[1]
    block = math.gcd(rows, 256)
    steps = rows // block
    along = pl.BlockSpec((block, width), lambda d, i: (d * steps + i, 0))
    per_doc = pl.BlockSpec((keys, width), lambda d, i: (d, 0))
    return pl.pallas_call(
        functools.partial(doc_backward_kernel, labels),
        grid=(n_docs, steps),
        in_specs=[
            along,
            per_doc,
            pl.BlockSpec((keys, width), lambda d, i: (d, 1)),
            along,
            along,
            pl.BlockSpec((heads, block, keys), lambda d, i: (0, d * steps + i, 0)),
            pl.BlockSpec((block, keys), lambda d, i: (i, 0)),
        ],
        out_specs=[along, per_doc, per_doc, whole((16 * labels, heads * 16))],
        out_shape=[
            jax.ShapeDtypeStruct((n_docs * rows, width), BFLOAT),
            jax.ShapeDtypeStruct((n_docs * keys, width), BFLOAT),
            jax.ShapeDtypeStruct((n_docs * keys, width), BFLOAT),
            jax.ShapeDtypeStruct((16 * labels, heads * 16), SINGLE),
        ],
        scratch_shapes=[
            pltpu.VMEM((keys, width), SINGLE),
            pltpu.VMEM((keys, width), SINGLE),
            pltpu.VMEM((heads, block, keys), BFLOAT),
        ],
        compiler_params=params(),
        cost_estimate=cost(70 * n_docs * rows * keys * width, 2 * heads * n_docs * rows * keys),
    )(q_rows, kv_rows, kv_rows, da_rows, mixture, probs, buckets)


def query_forward_kernel(q_ref, kv_ref, table_ref, bucket_ref, mix_ref, prob_ref):
    rows, width = q_ref.shape
    heads = prob_ref.shape[0]
    head_dim = width // heads
    index = bucket_ref[...]
    for step in range(heads // 2):
        lanes = slice(step * 2 * head_dim, (step + 1) * 2 * head_dim)
        q_pair = q_ref[:, lanes]
        k_pair = kv_ref[:, lanes]
        v_pair = kv_ref[:, width + lanes.start : width + lanes.stop]
        wide = first_lanes(q_pair.shape, head_dim)
        total = None
        for side in range(2):
            head = 2 * step + side
            mine = wide if side == 0 else ~wide
            table = jnp.broadcast_to(table_ref[head : head + 1, :], (rows, 128))
            bias = jnp.take_along_axis(table, index, axis=1, mode="promise_in_bounds")
            scores = nt(jnp.where(mine, q_pair, 0), k_pair) + bias
            shifted = jnp.exp(scores - jnp.max(scores, axis=-1, keepdims=True))
            inverse = 1.0 / jnp.sum(shifted, axis=-1, keepdims=True)
            soft = (shifted * inverse).astype(BFLOAT)
            prob_ref[head] = soft
            term = nn(soft, jnp.where(mine, v_pair, 0))
            total = term if total is None else total + term
        mix_ref[:, lanes] = total.astype(BFLOAT)


def query_forward(q_rows, kv_rows, table, buckets, start, count, heads):
    width = q_rows.shape[1]
    offset = start // 128
    return pl.pallas_call(
        query_forward_kernel,
        grid=(count // 128,),
        in_specs=[
            pl.BlockSpec((128, width), lambda i: (offset + i, 0)),
            pl.BlockSpec((128, 2 * width), lambda i: (offset + i, 0)),
            whole(table.shape),
            whole(buckets.shape),
        ],
        out_specs=[
            pl.BlockSpec((128, width), lambda i: (i, 0)),
            pl.BlockSpec((heads, 128, 128), lambda i: (0, i, 0)),
        ],
        out_shape=[
            jax.ShapeDtypeStruct((count, width), BFLOAT),
            jax.ShapeDtypeStruct((heads, count, 128), BFLOAT),
        ],
        compiler_params=params(),
        cost_estimate=cost(4 * count * 128 * width * 4, 10 * count * width),
    )(q_rows, kv_rows, table, buckets)


def query_backward_kernel(
    labels, q_ref, kv_ref, da_ref, mix_ref, prob_ref, bucket_ref, dq_ref, dkv_ref, sums_ref, ds_keep
):
    rows, width = q_ref.shape
    heads = prob_ref.shape[0]
    head_dim = width // heads

    @pl.when(pl.program_id(0) == 0)
    def _():
        sums_ref[...] = jnp.zeros_like(sums_ref)

    for step in range(heads // 2):
        lanes = slice(step * 2 * head_dim, (step + 1) * 2 * head_dim)
        right = slice(width + lanes.start, width + lanes.stop)
        dq, dk, dv, kept = attend_back(
            q_ref[:, lanes],
            kv_ref[:, lanes],
            kv_ref[:, right],
            da_ref[:, lanes],
            mix_ref[:, lanes],
            [prob_ref[2 * step], prob_ref[2 * step + 1]],
            head_dim,
        )
        ds_keep[2 * step] = kept[0]
        ds_keep[2 * step + 1] = kept[1]
        dq_ref[:, lanes] = dq.astype(BFLOAT)
        dkv_ref[:, lanes] = dk.astype(BFLOAT)
        dkv_ref[:, right] = dv.astype(BFLOAT)

    def group(number, carry):
        span = pl.ds(pl.multiple_of(number * 16, 16), 16)
        sums_ref[...] += bucket_products(
            bucket_ref[span, :], ds_keep[:, span, :].reshape(heads * 16, rows), labels
        )
        return carry

    lax.fori_loop(0, rows // 16, group, 0)


def query_backward(q_rows, kv_rows, da_rows, mixture, probs, buckets, start, labels):
    width = q_rows.shape[1]
    heads, count, _ = probs.shape
    offset = start // 128
    return pl.pallas_call(
        functools.partial(query_backward_kernel, labels),
        grid=(count // 128,),
        in_specs=[
            pl.BlockSpec((128, width), lambda i: (offset + i, 0)),
            pl.BlockSpec((128, 2 * width), lambda i: (offset + i, 0)),
            pl.BlockSpec((128, width), lambda i: (offset + i, 0)),
            pl.BlockSpec((128, width), lambda i: (offset + i, 0)),
            pl.BlockSpec((heads, 128, 128), lambda i: (0, i, 0)),
            whole(buckets.shape),
        ],
        out_specs=[
            pl.BlockSpec((128, width), lambda i: (i, 0)),
            pl.BlockSpec((128, 2 * width), lambda i: (i, 0)),
            whole((16 * labels, heads * 16)),
        ],
        out_shape=[
            jax.ShapeDtypeStruct((count, width), BFLOAT),
            jax.ShapeDtypeStruct((count, 2 * width), BFLOAT),
            jax.ShapeDtypeStruct((16 * labels, heads * 16), SINGLE),
        ],
        scratch_shapes=[pltpu.VMEM((heads, 128, 128), BFLOAT)],
        compiler_params=params(),
        cost_estimate=cost(8 * count * 128 * width * 4, 14 * count * width),
    )(q_rows, kv_rows, da_rows, mixture, probs, buckets)


def feed_kernel(
    chunk,
    x_ref,
    mix_ref,
    dy_ref,
    gain_ref,
    wo_ref,
    wu_ref,
    wd_ref,
    y_ref,
    dh_ref,
    da_ref,
    go_ref,
    gu_ref,
    gd_ref,
    gg_ref,
    go_acc,
    gu_acc,
    gd_acc,
    stage,
    sems,
):
    step = pl.program_id(0)
    hidden = wu_ref.shape[1]
    width = wu_ref.shape[0]

    @pl.when(step == 0)
    def _():
        go_acc[...] = jnp.zeros_like(go_acc)
        gu_acc[...] = jnp.zeros_like(gu_acc)
        gd_acc[...] = jnp.zeros_like(gd_acc)
        gg_ref[...] = jnp.zeros_like(gg_ref)

    mixture = mix_ref[...]
    dy = dy_ref[...]
    gain = gain_ref[...]
    residual = x_ref[...].astype(SINGLE) + nn(mixture, wo_ref[...])
    scale = scale_of(residual)
    second = (residual * scale * gain).astype(BFLOAT)
    y = residual
    grad_second = jnp.zeros_like(residual)
    for part in range(hidden // chunk):
        span = slice(part * chunk, (part + 1) * chunk)
        pre = nn(second, wu_ref[:, span])
        grad_hidden = nt(dy, wd_ref[span, :])
        square = pre * pre
        tanh = jnp.tanh(pre * (GELU_A + (GELU_A * GELU_B) * square))
        half = 0.5 + 0.5 * tanh
        act = pre * half
        slope = half + act * (1.0 - tanh) * (GELU_A + (3.0 * GELU_A * GELU_B) * square)
        act_low = act.astype(BFLOAT)
        grad_pre = (grad_hidden * slope).astype(BFLOAT)
        y = y + nn(act_low, wd_ref[span, :])
        grad_second = grad_second + nt(grad_pre, wu_ref[:, span])
        gd_acc[span, :] += tn(act_low, dy)
        gu_acc[:, span] += tn(second, grad_pre)
    y_ref[...] = y.astype(BFLOAT)
    gg_ref[...] += jnp.sum(grad_second * residual * scale, axis=0, keepdims=True)
    grad_res = dy.astype(SINGLE) + norm_back(residual, scale, grad_second * gain)
    dh_ref[...] = grad_res
    grad_low = grad_res.astype(BFLOAT)
    da_ref[...] = nt(grad_low, wo_ref[...]).astype(BFLOAT)
    go_acc[...] += tn(mixture, grad_low)

    @pl.when(step == pl.num_programs(0) - 1)
    def _():
        pieces = []
        rows, columns = stage.shape[1:]
        for acc, out in ((gd_acc, gd_ref), (gu_acc, gu_ref), (go_acc, go_ref)):
            for r in range(acc.shape[0] // rows):
                for c in range(acc.shape[1] // columns):
                    spot = (pl.ds(r * rows, rows), pl.ds(c * columns, columns))
                    pieces.append((acc, out, spot))
        flying = [None, None]
        for number, (acc, out, spot) in enumerate(pieces):
            slot = number % 2
            if flying[slot] is not None:
                flying[slot].wait()
            stage[slot] = acc[spot].astype(BFLOAT)
            flying[slot] = pltpu.make_async_copy(stage.at[slot], out.at[spot], sems.at[slot])
            flying[slot].start()
        for copy in flying:
            if copy is not None:
                copy.wait()


def feed(tokens, mixture, cotangent, gain, w_out, w_up, w_down):
    rows, width = tokens.shape
    hidden = w_up.shape[1]
    block = math.gcd(rows, 256)
    along = pl.BlockSpec((block, width), lambda i: (i, 0))
    anywhere = pl.BlockSpec(memory_space=pl.ANY)
    return pl.pallas_call(
        functools.partial(feed_kernel, math.gcd(hidden, 768)),
        grid=(rows // block,),
        in_specs=[
            along,
            along,
            along,
            whole((1, width)),
            whole(w_out.shape),
            whole(w_up.shape),
            whole(w_down.shape),
        ],
        out_specs=[along, along, along, anywhere, anywhere, anywhere, whole((1, width))],
        out_shape=[
            jax.ShapeDtypeStruct((rows, width), BFLOAT),
            jax.ShapeDtypeStruct((rows, width), SINGLE),
            jax.ShapeDtypeStruct((rows, width), BFLOAT),
            jax.ShapeDtypeStruct(w_out.shape, BFLOAT),
            jax.ShapeDtypeStruct(w_up.shape, BFLOAT),
            jax.ShapeDtypeStruct(w_down.shape, BFLOAT),
            jax.ShapeDtypeStruct((1, width), SINGLE),
        ],
        scratch_shapes=[
            pltpu.VMEM(w_out.shape, SINGLE),
            pltpu.VMEM(w_up.shape, SINGLE),
            pltpu.VMEM(w_down.shape, SINGLE),
            pltpu.VMEM((2, width, width), BFLOAT),
            pltpu.SemaphoreType.DMA((2,)),
        ],
        compiler_params=params(),
        cost_estimate=cost(2 * rows * width * (6 * hidden + 3 * width), 14 * rows * width),
    )(tokens, mixture, cotangent, gain.reshape(1, width), w_out, w_up, w_down)


def unproject_kernel(
    x_ref, gain_ref, dq_ref, dk_ref, dv_ref, dh_ref, wq_ref, wkv_ref, dx_ref, gq_ref, gkv_ref, gg_ref, gq_acc, gkv_acc
):
    step = pl.program_id(0)
    width = wq_ref.shape[0]

    @pl.when(step == 0)
    def _():
        gq_acc[...] = jnp.zeros_like(gq_acc)
        gkv_acc[...] = jnp.zeros_like(gkv_acc)
        gg_ref[...] = jnp.zeros_like(gg_ref)

    values = x_ref[...].astype(SINGLE)
    gain = gain_ref[...]
    scale = scale_of(values)
    normed = (values * scale * gain).astype(BFLOAT)
    dq, dk, dv = dq_ref[...], dk_ref[...], dv_ref[...]
    gq_acc[...] += tn(normed, dq)
    gkv_acc[:, :width] += tn(normed, dk)
    gkv_acc[:, width:] += tn(normed, dv)
    grad = nt(dq, wq_ref[...]) + nt(dk, wkv_ref[:, :width]) + nt(dv, wkv_ref[:, width:])
    gg_ref[...] += jnp.sum(grad * values * scale, axis=0, keepdims=True)
    dx_ref[...] = dh_ref[...] + norm_back(values, scale, grad * gain)

    @pl.when(step == pl.num_programs(0) - 1)
    def _():
        gq_ref[...] = gq_acc[...].astype(BFLOAT)
        gkv_ref[...] = gkv_acc[...].astype(BFLOAT)


def unproject(tokens, gain, dq, dk, dv, grad_res, w_query, w_keyval):
    rows, width = tokens.shape
    block = math.gcd(rows, 256)
    along = pl.BlockSpec((block, width), lambda i: (i, 0))
    return pl.pallas_call(
        unproject_kernel,
        grid=(rows // block,),
        in_specs=[
            along,
            whole((1, width)),
            along,
            along,
            along,
            along,
            whole(w_query.shape),
            whole(w_keyval.shape),
        ],
        out_specs=[along, whole(w_query.shape), whole(w_keyval.shape), whole((1, width))],
        out_shape=[
            jax.ShapeDtypeStruct((rows, width), SINGLE),
            jax.ShapeDtypeStruct(w_query.shape, BFLOAT),
            jax.ShapeDtypeStruct(w_keyval.shape, BFLOAT),
            jax.ShapeDtypeStruct((1, width), SINGLE),
        ],
        scratch_shapes=[pltpu.VMEM(w_query.shape, SINGLE), pltpu.VMEM(w_keyval.shape, SINGLE)],
        compiler_params=params(),
        cost_estimate=cost(12 * rows * width * width, 18 * rows * width),
    )(tokens, gain.reshape(1, width), dq, dk, dv, grad_res, w_query, w_keyval)


def bits_of(count):
    return [1 << place for place in reversed(range(count.bit_length() - 1))]


def axis_bits():
    dp_bits = [("dp", bit) for bit in bits_of(lax.axis_size("dp"))]
    seq_bits = [("seq", bit) for bit in bits_of(lax.axis_size("seq"))]
    return dp_bits, seq_bits


def gather_orders():
    dp_bits, seq_bits = axis_bits()
    far = (len(dp_bits) + 1) // 2
    z_bits, x_bits = dp_bits[:far], dp_bits[far:]
    y_bits, core_bits = seq_bits[:-1], seq_bits[-1:]
    return [z_bits + y_bits + x_bits + core_bits, z_bits + x_bits + y_bits + core_bits]


def swap(values, name, bit):
    count = lax.axis_size(name)
    return lax.ppermute(values, name, [(i, i ^ bit) for i in range(count)])


def is_high(name, bit):
    return (lax.axis_index(name) & bit) != 0


def gather_rows(shard, order):
    dp_bits, seq_bits = axis_bits()
    everything = dp_bits + seq_bits
    done = []
    held = shard
    for item in order:
        other = swap(held, *item)
        done.append(item)
        place = sorted(everything.index(one) for one in done).index(everything.index(item))
        high = is_high(*item)
        held = jnp.where(
            high, jnp.stack([other, held], place), jnp.stack([held, other], place)
        )
    return held.reshape(-1, shard.shape[1])


def gather_weights(shards, orders):
    pieces = []
    for shard, order in zip(shards, orders):
        pieces.append(gather_rows(shard, order))
    return pieces


def scatter_rows(values, order):
    dp_bits, seq_bits = axis_bits()
    left = dp_bits + seq_bits
    rows = values.shape[0] >> len(left)
    held = values.reshape((2,) * len(left) + (rows, values.shape[1]))
    for item in order:
        place = left.index(item)
        mine = is_high(*item).astype(jnp.int32)
        away = lax.dynamic_index_in_dim(held, 1 - mine, place, keepdims=False)
        kept = lax.dynamic_index_in_dim(held, mine, place, keepdims=False)
        other = swap(away, *item)
        held = kept.astype(SINGLE) + other.astype(SINGLE)
        left.remove(item)
        if left:
            held = held.astype(BFLOAT)
    return held


def scatter_columns(values, parts):
    orders = [order[::-1] for order in gather_orders()]
    columns = values.shape[1] // parts
    return jnp.concatenate(
        [
            scatter_rows(values[:, p * columns : (p + 1) * columns], orders[p % len(orders)])
            for p in range(parts)
        ],
        1,
    )


def sum_all(values):
    dp_bits, seq_bits = axis_bits()
    for item in seq_bits[::-1] + dp_bits[::-1]:
        values = values + swap(values, *item)
    return values


def own_document(shard):
    count = lax.axis_size("seq")
    n_docs = shard.shape[0]
    me = lax.axis_index("seq")
    if n_docs >= count:
        per = n_docs // count
        blocks = shard.reshape((count, per) + shard.shape[1:])
        sets, group = count, 1
    else:
        blocks = shard[:, None]
        sets, group = n_docs, count // n_docs
    got = []
    for r in range(sets):
        piece = lax.dynamic_index_in_dim(blocks, (me % sets) ^ r, 0, keepdims=False)
        route = [
            (u * sets + i, (i ^ r) * group + u) for u in range(group) for i in range(sets)
        ]
        if any(a != b for a, b in route):
            piece = lax.ppermute(piece, "seq", route)
        got.append(piece)
    stacked = jnp.stack(got, 0)
    mine = me // group
    ordered = [lax.dynamic_index_in_dim(stacked, mine ^ i, 0, keepdims=False) for i in range(sets)]
    return jnp.concatenate(ordered, 1).reshape(-1, shard.shape[-1])


def spread_document(rows, like):
    count = lax.axis_size("seq")
    n_docs, shard_rows, width = like.shape
    me = lax.axis_index("seq")
    if n_docs >= count:
        per = n_docs // count
        sets, group = count, 1
    else:
        per = 1
        sets, group = n_docs, count // n_docs
    blocks = rows.reshape(per, sets, shard_rows, width)
    mine = me // group
    got = []
    for r in range(sets):
        piece = lax.dynamic_index_in_dim(blocks, mine ^ r, 1, keepdims=False)
        route = [
            ((i ^ r) * group + u, u * sets + i) for u in range(group) for i in range(sets)
        ]
        if any(a != b for a, b in route):
            piece = lax.ppermute(piece, "seq", route)
        got.append(piece)
    stacked = jnp.stack(got, 0)
    ordered = [
        lax.dynamic_index_in_dim(stacked, (me % sets) ^ i, 0, keepdims=False) for i in range(sets)
    ]
    return jnp.concatenate(ordered, 0)


def gather_positions(shard):
    seq_bits = axis_bits()[1]
    done = []
    held = shard
    for item in seq_bits:
        other = swap(held, *item)
        high = is_high(*item)
        place = len(done)
        held = jnp.where(
            high, jnp.stack([other, held], place), jnp.stack([held, other], place)
        )
        done.append(item)
    return held.reshape(-1, shard.shape[1])


def on_device(
    doc_tokens,
    queries,
    doc_cot,
    query_cot,
    q_weight,
    kv_weight,
    out_weight,
    up_weight,
    down_weight,
    attn_gain,
    ff_gain,
    rel_bias,
    doc_buckets,
    query_buckets,
    topk_mask,
    positives,
    pos_count,
):
    n_docs, shard_rows, width = doc_tokens.shape
    n_query, query_len, _ = queries.shape
    bucket_count, heads = rel_bias.shape
    doc_len = doc_buckets.shape[1]
    doc_rows = n_docs * shard_rows
    query_total = n_query * query_len
    seq_size = lax.axis_size("seq")
    group = max(1, seq_size // n_docs)
    local_docs = max(1, n_docs // seq_size)
    local_rows = doc_len // group
    orders = gather_orders()

    tokens = jnp.concatenate(
        [own_document(doc_tokens), queries.reshape(query_total, width)], 0
    )
    w_query, w_key, w_value = gather_weights(
        [q_weight, kv_weight[:, :width], kv_weight[:, width:]], [orders[0], orders[1], orders[0]]
    )
    w_keyval = jnp.concatenate([w_key, w_value], 1)
    buckets = gather_positions(doc_buckets.astype(jnp.int16))
    if group > 1:
        part = lax.axis_index("seq") % group
        buckets = lax.dynamic_slice_in_dim(buckets, part * local_rows, local_rows, 0)

    fixed = jnp.round(rel_bias.T * FIXED).astype(jnp.int32)
    packed = (fixed[0::2] << 16) | (fixed[1::2] & 0xFFFF)
    doc_table = jnp.zeros((8, 128), jnp.int32).at[: heads // 2, :bucket_count].set(packed)
    query_table = jnp.zeros((16, 128), SINGLE).at[:heads, :bucket_count].set(rel_bias.T)
    query_table = query_table.at[:, bucket_count].set(-1e30)
    repeats = 128 // query_len
    same = jnp.kron(jnp.eye(repeats, dtype=jnp.int32), jnp.ones_like(query_buckets))
    tiled = jnp.where(same == 1, jnp.tile(query_buckets, (repeats, repeats)), bucket_count)

    q_rows, kv_rows = project(tokens, attn_gain, w_query, w_keyval)
    if group > 1:
        teams = [list(range(t * group, (t + 1) * group)) for t in range(seq_size // group)]
        kv_docs = lax.all_gather(
            kv_rows[:doc_rows], "seq", axis=0, tiled=True, axis_index_groups=teams
        )
    else:
        kv_docs = kv_rows
    doc_mix, doc_probs = doc_forward(
        q_rows, kv_docs, doc_table, buckets, local_docs, local_rows, heads
    )
    query_mix, query_probs = query_forward(
        q_rows, kv_rows, query_table, tiled, doc_rows, query_total, heads
    )
    mixture = jnp.concatenate([doc_mix, query_mix], 0)
    half = out_weight.shape[1] // 2
    half_up = up_weight.shape[1] // 2
    o1, o2, u1, u2, d1, d2 = gather_weights(
        [
            out_weight[:, :half],
            out_weight[:, half:],
            up_weight[:, :half_up],
            up_weight[:, half_up:],
            down_weight[:, :half],
            down_weight[:, half:],
        ],
        [orders[0], orders[1]] * 3,
    )
    w_out = jnp.concatenate([o1, o2], 1)
    w_up = jnp.concatenate([u1, u2], 1)
    w_down = jnp.concatenate([d1, d2], 1)
    cotangent = jnp.concatenate(
        [own_document(doc_cot), query_cot.reshape(query_total, width)], 0
    )
    outputs, grad_res, grad_mix, grad_out, grad_up, grad_down, grad_ff = feed(
        tokens, mixture, cotangent, ff_gain, w_out, w_up, w_down
    )
    grad_down_shard = scatter_columns(grad_down, 2)
    grad_up_shard = scatter_columns(grad_up, 2)
    grad_out_shard = scatter_columns(grad_out, 2)
    doc_out = spread_document(outputs[:doc_rows], doc_tokens)
    query_out = outputs[doc_rows:].reshape(queries.shape)

    doc_dq, doc_dk, doc_dv, doc_sums = doc_backward(
        q_rows, kv_docs, grad_mix, doc_mix, doc_probs, buckets, local_docs, local_rows, bucket_count
    )
    if group > 1:
        both = jnp.concatenate([doc_dk, doc_dv], 1)
        both = lax.psum_scatter(
            both, "seq", scatter_dimension=0, tiled=True, axis_index_groups=teams
        )
        doc_dk, doc_dv = both[:, :width], both[:, width:]
    query_dq, query_dkv, query_sums = query_backward(
        q_rows, kv_rows, grad_mix, mixture, query_probs, tiled, doc_rows, bucket_count
    )
    dq = jnp.concatenate([doc_dq, query_dq], 0)
    dk = jnp.concatenate([doc_dk, query_dkv[:, :width]], 0)
    dv = jnp.concatenate([doc_dv, query_dkv[:, width:]], 0)
    grad_tokens, grad_q, grad_kv, grad_attn = unproject(
        tokens, attn_gain, dq, dk, dv, grad_res, w_query, w_keyval
    )
    grad_q_shard = scatter_columns(grad_q, 2)
    grad_kv_shard = scatter_columns(grad_kv, 2)
    doc_dx = spread_document(grad_tokens[:doc_rows].astype(BFLOAT), doc_tokens).astype(SINGLE)
    query_dx = grad_tokens[doc_rows:].reshape(queries.shape)

    sums = (doc_sums + query_sums).reshape(16, bucket_count, heads, 16)
    keep = jnp.eye(16, dtype=SINGLE)[:, None, None, :]
    bias_local = jnp.sum(sums * keep, axis=(0, 3))
    matches = positives[:, :, None] == jnp.arange(doc_len, dtype=jnp.int32)[None, None, :]
    counted = jnp.arange(positives.shape[1], dtype=jnp.int32)[None, :] < pos_count[:, None]
    retrieved = jnp.sum(
        jnp.where(matches & counted[:, :, None], topk_mask[:, None, :].astype(SINGLE), 0.0)
    )
    flat = jnp.concatenate(
        [grad_attn[0], grad_ff[0], bias_local.reshape(-1), jnp.full((128,), retrieved)]
    )
    total = sum_all(flat)
    slots = float(n_query * lax.axis_size("dp") * seq_size * positives.shape[1])
    return (
        doc_out,
        query_out,
        doc_dx,
        query_dx,
        grad_q_shard,
        grad_kv_shard,
        grad_out_shard,
        grad_up_shard,
        grad_down_shard,
        total[:width],
        total[width : 2 * width],
        total[2 * width : 2 * width + bucket_count * heads].reshape(bucket_count, heads),
        total[-1] / slots,
    )


def solution(mesh):
    rows_all = P(("dp", "seq"), None)
    return jax.shard_map(
        on_device,
        mesh=mesh,
        in_specs=(
            P("dp", "seq", None),
            P(("dp", "seq"), None, None),
            P("dp", "seq", None),
            P(("dp", "seq"), None, None),
            rows_all,
            rows_all,
            rows_all,
            rows_all,
            rows_all,
            P(),
            P(),
            P(),
            P("seq", None),
            P(),
            rows_all,
            rows_all,
            P(("dp", "seq")),
        ),
        out_specs=(
            P("dp", "seq", None),
            P(("dp", "seq"), None, None),
            P("dp", "seq", None),
            P(("dp", "seq"), None, None),
            rows_all,
            rows_all,
            rows_all,
            rows_all,
            rows_all,
            P(),
            P(),
            P(),
            P(),
        ),
        check_vma=False,
    )
```

time: 1680 us -> 741 us (0.44)
  waiting for transfers between devices: 954 us -> 233 us
  matrix products: 381 us -> 0 us
  Pallas kernels: 0 us -> 246 us
  starting transfers between devices: 0.6 us -> 115 us
  local copies, waits for them, and re-layouts: 176 us -> 62.3 us
  blocking collectives: 40 us -> 0 us
  other arithmetic: 94.7 us -> 68 us
    reduce_scatter x9 -> x0, waiting for transfers between devices: 519 us -> none  [the longest x1 142 us: on_device(): lax.psum_scatter(grad_down, ('dp', 'seq'), scatter_dimension=0, tiled=True)]
    all_gather x13 -> x0, waiting for transfers between devices: 430 us -> none  [the longest x4 117 us: doc_forward(): gathered = lax.all_gather(keyval_block, 'seq', axis=0, tiled=True)]
    dot_general x67 -> x0, matrix products: 381 us -> none  [the longest x4 60.5 us: doc_backward(): jnp.einsum('ihd,jhd->hij', query_block, key_rows, preferred_element_type=...]
    pallas_call x0 -> x7, Pallas kernels: none -> 246 us  [the longest x1 70 us: doc_backward(): pl.pallas_call(functools.partial(doc_backward_kernel, labels), grid=(n_do...]
    ppermute x0 -> x114, waiting for transfers between devices: none -> 233 us  [the longest x102 196 us: swap(): return lax.ppermute(values, name, [(i, i ^ bit) for i in range(count)])]
    ppermute x0 -> x114, starting transfers between devices: none -> 115 us  [the longest x102 109 us: swap(): return lax.ppermute(values, name, [(i, i ^ bit) for i in range(count)])]
    add x6 -> x16, other arithmetic: 71.7 us -> 1.26 us  [the longest x1 1.11 us: on_device(): sums = (doc_sums + query_sums).reshape(16, bucket_count, heads, 16)]
    psum x1 -> x0, blocking collectives: 40 us -> none  [on_device(): lax.psum((gain_pair, bias_local, retrieved), ('dp', 'seq'))]
  transfers between devices with their start and end apart: 22 -> 114, of which waited for: 20 -> 65; matrix products, arithmetic and copies ran while one was open for 18% -> 14% of each run, Pallas kernels for 0% -> 9%
where the time goes in v1:
time: 741 us; the launch traced here: 730 us
  Pallas kernels  246 us (33%)
  waiting for transfers between devices  233 us (31%)
  starting transfers between devices  115 us (16%)
  other arithmetic  68 us (9%)
  local copies, waits for them, and re-layouts  62.3 us (8%)
    ppermute x102, waiting for transfers between devices, swap(): return lax.ppermute(values, name, [(i, i ^ bit) for i in range(count)])  196 us
    ppermute x102, starting transfers between devices, swap(): return lax.ppermute(values, name, [(i, i ^ bit) for i in range(count)])  109 us
    pallas_call x1, Pallas kernels, doc_backward(): pl.pallas_call(functools.partial(doc_backward_kernel, labels), grid=(n_do...  70 us
    pallas_call x1, Pallas kernels, feed(): pl.pallas_call(functools.partial(feed_kernel, math.gcd(hidden, 768)), gri...  69.3 us
    pallas_call x1, Pallas kernels, doc_forward(): pl.pallas_call(doc_forward_kernel, grid=(n_docs, steps), in_specs=[pl.Blo...  47.2 us
    ppermute x6, waiting for transfers between devices, spread_document(): piece = lax.ppermute(piece, 'seq', route)  25.8 us
    select_n x78, other arithmetic, gather_rows(): jnp.where(high, jnp.stack([other, held], place), jnp.stack([held, other],...  23.1 us
    pallas_call x1, Pallas kernels, unproject(): pl.pallas_call(unproject_kernel, grid=(rows // block,), in_specs=[along,...  20.5 us
  transfers between devices with their start and end apart: 114, of which 65 were waited for; matrix products, arithmetic and copies ran while one was open for 14% of the time, Pallas kernels for 9%

profile of v1, /device:TPU:0, one launch (start us, length us, event | category | flops | bytes accessed | tf_op | source)
XLA Modules:
  0.0 729.7 jit_solution(12884956780171356360)
XLA Ops:
  2.1 4.0 collective-permute-start.8
  6.2 2.5 dynamic-slice_bitcast_fusion.27
  11.1 2.6 collective-permute-start.23
  16.6 2.5 dynamic-slice_bitcast_fusion.22
  27.5 4.7 collective-permute-done.28
  34.1 4.7 collective-permute-done.3
  40.1 2.2 collective-permute-start.29
  46.3 2.4 collective-permute-done.24
  50.7 3.3 collective-permute-done.33
  57.1 4.4 collective-permute-done.43
  63.9 2.3 collective-permute-done.9
  71.8 3.1 collective-permute-done.25
  77.1 3.5 collective-permute-done.39
  89.1 4.3 collective-permute-done.15
  95.2 3.4 collective-permute-done.5
  111.3 6.3 collective-permute-done.21
  119.2 4.7 collective-permute-done.22
  131.4 12.2 %collective-permute-done.35 = bf16[2,2,24,1536]{3,2,0,1:T(8,128)(2,1)S(1)} collective-permute-done((bf16[2,2,24,1536]{3,2,0,1:T(8,128)(2,1)S(1)}, bf16[2,2,24,1536]{3,2,0,1:T(8,128)(2,1)S(1)}, u32[]{:S(2)}, u32[]{:S(2)}) %collective-permute-start.35) | collective-permute-done | bytes 294944 | tf_op jit(solution)/shard_map/ppermute | solution.py:633
  146.0 3.9 collective-permute-done.45
  159.1 2.5 collective-permute-start.46
  163.1 7.6 %collective-permute-done.41 = bf16[2,2,2,24,1536]{4,3,0,1,2:T(8,128)(2,1)S(1)} collective-permute-done((bf16[2,2,2,24,1536]{4,3,0,1,2:T(8,128)(2,1)S(1)}, bf16[2,2,2,24,1536]{4,3,0,1,2:T(8,128)(2,1)S(1)}, u32[]{:S(2)}, u32[]{:S(2)}) %collective-permute-start.41) | collective-permute-done | bytes 589856 | tf_op jit(solution)/shard_map/ppermute | solution.py:633
  172.1 10.3 %collective-permute-done.51 = bf16[2,2,2,96,384]{4,3,0,1,2:T(8,128)(2,1)S(1)} collective-permute-done((bf16[2,2,2,96,384]{4,3,0,1,2:T(8,128)(2,1)S(1)}, bf16[2,2,2,96,384]{4,3,0,1,2:T(8,128)(2,1)S(1)}, u32[]{:S(2)}, u32[]{:S(2)}) %collective-permute-start.51) | collective-permute-done | bytes 589856 | tf_op jit(solution)/shard_map/ppermute | solution.py:633
  195.2 10.3 %shard_map.264 = (bf16[1536,768]{1,0:T(8,128)(2,1)}, bf16[1536,1536]{1,0:T(8,128)(2,1)}) custom-call(bf16[1536,768]{1,0:T(8,128)(2,1)} %pad_maximum_fusion.2.x_ref, f32[1,768]{1,0:T(1,128)} %reshape.4141.gain_ref, bf16[768,768]{1,0:T(8,128)(2,1)} %bitcast.681, bf16[768,1536]{1,0:T(8,128)(2,1)} %pad_maximum_fusion.3.wkv_ref), custom_call_target="tpu_custom_call" | custom-call | flops 5435817984 | bytes 14155776 | tf_op jit(solution)/shard_map/pallas_call | solution.py:68
  205.5 11.8 %shard_map.266 = (bf16[512,768]{1,0:T(8,128)(2,1)}, bf16[12,512,128]{2,1,0:T(8,128)(2,1)}) custom-call(bf16[1536,768]{1,0:T(8,128)(2,1)} %get-tuple-element.73.q_ref, bf16[1536,1536]{1,0:T(8,128)(2,1)} %get-tuple-element.74.k_ref.v_ref.kv_ref, f32[16,128]{1,0:T(8,128)} %copy-done.55, s32[128,128]{1,0:T(8,128)} %select_n.1264.bucket_ref), custom_call_target="tpu_custom_call" | custom-call | flops 805306368 | bytes 3932160 | tf_op jit(solution)/shard_map/pallas_call | solution.py:335
  217.3 3.8 add_select_fusion
  221.1 47.2 %shard_map.265 = (bf16[1024,768]{1,0:T(8,128)(2,1)}, bf16[12,1024,1024]{2,1,0:T(8,128)(2,1)}) custom-call(bf16[1536,768]{1,0:T(8,128)(2,1)} %get-tuple-element.73.q_ref, bf16[1536,1536]{1,0:T(8,128)(2,1)} %get-tuple-element.74.k_ref.v_ref.kv_ref, bf16[1536,1536]{1,0:T(8,128)(2,1)} %get-tuple-element.74.k_ref.v_ref.kv_ref, s32[8,128]{1,0:T(8,128)} %scatter.10.table_ref, ...), custom_call_target="tpu_custom_call" | custom-call | flops 24159191040 | bytes 25165824 | tf_op jit(solution)/shard_map/pallas_call | solution.py:140
  281.8 2.7 pad_maximum_fusion.wu_ref
  284.5 2.5 pad_maximum_fusion.1.wd_ref
  286.9 69.3 %shard_map.267 = (bf16[1536,768]{1,0:T(8,128)(2,1)}, f32[1536,768]{1,0:T(8,128)}, bf16[1536,768]{1,0:T(8,128)(2,1)}, bf16[768,768]{1,0:T(8,128)(2,1)}, bf16[768,...) custom-call(bf16[1536,768]{1,0:T(8,128)(2,1)} %pad_maximum_fusion.2.x_ref, ...), custom_call_target="tpu_custom_call" | custom-call | flops 48922361856 | bytes 16515072 | tf_op jit(solution)/shard_map/pallas_call | solution.py:519
  356.3 70.0 %shard_map.268 = (bf16[1024,768]{1,0:T(8,128)(2,1)}, bf16[1024,768]{1,0:T(8,128)(2,1)}, bf16[1024,768]{1,0:T(8,128)(2,1)}, f32[512,192]{1,0:T(8,128)}) custom-call(bf16[1536,768]{1,0:T(8,128)(2,1)} %get-tuple-element.73.q_ref, bf16[1536,1536]{1,0:T(8,128)(2,1)} %get-tuple-element.74.k_ref.v_ref.kv_ref, ...), custom_call_target="tpu_custom_call" | custom-call | flops 56371445760 | bytes 25165824 | tf_op jit(solution)/shard_map/pallas_call | solution.py:276
  426.2 16.8 %shard_map.269 = (bf16[512,768]{1,0:T(8,128)(2,1)}, bf16[512,1536]{1,0:T(8,128)(2,1)}, f32[512,192]{1,0:T(8,128)}) custom-call(bf16[1536,768]{1,0:T(8,128)(2,1)} %get-tuple-element.73.q_ref, bf16[1536,1536]{1,0:T(8,128)(2,1)} %get-tuple-element.74.k_ref.v_ref.kv_ref, bf16[1536,768]{1,0:T(8,128)(2,1)} %get-tuple-element.78.da_ref, ...), custom_call_target="tpu_custom_call" | custom-call | flops 1610612736 | bytes 5505024 | tf_op jit(solution)/shard_map/pallas_call | solution.py:400
  453.4 20.5 %shard_map.270 = (f32[1536,768]{1,0:T(8,128)}, bf16[768,768]{1,0:T(8,128)(2,1)}, bf16[768,1536]{1,0:T(8,128)(2,1)}, f32[1,768]{1,0:T(1,128)}) custom-call(bf16[1536,768]{1,0:T(8,128)(2,1)} %pad_maximum_fusion.2.x_ref, f32[1,768]{1,0:T(1,128)} %reshape.4141.gain_ref, bf16[1536,768]{1,0:T(8,128)(2,1)} %pad_maximum_fusion.5.dq_ref, ...), custom_call_target="tpu_custom_call" | custom-call | flops 10871635968 | bytes 21233664 | tf_op jit(solution)/shard_map/pallas_call | solution.py:587
  475.4 2.8 fusion.85
  478.2 2.8 fusion.86
  496.5 3.1 collective-permute-done.110
  527.2 3.4 collective-permute-done.54
  530.6 7.6 %collective-permute-done.55 = bf16[1,256,768]{2,1,0:T(8,128)(2,1)S(1)} collective-permute-done((bf16[1,256,768]{2,1,0:T(8,128)(2,1)}, bf16[1,256,768]{2,1,0:T(8,128)(2,1)S(1)}, u32[]{:S(2)}, u32[]{:S(2)}) %collective-permute-start.55) | collective-permute-done | bytes 393248 | tf_op jit(solution)/shard_map/ppermute | solution.py:745
  540.3 7.1 collective-permute-done.57
  547.4 7.6 %collective-permute-done.58 = bf16[1,256,768]{2,1,0:T(8,128)(2,1)S(1)} collective-permute-done((bf16[1,256,768]{2,1,0:T(8,128)(2,1)S(1)}, bf16[1,256,768]{2,1,0:T(8,128)(2,1)S(1)}, u32[]{:S(2)}, u32[]{:S(2)}) %collective-permute-start.58) | collective-permute-done | bytes 393248 | tf_op jit(solution)/shard_map/ppermute | solution.py:745
  562.4 3.8 collective-permute-done.60
  567.6 4.0 collective-permute-done.85
  573.1 4.5 collective-permute-done.65
  579.0 2.9 collective-permute-done.81
  583.2 3.3 collective-permute-done.86
  588.0 3.0 collective-permute-done.61
  592.2 3.0 collective-permute-done.66
  595.7 3.5 collective-permute-done.82
  599.7 3.5 collective-permute-done.87
  603.6 3.5 collective-permute-done.62
  607.6 3.5 collective-permute-done.67
  612.9 2.9 collective-permute-done.83
  617.6 2.9 collective-permute-done.88
  622.2 2.9 collective-permute-done.63
  626.9 2.9 collective-permute-done.68
  633.3 7.5 %collective-permute-done.70 = bf16[2,2,2,24,768]{4,3,0,1,2:T(8,128)(2,1)S(1)} collective-permute-done((bf16[2,2,2,24,768]{4,3,0,1,2:T(8,128)(2,1)S(1)}, bf16[2,2,2,24,768]{4,3,0,1,2:T(8,128)(2,1)S(1)}, u32[]{:S(2)}, u32[]{:S(2)}) %collective-permute-start.70) | collective-permute-done | bytes 294944 | tf_op jit(solution)/shard_map/ppermute | solution.py:633
  642.3 6.7 collective-permute-done.75
  650.4 3.7 collective-permute-done.71
  655.5 3.8 collective-permute-done.76
  659.7 3.9 collective-permute-done.72
  664.0 3.9 collective-permute-done.77
  670.0 3.0 collective-permute-done.73
  674.8 3.1 collective-permute-done.78
  684.7 10.6 %collective-permute-done.100 = bf16[2,2,2,96,384]{4,3,0,1,2:T(8,128)(2,1)S(1)} collective-permute-done((bf16[2,2,2,96,384]{4,3,0,1,2:T(8,128)(2,1)S(1)}, bf16[2,2,2,96,384]{4,3,0,1,2:T(8,128)(2,1)S(1)}, u32[]{:S(2)}, u32[]{:S(2)}) %collective-permute-start.100) | collective-permute-done | bytes 589856 | tf_op jit(solution)/shard_map/ppermute | solution.py:633
  698.1 7.0 collective-permute-done.90
  (592 shorter events, 234.1 us)
Async XLA Ops:
  2.1 31.7 %collective-permute-start.8 = (bf16[24,768]{1,0:T(8,128)(2,1)}, bf16[24,768]{1,0:T(8,128)(2,1)S(1)}, u32[]{:S(2)}, u32[]{:S(2)}) collective-permute-start(bf16[24,768]{1,0:T(8,128)(2,1)} %get-tuple-element.247), channel_id=1, source_target_pairs={{0,16},{4,20},{8,24},{12,28},{16,0},{20,4},{24,8},{28,12},{1,17},{... | collective-permute-start | bytes 110600 | tf_op jit(solution)/shard_map/ppermute | solution.py:633
  6.2 33.9 %collective-permute-start.13 = (bf16[24,768]{1,0:T(8,128)(2,1)}, bf16[24,768]{1,0:T(8,128)(2,1)}, u32[]{:S(2)}, u32[]{:S(2)}) collective-permute-start(bf16[24,768]{1,0:T(8,128)(2,1)} %get-tuple-element.246), channel_id=1, source_target_pairs={{0,16},{4,20},{8,24},{12,28},{16,0},{20,4},{24,8},{28,12},{1,17},{... | collective-permute-start | bytes 110600 | tf_op jit(solution)/shard_map/ppermute | solution.py:633
  8.7 97.3 %collective-permute-start = (bf16[1,256,768]{2,1,0:T(8,128)(2,1)}, bf16[1,256,768]{2,1,0:T(8,128)(2,1)}, u32[]{:S(2)}, u32[]{:S(2)}) collective-permute-start(bf16[1,256,768]{2,1,0:T(8,128)(2,1)} %get-tuple-element.181), channel_id=1, source_target_pairs={{0,1},{1,0},{2,3},{3,2},{4,5},{5,4},{6,7},{7,6},{8,9},{9,8},{10,11... | collective-permute-start | bytes 1179656 | tf_op jit(solution)/shard_map/ppermute | solution.py:718
  8.7 97.4 %collective-permute-start.1 = (bf16[1,256,768]{2,1,0:T(8,128)(2,1)}, bf16[1,256,768]{2,1,0:T(8,128)(2,1)}, u32[]{:S(2)}, u32[]{:S(2)}) collective-permute-start(bf16[1,256,768]{2,1,0:T(8,128)(2,1)} %get-tuple-element.183), channel_id=1, source_target_pairs={{0,2},{1,3},{2,0},{3,1},{4,6},{5,7},{6,4},{7,5},{8,10},{9,11},{10,... | collective-permute-start | bytes 1179656 | tf_op jit(solution)/shard_map/ppermute | solution.py:718
  11.1 15.9 %collective-permute-start.23 = (bf16[24,384]{1,0:T(8,128)(2,1)}, bf16[24,384]{1,0:T(8,128)(2,1)S(1)}, u32[]{:S(2)}, u32[]{:S(2)}) collective-permute-start(bf16[24,384]{1,0:T(8,128)(2,1)} %get-tuple-element.255), channel_id=1, source_target_pairs={{0,16},{4,20},{8,24},{12,28},{16,0},{20,4},{24,8},{28,12},{1,17},{... | collective-permute-start | bytes 55304 | tf_op jit(solution)/shard_map/ppermute | solution.py:633
  32.1 75.7 %collective-permute-start.2 = (bf16[1,256,768]{2,1,0:T(8,128)(2,1)}, bf16[1,256,768]{2,1,0:T(8,128)(2,1)S(1)}, u32[]{:S(2)}, u32[]{:S(2)}) collective-permute-start(bf16[1,256,768]{2,1,0:T(8,128)(2,1)} %get-tuple-element.182), channel_id=1, source_target_pairs={{0,3},{1,2},{2,1},{3,0},{4,7},{5,6},{6,5},{7,4},{8,11},{9,10},{10,... | collective-permute-start | bytes 1179656 | tf_op jit(solution)/shard_map/ppermute | solution.py:718
  38.8 17.2 %collective-permute-start.38 = (bf16[24,1536]{1,0:T(8,128)(2,1)}, bf16[24,1536]{1,0:T(8,128)(2,1)S(1)}, u32[]{:S(2)}, u32[]{:S(2)}) collective-permute-start(bf16[24,1536]{1,0:T(8,128)(2,1)} %get-tuple-element.226), channel_id=1, source_target_pairs={{0,16},{4,20},{8,24},{12,28},{16,0},{20,4},{24,8},{28,12},{1,17},{... | collective-permute-start | bytes 221192 | tf_op jit(solution)/shard_map/ppermute | solution.py:633
  53.9 9.7 %collective-permute-start.48 = (bf16[96,384]{1,0:T(8,128)(2,1)S(1)}, bf16[96,384]{1,0:T(8,128)(2,1)S(1)}, u32[]{:S(2)}, u32[]{:S(2)}) collective-permute-start(bf16[96,384]{1,0:T(8,128)(2,1)S(1)} %copy-done.48), channel_id=1, source_target_pairs={{0,16},{4,20},{8,24},{12,28},{16,0},{20,4},{24,8},{28,12},{1,17},{... | collective-permute-start | bytes 221192 | tf_op jit(solution)/shard_map/ppermute | solution.py:633
  68.1 8.6 %collective-permute-start.30 = (bf16[2,2,24,384]{3,2,0,1:T(8,128)(2,1)S(1)}, bf16[2,2,24,384]{3,2,0,1:T(8,128)(2,1)S(1)}, u32[]{:S(2)}, u32[]{:S(2)}) collective-permute-start(bf16[2,2,24,384]{3,2,0,1:T(8,128)(2,1)S(1)} %maximum_select_fusion.71), channel_id=1, source_target_pairs={{0,4},{4,0},{8,12},{12,8},{16,20},{20,16},{24,28},{28,24},{1,5},{5... | collective-permute-start | bytes 221192 | tf_op jit(solution)/shard_map/ppermute | solution.py:633
  85.7 14.6 %collective-permute-start.10 = (bf16[2,2,24,768]{3,2,0,1:T(8,128)(2,1)S(1)}, bf16[2,2,24,768]{3,2,0,1:T(8,128)(2,1)S(1)}, u32[]{:S(2)}, u32[]{:S(2)}) collective-permute-start(bf16[2,2,24,768]{3,2,0,1:T(8,128)(2,1)S(1)} %maximum_select_fusion.51), channel_id=1, source_target_pairs={{0,4},{4,0},{8,12},{12,8},{16,20},{20,16},{24,28},{28,24},{1,5},{5... | collective-permute-start | bytes 442376 | tf_op jit(solution)/shard_map/ppermute | solution.py:633
  103.7 7.0 collective-permute-start.20
  105.5 12.1 %collective-permute-start.21 = (bf16[1,256,768]{2,1,0:T(8,128)(2,1)S(1)}, bf16[1,256,768]{2,1,0:T(8,128)(2,1)S(1)}, u32[]{:S(2)}, u32[]{:S(2)}) collective-permute-start(bf16[1,256,768]{2,1,0:T(8,128)(2,1)S(1)} %copy-done.33), channel_id=1, source_target_pairs={{0,2},{1,3},{2,0},{3,1},{4,6},{5,7},{6,4},{7,5},{8,10},{9,11},{10,... | collective-permute-start | bytes 1179656 | tf_op jit(solution)/shard_map/ppermute | solution.py:718
  105.9 17.9 %collective-permute-start.22 = (bf16[1,256,768]{2,1,0:T(8,128)(2,1)S(1)}, bf16[1,256,768]{2,1,0:T(8,128)(2,1)S(1)}, u32[]{:S(2)}, u32[]{:S(2)}) collective-permute-start(bf16[1,256,768]{2,1,0:T(8,128)(2,1)S(1)} %copy-done.32), channel_id=1, source_target_pairs={{0,3},{1,2},{2,1},{3,0},{4,7},{5,6},{6,5},{7,4},{8,11},{9,10},{10,... | collective-permute-start | bytes 1179656 | tf_op jit(solution)/shard_map/ppermute | solution.py:718
  106.1 46.3 %collective-permute-start.18 = (s16[256,1024]{1,0:T(8,128)(2,1)S(1)}, s16[256,1024]{1,0:T(8,128)(2,1)S(1)}, u32[]{:S(2)}, u32[]{:S(2)}) collective-permute-start(s16[256,1024]{1,0:T(8,128)(2,1)S(1)} %copy-done.30), channel_id=1, source_target_pairs={{0,2},{1,3},{2,0},{3,1},{4,6},{5,7},{6,4},{7,5},{8,10},{9,11},{10,... | collective-permute-start | bytes 1572872 | tf_op jit(solution)/shard_map/ppermute | solution.py:633
  107.8 36.2 %collective-permute-start.40 = (bf16[2,2,24,1536]{3,2,0,1:T(8,128)(2,1)S(1)}, bf16[2,2,24,1536]{3,2,0,1:T(8,128)(2,1)S(1)}, u32[]{:S(2)}, u32[]{:S(2)}) collective-permute-start(bf16[2,2,24,1536]{3,2,0,1:T(8,128)(2,1)S(1)} %maximum_select_fusion.43), channel_id=1, source_target_pairs={{0,4},{4,0},{8,12},{12,8},{16,20},{20,16},{24,28},{28,24},{1,5},{5... | collective-permute-start | bytes 884744 | tf_op jit(solution)/shard_map/ppermute | solution.py:633
  110.7 32.8 %collective-permute-start.35 = (bf16[2,2,24,1536]{3,2,0,1:T(8,128)(2,1)S(1)}, bf16[2,2,24,1536]{3,2,0,1:T(8,128)(2,1)S(1)}, u32[]{:S(2)}, u32[]{:S(2)}) collective-permute-start(bf16[2,2,24,1536]{3,2,0,1:T(8,128)(2,1)S(1)} %maximum_select_fusion.41), channel_id=1, source_target_pairs={{0,2},{1,3},{2,0},{3,1},{4,6},{5,7},{6,4},{7,5},{8,10},{9,11},{10,... | collective-permute-start | bytes 884744 | tf_op jit(solution)/shard_map/ppermute | solution.py:633
  117.6 34.2 %collective-permute-start.50 = (bf16[2,2,96,384]{3,2,0,1:T(8,128)(2,1)S(1)}, bf16[2,2,96,384]{3,2,0,1:T(8,128)(2,1)S(1)}, u32[]{:S(2)}, u32[]{:S(2)}) collective-permute-start(bf16[2,2,96,384]{3,2,0,1:T(8,128)(2,1)S(1)} %maximum_select_fusion.47), channel_id=1, source_target_pairs={{0,4},{4,0},{8,12},{12,8},{16,20},{20,16},{24,28},{28,24},{1,5},{5... | collective-permute-start | bytes 884744 | tf_op jit(solution)/shard_map/ppermute | solution.py:633
  123.8 26.1 %collective-permute-start.45 = (bf16[2,2,96,384]{3,2,0,1:T(8,128)(2,1)S(1)}, bf16[2,2,96,384]{3,2,0,1:T(8,128)(2,1)S(1)}, u32[]{:S(2)}, u32[]{:S(2)}) collective-permute-start(bf16[2,2,96,384]{3,2,0,1:T(8,128)(2,1)S(1)} %maximum_select_fusion.45), channel_id=1, source_target_pairs={{0,2},{1,3},{2,0},{3,1},{4,6},{5,7},{6,4},{7,5},{8,10},{9,11},{10,... | collective-permute-start | bytes 884744 | tf_op jit(solution)/shard_map/ppermute | solution.py:633
  143.6 10.9 %collective-permute-start.11 = (bf16[2,2,2,24,768]{4,3,0,1,2:T(8,128)(2,1)S(1)}, bf16[2,2,2,24,768]{4,3,0,1,2:T(8,128)(2,1)S(1)}, u32[]{:S(2)}, u32[]{:S(2)}) collective-permute-start(bf16[2,2,2,24,768]{4,3,0,1,2:T(8,128)(2,1)S(1)} %maximum_select_fusion.33), channel_id=1, source_target_pairs={{0,2},{1,3},{2,0},{3,1},{4,6},{5,7},{6,4},{7,5},{8,10},{9,11},{10,... | collective-permute-start | bytes 884744 | tf_op jit(solution)/shard_map/ppermute | solution.py:633
  144.1 11.8 %collective-permute-start.16 = (bf16[2,2,2,24,768]{4,3,0,1,2:T(8,128)(2,1)S(1)}, bf16[2,2,2,24,768]{4,3,0,1,2:T(8,128)(2,1)S(1)}, u32[]{:S(2)}, u32[]{:S(2)}) collective-permute-start(bf16[2,2,2,24,768]{4,3,0,1,2:T(8,128)(2,1)S(1)} %maximum_select_fusion.35), channel_id=1, source_target_pairs={{0,4},{4,0},{8,12},{12,8},{16,20},{20,16},{24,28},{28,24},{1,5},{5... | collective-permute-start | bytes 884744 | tf_op jit(solution)/shard_map/ppermute | solution.py:633
  149.9 7.8 %collective-permute-start.6 = (bf16[2,2,2,24,768]{4,3,0,1,2:T(8,128)(2,1)S(1)}, bf16[2,2,2,24,768]{4,3,0,1,2:T(8,128)(2,1)S(1)}, u32[]{:S(2)}, u32[]{:S(2)}) collective-permute-start(bf16[2,2,2,24,768]{4,3,0,1,2:T(8,128)(2,1)S(1)} %maximum_select_fusion.31), channel_id=1, source_target_pairs={{0,4},{4,0},{8,12},{12,8},{16,20},{20,16},{24,28},{28,24},{1,5},{5... | collective-permute-start | bytes 884744 | tf_op jit(solution)/shard_map/ppermute | solution.py:633
  151.8 7.3 collective-permute-start.32
  152.4 9.4 %collective-permute-start.27 = (bf16[2,2,2,2,24,384]{5,4,0,1,3,2:T(8,128)(2,1)S(1)}, bf16[2,2,2,2,24,384]{5,4,0,1,3,2:T(8,128)(2,1)S(1)}, u32[]{:S(2)}, u32[]{:S(2)}) collective-permute-start(bf16[2,2,2,2,24,384]{5,4,0,1,3,2:T(8,128)(2,1)S(1)} %maximum_select_fusion.37), channel_id=1, source_target_pairs={{0,1},{1,0},{2,3},{3,2},{4,5},{5,4},{6,7},{7,6},{8,9},{9,8},{10,11... | collective-permute-start | bytes 884744 | tf_op jit(solution)/shard_map/ppermute | solution.py:633
  154.4 16.3 %collective-permute-start.41 = (bf16[2,2,2,24,1536]{4,3,0,1,2:T(8,128)(2,1)S(1)}, bf16[2,2,2,24,1536]{4,3,0,1,2:T(8,128)(2,1)S(1)}, u32[]{:S(2)}, u32[]{:S(2)}) collective-permute-start(bf16[2,2,2,24,1536]{4,3,0,1,2:T(8,128)(2,1)S(1)} %maximum_select_fusion.25), channel_id=1, source_target_pairs={{0,2},{1,3},{2,0},{3,1},{4,6},{5,7},{6,4},{7,5},{8,10},{9,11},{10,... | collective-permute-start | bytes 1769480 | tf_op jit(solution)/shard_map/ppermute | solution.py:633
  155.9 27.8 %collective-permute-start.36 = (bf16[2,2,2,24,1536]{4,3,0,1,2:T(8,128)(2,1)S(1)}, bf16[2,2,2,24,1536]{4,3,0,1,2:T(8,128)(2,1)S(1)}, u32[]{:S(2)}, u32[]{:S(2)}) collective-permute-start(bf16[2,2,2,24,1536]{4,3,0,1,2:T(8,128)(2,1)S(1)} %maximum_select_fusion.23), channel_id=1, source_target_pairs={{0,4},{4,0},{8,12},{12,8},{16,20},{20,16},{24,28},{28,24},{1,5},{5... | collective-permute-start | bytes 1769480 | tf_op jit(solution)/shard_map/ppermute | solution.py:633
  157.7 24.7 %collective-permute-start.51 = (bf16[2,2,2,96,384]{4,3,0,1,2:T(8,128)(2,1)S(1)}, bf16[2,2,2,96,384]{4,3,0,1,2:T(8,128)(2,1)S(1)}, u32[]{:S(2)}, u32[]{:S(2)}) collective-permute-start(bf16[2,2,2,96,384]{4,3,0,1,2:T(8,128)(2,1)S(1)} %maximum_select_fusion.29), channel_id=1, source_target_pairs={{0,2},{1,3},{2,0},{3,1},{4,6},{5,7},{6,4},{7,5},{8,10},{9,11},{10,... | collective-permute-start | bytes 1769480 | tf_op jit(solution)/shard_map/ppermute | solution.py:633
  159.1 27.5 %collective-permute-start.46 = (bf16[2,2,2,96,384]{4,3,0,1,2:T(8,128)(2,1)S(1)}, bf16[2,2,2,96,384]{4,3,0,1,2:T(8,128)(2,1)S(1)}, u32[]{:S(2)}, u32[]{:S(2)}) collective-permute-start(bf16[2,2,2,96,384]{4,3,0,1,2:T(8,128)(2,1)S(1)} %maximum_select_fusion.27), channel_id=1, source_target_pairs={{0,4},{4,0},{8,12},{12,8},{16,20},{20,16},{24,28},{28,24},{1,5},{5... | collective-permute-start | bytes 1769480 | tf_op jit(solution)/shard_map/ppermute | solution.py:633
  161.8 55.5 %collective-permute-start.19 = (s16[2,256,1024]{2,1,0:T(8,128)(2,1)}, s16[2,256,1024]{2,1,0:T(8,128)(2,1)}, u32[]{:S(2)}, u32[]{:S(2)}) collective-permute-start(s16[2,256,1024]{2,1,0:T(8,128)(2,1)} %add_select_fusion.1), channel_id=1, source_target_pairs={{0,1},{1,0},{2,3},{3,2},{4,5},{5,4},{6,7},{7,6},{8,9},{9,8},{10,11... | collective-permute-start | bytes 3145736 | tf_op jit(solution)/shard_map/ppermute | solution.py:633
  170.7 19.6 %collective-permute-start.12 = (bf16[2,2,2,2,24,768]{5,4,0,1,2,3:T(8,128)(2,1)S(1)}, bf16[2,2,2,2,24,768]{5,4,0,1,2,3:T(8,128)(2,1)S(1)}, u32[]{:S(2)}, u32[]{:S(2)}) collective-permute-start(bf16[2,2,2,2,24,768]{5,4,0,1,2,3:T(8,128)(2,1)S(1)} %maximum_select_fusion.17), channel_id=1, source_target_pairs={{0,1},{1,0},{2,3},{3,2},{4,5},{5,4},{6,7},{7,6},{8,9},{9,8},{10,11... | collective-permute-start | bytes 1769480 | tf_op jit(solution)/shard_map/ppermute | solution.py:633
  182.4 8.6 %collective-permute-start.17 = (bf16[2,2,2,2,24,768]{5,4,0,1,3,2:T(8,128)(2,1)S(1)}, bf16[2,2,2,2,24,768]{5,4,0,1,3,2:T(8,128)(2,1)S(1)}, u32[]{:S(2)}, u32[]{:S(2)}) collective-permute-start(bf16[2,2,2,2,24,768]{5,4,0,1,3,2:T(8,128)(2,1)S(1)} %maximum_select_fusion.19), channel_id=1, source_target_pairs={{0,1},{1,0},{2,3},{3,2},{4,5},{5,4},{6,7},{7,6},{8,9},{9,8},{10,11... | collective-permute-start | bytes 1769480 | tf_op jit(solution)/shard_map/ppermute | solution.py:633
  183.7 7.8 %collective-permute-start.7 = (bf16[2,2,2,2,24,768]{5,4,0,1,3,2:T(8,128)(2,1)S(1)}, bf16[2,2,2,2,24,768]{5,4,0,1,3,2:T(8,128)(2,1)S(1)}, u32[]{:S(2)}, u32[]{:S(2)}) collective-permute-start(bf16[2,2,2,2,24,768]{5,4,0,1,3,2:T(8,128)(2,1)S(1)} %maximum_select_fusion.15), channel_id=1, source_target_pairs={{0,1},{1,0},{2,3},{3,2},{4,5},{5,4},{6,7},{7,6},{8,9},{9,8},{10,11... | collective-permute-start | bytes 1769480 | tf_op jit(solution)/shard_map/ppermute | solution.py:633
  186.6 83.3 %collective-permute-start.42 = (bf16[2,2,2,2,24,1536]{5,4,0,1,2,3:T(8,128)(2,1)}, bf16[2,2,2,2,24,1536]{5,4,0,1,2,3:T(8,128)(2,1)S(1)}, u32[]{:S(2)}, u32[]{:S(2)}) collective-permute-start(bf16[2,2,2,2,24,1536]{5,4,0,1,2,3:T(8,128)(2,1)} %maximum_select_fusion.9), channel_id=1, source_target_pairs={{0,1},{1,0},{2,3},{3,2},{4,5},{5,4},{6,7},{7,6},{8,9},{9,8},{10,11... | collective-permute-start | bytes 3538952 | tf_op jit(solution)/shard_map/ppermute | solution.py:633
  190.3 81.3 %collective-permute-start.37 = (bf16[2,2,2,2,24,1536]{5,4,0,1,3,2:T(8,128)(2,1)}, bf16[2,2,2,2,24,1536]{5,4,0,1,3,2:T(8,128)(2,1)}, u32[]{:S(2)}, u32[]{:S(2)}) collective-permute-start(bf16[2,2,2,2,24,1536]{5,4,0,1,3,2:T(8,128)(2,1)} %maximum_select_fusion.7), channel_id=1, source_target_pairs={{0,1},{1,0},{2,3},{3,2},{4,5},{5,4},{6,7},{7,6},{8,9},{9,8},{10,11... | collective-permute-start | bytes 3538952 | tf_op jit(solution)/shard_map/ppermute | solution.py:633
  191.0 83.9 %collective-permute-start.52 = (bf16[2,2,2,2,96,384]{5,4,0,1,2,3:T(8,128)(2,1)}, bf16[2,2,2,2,96,384]{5,4,0,1,2,3:T(8,128)(2,1)}, u32[]{:S(2)}, u32[]{:S(2)}) collective-permute-start(bf16[2,2,2,2,96,384]{5,4,0,1,2,3:T(8,128)(2,1)} %maximum_select_fusion.13), channel_id=1, source_target_pairs={{0,1},{1,0},{2,3},{3,2},{4,5},{5,4},{6,7},{7,6},{8,9},{9,8},{10,11... | collective-permute-start | bytes 3538952 | tf_op jit(solution)/shard_map/ppermute | solution.py:633
  191.5 86.9 %collective-permute-start.47 = (bf16[2,2,2,2,96,384]{5,4,0,1,3,2:T(8,128)(2,1)}, bf16[2,2,2,2,96,384]{5,4,0,1,3,2:T(8,128)(2,1)}, u32[]{:S(2)}, u32[]{:S(2)}) collective-permute-start(bf16[2,2,2,2,96,384]{5,4,0,1,3,2:T(8,128)(2,1)} %maximum_select_fusion.11), channel_id=1, source_target_pairs={{0,1},{1,0},{2,3},{3,2},{4,5},{5,4},{6,7},{7,6},{8,9},{9,8},{10,11... | collective-permute-start | bytes 3538952 | tf_op jit(solution)/shard_map/ppermute | solution.py:633
  475.3 20.5 %collective-permute-start.109 = (f32[2048]{0:T(1024)S(1)}, f32[2048]{0:T(1024)S(1)}, u32[]{:S(2)}, u32[]{:S(2)}) collective-permute-start(f32[2048]{0:T(1024)S(1)} %pad_maximum_fusion.19), channel_id=1, source_target_pairs={{0,1},{1,0},{2,3},{3,2},{4,5},{5,4},{6,7},{7,6},{8,9},{9,8},{10,11... | collective-permute-start | bytes 24584 | tf_op jit(solution)/shard_map/ppermute | solution.py:633
  495.3 23.1 %collective-permute-start.79 = (bf16[2,2,2,2,24,384]{5,4,0,1,3,2:T(8,128)(2,1)}, bf16[2,2,2,2,24,384]{5,4,0,1,3,2:T(8,128)(2,1)}, u32[]{:S(2)}, u32[]{:S(2)}) collective-permute-start(bf16[2,2,2,2,24,384]{5,4,0,1,3,2:T(8,128)(2,1)} %bitcast.626), channel_id=1, source_target_pairs={{0,1},{1,0},{2,3},{3,2},{4,5},{5,4},{6,7},{7,6},{8,9},{9,8},{10,11... | collective-permute-start | bytes 884744 | tf_op jit(solution)/shard_map/ppermute | solution.py:633
  502.8 18.1 %collective-permute-start.84 = (bf16[2,2,2,2,24,384]{5,4,0,1,2,3:T(8,128)(2,1)}, bf16[2,2,2,2,24,384]{5,4,0,1,2,3:T(8,128)(2,1)}, u32[]{:S(2)}, u32[]{:S(2)}) collective-permute-start(bf16[2,2,2,2,24,384]{5,4,0,1,2,3:T(8,128)(2,1)} %bitcast.625), channel_id=1, source_target_pairs={{0,1},{1,0},{2,3},{3,2},{4,5},{5,4},{6,7},{7,6},{8,9},{9,8},{10,11... | collective-permute-start | bytes 884744 | tf_op jit(solution)/shard_map/ppermute | solution.py:633
  508.6 14.1 %collective-permute-start.59 = (bf16[2,2,2,2,24,384]{5,4,0,1,3,2:T(8,128)(2,1)}, bf16[2,2,2,2,24,384]{5,4,0,1,3,2:T(8,128)(2,1)}, u32[]{:S(2)}, u32[]{:S(2)}) collective-permute-start(bf16[2,2,2,2,24,384]{5,4,0,1,3,2:T(8,128)(2,1)} %bitcast.628), channel_id=1, source_target_pairs={{0,1},{1,0},{2,3},{3,2},{4,5},{5,4},{6,7},{7,6},{8,9},{9,8},{10,11... | collective-permute-start | bytes 884744 | tf_op jit(solution)/shard_map/ppermute | solution.py:633
  509.3 15.0 %collective-permute-start.64 = (bf16[2,2,2,2,24,384]{5,4,0,1,2,3:T(8,128)(2,1)}, bf16[2,2,2,2,24,384]{5,4,0,1,2,3:T(8,128)(2,1)}, u32[]{:S(2)}, u32[]{:S(2)}) collective-permute-start(bf16[2,2,2,2,24,384]{5,4,0,1,2,3:T(8,128)(2,1)} %bitcast.627), channel_id=1, source_target_pairs={{0,1},{1,0},{2,3},{3,2},{4,5},{5,4},{6,7},{7,6},{8,9},{9,8},{10,11... | collective-permute-start | bytes 884744 | tf_op jit(solution)/shard_map/ppermute | solution.py:633
  514.4 12.4 %collective-permute-start.53 = (bf16[1,256,768]{2,1,0:T(8,128)(2,1)}, bf16[1,256,768]{2,1,0:T(8,128)(2,1)}, u32[]{:S(2)}, u32[]{:S(2)}) collective-permute-start(bf16[1,256,768]{2,1,0:T(8,128)(2,1)} %get-tuple-element.167), channel_id=1, source_target_pairs={{1,0},{0,1},{3,2},{2,3},{5,4},{4,5},{7,6},{6,7},{9,8},{8,9},{11,10... | collective-permute-start | bytes 1179656 | tf_op jit(solution)/shard_map/ppermute | solution.py:745
  518.4 12.2 %collective-permute-start.54 = (bf16[1,256,768]{2,1,0:T(8,128)(2,1)}, bf16[1,256,768]{2,1,0:T(8,128)(2,1)S(1)}, u32[]{:S(2)}, u32[]{:S(2)}) collective-permute-start(bf16[1,256,768]{2,1,0:T(8,128)(2,1)} %get-tuple-element.166), channel_id=1, source_target_pairs={{2,0},{3,1},{0,2},{1,3},{6,4},{7,5},{4,6},{5,7},{10,8},{11,9},{8,1... | collective-permute-start | bytes 1179656 | tf_op jit(solution)/shard_map/ppermute | solution.py:745
  521.0 17.3 %collective-permute-start.55 = (bf16[1,256,768]{2,1,0:T(8,128)(2,1)}, bf16[1,256,768]{2,1,0:T(8,128)(2,1)S(1)}, u32[]{:S(2)}, u32[]{:S(2)}) collective-permute-start(bf16[1,256,768]{2,1,0:T(8,128)(2,1)} %get-tuple-element.165), channel_id=1, source_target_pairs={{3,0},{2,1},{1,2},{0,3},{7,4},{6,5},{5,6},{4,7},{11,8},{10,9},{9,1... | collective-permute-start | bytes 1179656 | tf_op jit(solution)/shard_map/ppermute | solution.py:745
  522.7 17.5 %collective-permute-start.56 = (bf16[1,256,768]{2,1,0:T(8,128)(2,1)S(1)}, bf16[1,256,768]{2,1,0:T(8,128)(2,1)S(1)}, u32[]{:S(2)}, u32[]{:S(2)}) collective-permute-start(bf16[1,256,768]{2,1,0:T(8,128)(2,1)S(1)} %copy-done.37), channel_id=1, source_target_pairs={{1,0},{0,1},{3,2},{2,3},{5,4},{4,5},{7,6},{6,7},{9,8},{8,9},{11,10... | collective-permute-start | bytes 1179656 | tf_op jit(solution)/shard_map/ppermute | solution.py:745
  524.3 23.1 %collective-permute-start.57 = (bf16[1,256,768]{2,1,0:T(8,128)(2,1)S(1)}, bf16[1,256,768]{2,1,0:T(8,128)(2,1)S(1)}, u32[]{:S(2)}, u32[]{:S(2)}) collective-permute-start(bf16[1,256,768]{2,1,0:T(8,128)(2,1)S(1)} %copy-done.36), channel_id=1, source_target_pairs={{2,0},{3,1},{0,2},{1,3},{6,4},{7,5},{4,6},{5,7},{10,8},{11,9},{8,1... | collective-permute-start | bytes 1179656 | tf_op jit(solution)/shard_map/ppermute | solution.py:745
  526.8 28.3 %collective-permute-start.58 = (bf16[1,256,768]{2,1,0:T(8,128)(2,1)S(1)}, bf16[1,256,768]{2,1,0:T(8,128)(2,1)S(1)}, u32[]{:S(2)}, u32[]{:S(2)}) collective-permute-start(bf16[1,256,768]{2,1,0:T(8,128)(2,1)S(1)} %copy-done.35), channel_id=1, source_target_pairs={{3,0},{2,1},{1,2},{0,3},{7,4},{6,5},{5,6},{4,7},{11,8},{10,9},{9,1... | collective-permute-start | bytes 1179656 | tf_op jit(solution)/shard_map/ppermute | solution.py:745
  530.6 148.0 %collective-permute-start.99 = (bf16[2,2,2,2,96,384]{5,4,0,1,3,2:T(8,128)(2,1)S(1)}, bf16[2,2,2,2,96,384]{5,4,0,1,3,2:T(8,128)(2,1)S(1)}, u32[]{:S(2)}, u32[]{:S(2)}) collective-permute-start(bf16[2,2,2,2,96,384]{5,4,0,1,3,2:T(8,128)(2,1)S(1)} %bitcast.679), channel_id=1, source_target_pairs={{0,1},{1,0},{2,3},{3,2},{4,5},{5,4},{6,7},{7,6},{8,9},{9,8},{10,11... | collective-permute-start | bytes 3538952 | tf_op jit(solution)/shard_map/ppermute | solution.py:633
  538.2 142.1 %collective-permute-start.104 = (bf16[2,2,2,2,96,384]{5,4,0,1,2,3:T(8,128)(2,1)S(1)}, bf16[2,2,2,2,96,384]{5,4,0,1,2,3:T(8,128)(2,1)S(1)}, u32[]{:S(2)}, u32[]{:S(2)}) collective-permute-start(bf16[2,2,2,2,96,384]{5,4,0,1,2,3:T(8,128)(2,1)S(1)} %bitcast.680), channel_id=1, source_target_pairs={{0,1},{1,0},{2,3},{3,2},{4,5},{5,4},{6,7},{7,6},{8,9},{9,8},{10,11... | collective-permute-start | bytes 3538952 | tf_op jit(solution)/shard_map/ppermute | solution.py:633
  540.2 141.3 %collective-permute-start.89 = (bf16[2,2,2,2,24,1536]{5,4,0,1,3,2:T(8,128)(2,1)S(1)}, bf16[2,2,2,2,24,1536]{5,4,0,1,3,2:T(8,128)(2,1)S(1)}, u32[]{:S(2)}, u32[]{:S(2)}) collective-permute-start(bf16[2,2,2,2,24,1536]{5,4,0,1,3,2:T(8,128)(2,1)S(1)} %bitcast.678), channel_id=1, source_target_pairs={{0,1},{1,0},{2,3},{3,2},{4,5},{5,4},{6,7},{7,6},{8,9},{9,8},{10,11... | collective-permute-start | bytes 3538952 | tf_op jit(solution)/shard_map/ppermute | solution.py:633
  547.4 83.6 %collective-permute-start.69 = (bf16[2,2,2,2,24,768]{5,4,0,1,3,2:T(8,128)(2,1)S(1)}, bf16[2,2,2,2,24,768]{5,4,0,1,3,2:T(8,128)(2,1)S(1)}, u32[]{:S(2)}, u32[]{:S(2)}) collective-permute-start(bf16[2,2,2,2,24,768]{5,4,0,1,3,2:T(8,128)(2,1)S(1)} %bitcast.709), channel_id=1, source_target_pairs={{0,1},{1,0},{2,3},{3,2},{4,5},{5,4},{6,7},{7,6},{8,9},{9,8},{10,11... | collective-permute-start | bytes 1769480 | tf_op jit(solution)/shard_map/ppermute | solution.py:633
  631.1 52.3 %collective-permute-start.94 = (bf16[2,2,2,2,24,1536]{5,4,0,1,2,3:T(8,128)(2,1)S(1)}, bf16[2,2,2,2,24,1536]{5,4,0,1,2,3:T(8,128)(2,1)S(1)}, u32[]{:S(2)}, u32[]{:S(2)}) collective-permute-start(bf16[2,2,2,2,24,1536]{5,4,0,1,2,3:T(8,128)(2,1)S(1)} %bitcast.677), channel_id=1, source_target_pairs={{0,1},{1,0},{2,3},{3,2},{4,5},{5,4},{6,7},{7,6},{8,9},{9,8},{10,11... | collective-permute-start | bytes 3538952 | tf_op jit(solution)/shard_map/ppermute | solution.py:633
  631.8 9.0 %collective-permute-start.70 = (bf16[2,2,2,24,768]{4,3,0,1,2:T(8,128)(2,1)S(1)}, bf16[2,2,2,24,768]{4,3,0,1,2:T(8,128)(2,1)S(1)}, u32[]{:S(2)}, u32[]{:S(2)}) collective-permute-start(bf16[2,2,2,24,768]{4,3,0,1,2:T(8,128)(2,1)S(1)} %dynamic-slice_bitcast_fusion.33), channel_id=1, source_target_pairs={{0,4},{4,0},{8,12},{12,8},{16,20},{20,16},{24,28},{28,24},{1,5},{5... | collective-permute-start | bytes 884744 | tf_op jit(solution)/shard_map/ppermute | solution.py:633
  640.8 8.1 %collective-permute-start.75 = (bf16[2,2,2,24,768]{4,3,0,1,2:T(8,128)(2,1)S(1)}, bf16[2,2,2,24,768]{4,3,0,1,2:T(8,128)(2,1)S(1)}, u32[]{:S(2)}, u32[]{:S(2)}) collective-permute-start(bf16[2,2,2,24,768]{4,3,0,1,2:T(8,128)(2,1)S(1)} %dynamic-slice_bitcast_fusion.32), channel_id=1, source_target_pairs={{0,2},{1,3},{2,0},{3,1},{4,6},{5,7},{6,4},{7,5},{8,10},{9,11},{10,... | collective-permute-start | bytes 884744 | tf_op jit(solution)/shard_map/ppermute | solution.py:633
  679.0 16.3 %collective-permute-start.100 = (bf16[2,2,2,96,384]{4,3,0,1,2:T(8,128)(2,1)S(1)}, bf16[2,2,2,96,384]{4,3,0,1,2:T(8,128)(2,1)S(1)}, u32[]{:S(2)}, u32[]{:S(2)}) collective-permute-start(bf16[2,2,2,96,384]{4,3,0,1,2:T(8,128)(2,1)S(1)} %dynamic-slice_bitcast_fusion.1), channel_id=1, source_target_pairs={{0,4},{4,0},{8,12},{12,8},{16,20},{20,16},{24,28},{28,24},{1,5},{5... | collective-permute-start | bytes 1769480 | tf_op jit(solution)/shard_map/ppermute | solution.py:633
  680.7 16.3 %collective-permute-start.105 = (bf16[2,2,2,96,384]{4,3,0,1,2:T(8,128)(2,1)S(1)}, bf16[2,2,2,96,384]{4,3,0,1,2:T(8,128)(2,1)S(1)}, u32[]{:S(2)}, u32[]{:S(2)}) collective-permute-start(bf16[2,2,2,96,384]{4,3,0,1,2:T(8,128)(2,1)S(1)} %dynamic-slice_bitcast_fusion), channel_id=1, source_target_pairs={{0,2},{1,3},{2,0},{3,1},{4,6},{5,7},{6,4},{7,5},{8,10},{9,11},{10,... | collective-permute-start | bytes 1769480 | tf_op jit(solution)/shard_map/ppermute | solution.py:633
  682.1 23.0 %collective-permute-start.90 = (bf16[2,2,2,24,1536]{4,3,0,1,2:T(8,128)(2,1)S(1)}, bf16[2,2,2,24,1536]{4,3,0,1,2:T(8,128)(2,1)S(1)}, u32[]{:S(2)}, u32[]{:S(2)}) collective-permute-start(bf16[2,2,2,24,1536]{4,3,0,1,2:T(8,128)(2,1)S(1)} %dynamic-slice_bitcast_fusion.3), channel_id=1, source_target_pairs={{0,4},{4,0},{8,12},{12,8},{16,20},{20,16},{24,28},{28,24},{1,5},{5... | collective-permute-start | bytes 1769480 | tf_op jit(solution)/shard_map/ppermute | solution.py:633
  683.7 22.9 %collective-permute-start.95 = (bf16[2,2,2,24,1536]{4,3,0,1,2:T(8,128)(2,1)S(1)}, bf16[2,2,2,24,1536]{4,3,0,1,2:T(8,128)(2,1)S(1)}, u32[]{:S(2)}, u32[]{:S(2)}) collective-permute-start(bf16[2,2,2,24,1536]{4,3,0,1,2:T(8,128)(2,1)S(1)} %dynamic-slice_bitcast_fusion.2), channel_id=1, source_target_pairs={{0,2},{1,3},{2,0},{3,1},{4,6},{5,7},{6,4},{7,5},{8,10},{9,11},{10,... | collective-permute-start | bytes 1769480 | tf_op jit(solution)/shard_map/ppermute | solution.py:633
  695.5 14.2 %collective-permute-start.101 = (bf16[2,2,96,384]{3,2,0,1:T(8,128)(2,1)S(1)}, bf16[2,2,96,384]{3,2,0,1:T(8,128)(2,1)S(1)}, u32[]{:S(2)}, u32[]{:S(2)}) collective-permute-start(bf16[2,2,96,384]{3,2,0,1:T(8,128)(2,1)S(1)} %dynamic-slice_bitcast_fusion.29), channel_id=1, source_target_pairs={{0,2},{1,3},{2,0},{3,1},{4,6},{5,7},{6,4},{7,5},{8,10},{9,11},{10,... | collective-permute-start | bytes 884744 | tf_op jit(solution)/shard_map/ppermute | solution.py:633
  697.3 12.8 %collective-permute-start.106 = (bf16[2,2,96,384]{3,2,0,1:T(8,128)(2,1)S(1)}, bf16[2,2,96,384]{3,2,0,1:T(8,128)(2,1)S(1)}, u32[]{:S(2)}, u32[]{:S(2)}) collective-permute-start(bf16[2,2,96,384]{3,2,0,1:T(8,128)(2,1)S(1)} %dynamic-slice_bitcast_fusion.28), channel_id=1, source_target_pairs={{0,4},{4,0},{8,12},{12,8},{16,20},{20,16},{24,28},{28,24},{1,5},{5... | collective-permute-start | bytes 884744 | tf_op jit(solution)/shard_map/ppermute | solution.py:633
  705.3 7.6 %collective-permute-start.91 = (bf16[2,2,24,1536]{3,2,0,1:T(8,128)(2,1)S(1)}, bf16[2,2,24,1536]{3,2,0,1:T(8,128)(2,1)S(1)}, u32[]{:S(2)}, u32[]{:S(2)}) collective-permute-start(bf16[2,2,24,1536]{3,2,0,1:T(8,128)(2,1)S(1)} %dynamic-slice_bitcast_fusion.31), channel_id=1, source_target_pairs={{0,2},{1,3},{2,0},{3,1},{4,6},{5,7},{6,4},{7,5},{8,10},{9,11},{10,... | collective-permute-start | bytes 884744 | tf_op jit(solution)/shard_map/ppermute | solution.py:633
  706.9 6.8 collective-permute-start.96
  710.3 7.8 %collective-permute-start.107 = (bf16[2,96,384]{2,1,0:T(8,128)(2,1)S(1)}, bf16[2,96,384]{2,1,0:T(8,128)(2,1)S(1)}, u32[]{:S(2)}, u32[]{:S(2)}) collective-permute-start(bf16[2,96,384]{2,1,0:T(8,128)(2,1)S(1)} %dynamic-slice_bitcast_fusion.34), channel_id=1, source_target_pairs={{0,8},{4,12},{8,0},{12,4},{16,24},{20,28},{24,16},{28,20},{1,9},{5... | collective-permute-start | bytes 442376 | tf_op jit(solution)/shard_map/ppermute | solution.py:633
  713.0 6.7 collective-permute-start.92
  713.7 7.5 %collective-permute-start.97 = (bf16[2,24,1536]{2,1,0:T(8,128)(2,1)S(1)}, bf16[2,24,1536]{2,1,0:T(8,128)(2,1)S(1)}, u32[]{:S(2)}, u32[]{:S(2)}) collective-permute-start(bf16[2,24,1536]{2,1,0:T(8,128)(2,1)S(1)} %dynamic-slice_bitcast_fusion.36), channel_id=1, source_target_pairs={{0,8},{4,12},{8,0},{12,4},{16,24},{20,28},{24,16},{28,20},{1,9},{5... | collective-permute-start | bytes 442376 | tf_op jit(solution)/shard_map/ppermute | solution.py:633
  (113 other events, 994.8 us)

commit v2 on v1

--- a/solution.py
+++ b/solution.py
@@ -55,14 +55,15 @@
     return lax.broadcasted_iota(jnp.int32, shape, 1) < head_dim
 
 
-def project_kernel(x_ref, gain_ref, wq_ref, wkv_ref, q_ref, kv_ref):
+def project_kernel(x_ref, gain_ref, w_ref, q_ref, kv_ref):
     values = x_ref[...].astype(SINGLE)
     normed = (values * scale_of(values) * gain_ref[...]).astype(BFLOAT)
-    q_ref[...] = nn(normed, wq_ref[...]).astype(BFLOAT)
-    kv_ref[...] = nn(normed, wkv_ref[...]).astype(BFLOAT)
-
-
-def project(tokens, gain, w_query, w_keyval):
+    width = values.shape[1]
+    q_ref[...] = nn(normed, w_ref[:, :width]).astype(BFLOAT)
+    kv_ref[...] = nn(normed, w_ref[:, width:]).astype(BFLOAT)
+
+
+def project(tokens, gain, w_qkv):
     rows, width = tokens.shape
     block = math.gcd(rows, 256)
     return pl.pallas_call(
@@ -71,8 +72,7 @@
         in_specs=[
             pl.BlockSpec((block, width), lambda i: (i, 0)),
             whole((1, width)),
-            whole(w_query.shape),
-            whole(w_keyval.shape),
+            whole(w_qkv.shape),
         ],
         out_specs=[
             pl.BlockSpec((block, width), lambda i: (i, 0)),
@@ -84,7 +84,7 @@
         ],
         compiler_params=params(),
         cost_estimate=cost(6 * rows * width * width, 12 * rows * width),
-    )(tokens, gain.reshape(1, width), w_query, w_keyval)
+    )(tokens, gain.reshape(1, width), w_qkv)
 
 
 def doc_forward_kernel(q_ref, k_ref, v_ref, table_ref, bucket_ref, mix_ref, prob_ref):
@@ -430,44 +430,40 @@
     mix_ref,
     dy_ref,
     gain_ref,
-    wo_ref,
-    wu_ref,
+    wou_ref,
     wd_ref,
     y_ref,
     dh_ref,
     da_ref,
-    go_ref,
-    gu_ref,
+    gou_ref,
     gd_ref,
     gg_ref,
-    go_acc,
-    gu_acc,
+    gou_acc,
     gd_acc,
     stage,
     sems,
 ):
     step = pl.program_id(0)
-    hidden = wu_ref.shape[1]
-    width = wu_ref.shape[0]
+    hidden, width = wd_ref.shape
 
     @pl.when(step == 0)
     def _():
-        go_acc[...] = jnp.zeros_like(go_acc)
-        gu_acc[...] = jnp.zeros_like(gu_acc)
+        gou_acc[...] = jnp.zeros_like(gou_acc)
         gd_acc[...] = jnp.zeros_like(gd_acc)
         gg_ref[...] = jnp.zeros_like(gg_ref)
 
     mixture = mix_ref[...]
     dy = dy_ref[...]
     gain = gain_ref[...]
-    residual = x_ref[...].astype(SINGLE) + nn(mixture, wo_ref[...])
+    residual = x_ref[...].astype(SINGLE) + nn(mixture, wou_ref[:, :width])
     scale = scale_of(residual)
     second = (residual * scale * gain).astype(BFLOAT)
     y = residual
     grad_second = jnp.zeros_like(residual)
     for part in range(hidden // chunk):
         span = slice(part * chunk, (part + 1) * chunk)
-        pre = nn(second, wu_ref[:, span])
+        past = slice(width + part * chunk, width + (part + 1) * chunk)
+        pre = nn(second, wou_ref[:, past])
         grad_hidden = nt(dy, wd_ref[span, :])
         square = pre * pre
         tanh = jnp.tanh(pre * (GELU_A + (GELU_A * GELU_B) * square))
@@ -477,22 +473,22 @@
         act_low = act.astype(BFLOAT)
         grad_pre = (grad_hidden * slope).astype(BFLOAT)
         y = y + nn(act_low, wd_ref[span, :])
-        grad_second = grad_second + nt(grad_pre, wu_ref[:, span])
+        grad_second = grad_second + nt(grad_pre, wou_ref[:, past])
         gd_acc[span, :] += tn(act_low, dy)
-        gu_acc[:, span] += tn(second, grad_pre)
+        gou_acc[:, past] += tn(second, grad_pre)
     y_ref[...] = y.astype(BFLOAT)
     gg_ref[...] += jnp.sum(grad_second * residual * scale, axis=0, keepdims=True)
     grad_res = dy.astype(SINGLE) + norm_back(residual, scale, grad_second * gain)
     dh_ref[...] = grad_res
     grad_low = grad_res.astype(BFLOAT)
-    da_ref[...] = nt(grad_low, wo_ref[...]).astype(BFLOAT)
-    go_acc[...] += tn(mixture, grad_low)
+    da_ref[...] = nt(grad_low, wou_ref[:, :width]).astype(BFLOAT)
+    gou_acc[:, :width] += tn(mixture, grad_low)
 
     @pl.when(step == pl.num_programs(0) - 1)
     def _():
         pieces = []
         rows, columns = stage.shape[1:]
-        for acc, out in ((gd_acc, gd_ref), (gu_acc, gu_ref), (go_acc, go_ref)):
+        for acc, out in ((gd_acc, gd_ref), (gou_acc, gou_ref)):
             for r in range(acc.shape[0] // rows):
                 for c in range(acc.shape[1] // columns):
                     spot = (pl.ds(r * rows, rows), pl.ds(c * columns, columns))
@@ -510,9 +506,9 @@
                 copy.wait()
 
 
-def feed(tokens, mixture, cotangent, gain, w_out, w_up, w_down):
+def feed(tokens, mixture, cotangent, gain, w_out_up, w_down):
     rows, width = tokens.shape
-    hidden = w_up.shape[1]
+    hidden = w_down.shape[0]
     block = math.gcd(rows, 256)
     along = pl.BlockSpec((block, width), lambda i: (i, 0))
     anywhere = pl.BlockSpec(memory_space=pl.ANY)
@@ -524,90 +520,79 @@
             along,
             along,
             whole((1, width)),
-            whole(w_out.shape),
-            whole(w_up.shape),
+            whole(w_out_up.shape),
             whole(w_down.shape),
         ],
-        out_specs=[along, along, along, anywhere, anywhere, anywhere, whole((1, width))],
+        out_specs=[along, along, along, anywhere, anywhere, whole((1, width))],
         out_shape=[
             jax.ShapeDtypeStruct((rows, width), BFLOAT),
             jax.ShapeDtypeStruct((rows, width), SINGLE),
             jax.ShapeDtypeStruct((rows, width), BFLOAT),
-            jax.ShapeDtypeStruct(w_out.shape, BFLOAT),
-            jax.ShapeDtypeStruct(w_up.shape, BFLOAT),
+            jax.ShapeDtypeStruct(w_out_up.shape, BFLOAT),
             jax.ShapeDtypeStruct(w_down.shape, BFLOAT),
             jax.ShapeDtypeStruct((1, width), SINGLE),
         ],
         scratch_shapes=[
-            pltpu.VMEM(w_out.shape, SINGLE),
-            pltpu.VMEM(w_up.shape, SINGLE),
+            pltpu.VMEM(w_out_up.shape, SINGLE),
             pltpu.VMEM(w_down.shape, SINGLE),
             pltpu.VMEM((2, width, width), BFLOAT),
             pltpu.SemaphoreType.DMA((2,)),
         ],
         compiler_params=params(),
         cost_estimate=cost(2 * rows * width * (6 * hidden + 3 * width), 14 * rows * width),
-    )(tokens, mixture, cotangent, gain.reshape(1, width), w_out, w_up, w_down)
+    )(tokens, mixture, cotangent, gain.reshape(1, width), w_out_up, w_down)
 
 
 def unproject_kernel(
-    x_ref, gain_ref, dq_ref, dk_ref, dv_ref, dh_ref, wq_ref, wkv_ref, dx_ref, gq_ref, gkv_ref, gg_ref, gq_acc, gkv_acc
+    x_ref, gain_ref, dq_ref, dk_ref, dv_ref, dh_ref, w_ref, dx_ref, low_ref, gw_ref, gg_ref, acc
 ):
     step = pl.program_id(0)
-    width = wq_ref.shape[0]
+    width = w_ref.shape[0]
 
     @pl.when(step == 0)
     def _():
-        gq_acc[...] = jnp.zeros_like(gq_acc)
-        gkv_acc[...] = jnp.zeros_like(gkv_acc)
+        acc[...] = jnp.zeros_like(acc)
         gg_ref[...] = jnp.zeros_like(gg_ref)
 
     values = x_ref[...].astype(SINGLE)
     gain = gain_ref[...]
     scale = scale_of(values)
     normed = (values * scale * gain).astype(BFLOAT)
-    dq, dk, dv = dq_ref[...], dk_ref[...], dv_ref[...]
-    gq_acc[...] += tn(normed, dq)
-    gkv_acc[:, :width] += tn(normed, dk)
-    gkv_acc[:, width:] += tn(normed, dv)
-    grad = nt(dq, wq_ref[...]) + nt(dk, wkv_ref[:, :width]) + nt(dv, wkv_ref[:, width:])
+    grad = jnp.zeros_like(values)
+    for number, ref in enumerate((dq_ref, dk_ref, dv_ref)):
+        span = slice(number * width, (number + 1) * width)
+        part = ref[...]
+        acc[:, span] += tn(normed, part)
+        grad = grad + nt(part, w_ref[:, span])
     gg_ref[...] += jnp.sum(grad * values * scale, axis=0, keepdims=True)
-    dx_ref[...] = dh_ref[...] + norm_back(values, scale, grad * gain)
+    dx = dh_ref[...] + norm_back(values, scale, grad * gain)
+    dx_ref[...] = dx
+    low_ref[...] = dx.astype(BFLOAT)
 
     @pl.when(step == pl.num_programs(0) - 1)
     def _():
-        gq_ref[...] = gq_acc[...].astype(BFLOAT)
-        gkv_ref[...] = gkv_acc[...].astype(BFLOAT)
-
-
-def unproject(tokens, gain, dq, dk, dv, grad_res, w_query, w_keyval):
+        gw_ref[...] = acc[...].astype(BFLOAT)
+
+
+def unproject(tokens, gain, dq, dk, dv, grad_res, w_qkv):
     rows, width = tokens.shape
     block = math.gcd(rows, 256)
     along = pl.BlockSpec((block, width), lambda i: (i, 0))
     return pl.pallas_call(
         unproject_kernel,
         grid=(rows // block,),
-        in_specs=[
-            along,
-            whole((1, width)),
-            along,
-            along,
-            along,
-            along,
-            whole(w_query.shape),
-            whole(w_keyval.shape),
-        ],
-        out_specs=[along, whole(w_query.shape), whole(w_keyval.shape), whole((1, width))],
+        in_specs=[along, whole((1, width)), along, along, along, along, whole(w_qkv.shape)],
+        out_specs=[along, along, whole(w_qkv.shape), whole((1, width))],
         out_shape=[
             jax.ShapeDtypeStruct((rows, width), SINGLE),
-            jax.ShapeDtypeStruct(w_query.shape, BFLOAT),
-            jax.ShapeDtypeStruct(w_keyval.shape, BFLOAT),
+            jax.ShapeDtypeStruct((rows, width), BFLOAT),
+            jax.ShapeDtypeStruct(w_qkv.shape, BFLOAT),
             jax.ShapeDtypeStruct((1, width), SINGLE),
         ],
-        scratch_shapes=[pltpu.VMEM(w_query.shape, SINGLE), pltpu.VMEM(w_keyval.shape, SINGLE)],
+        scratch_shapes=[pltpu.VMEM(w_qkv.shape, SINGLE)],
         compiler_params=params(),
         cost_estimate=cost(12 * rows * width * width, 18 * rows * width),
-    )(tokens, gain.reshape(1, width), dq, dk, dv, grad_res, w_query, w_keyval)
+    )(tokens, gain.reshape(1, width), dq, dk, dv, grad_res, w_qkv)
 
 
 def bits_of(count):
@@ -651,13 +636,6 @@
             high, jnp.stack([other, held], place), jnp.stack([held, other], place)
         )
     return held.reshape(-1, shard.shape[1])
-
-
-def gather_weights(shards, orders):
-    pieces = []
-    for shard, order in zip(shards, orders):
-        pieces.append(gather_rows(shard, order))
-    return pieces
 
 
 def scatter_rows(values, order):
@@ -764,6 +742,416 @@
         )
         done.append(item)
     return held.reshape(-1, shard.shape[1])
+
+
+class Spot:
+    def __init__(self):
+        self.dp = lax.axis_index("dp")
+        self.seq = lax.axis_index("seq")
+        self.core = self.seq % 2
+        self.y = self.seq // 2
+        self.x = self.dp % 2
+        self.z = self.dp // 2
+
+    def partner(self, z=0, x=0, y=0, core=0):
+        dp = self.flip(self.z, z) * 2 + self.flip(self.x, x)
+        seq = self.flip(self.y, y) * 2 + self.flip(self.core, core)
+        return (dp, seq)
+
+    @staticmethod
+    def flip(value, bits):
+        if bits == 0:
+            return value
+        if bits == 1:
+            return value + 1 - 2 * (value % 2)
+        if bits == 2:
+            return (value + 2) % 4
+        return 3 - value
+
+    def chip(self, z=0, x=0, y=0):
+        return (self.flip(self.z, z) * 2 + self.flip(self.x, x)) * 2 + self.flip(self.y, y)
+
+
+def send(source, target, sems, number, device):
+    return pltpu.make_async_remote_copy(
+        src_ref=source,
+        dst_ref=target,
+        send_sem=sems.at[0, number],
+        recv_sem=sems.at[1, number],
+        device_id=device,
+        device_id_type=pl.DeviceIdType.MESH,
+    )
+
+
+def greet(partners):
+    barrier = pltpu.get_barrier_semaphore()
+    for device in partners:
+        pl.semaphore_signal(barrier, inc=1, device_id=device, device_id_type=pl.DeviceIdType.MESH)
+    pl.semaphore_wait(barrier, len(partners))
+
+
+GATHER_COPIES = 1 + 3 + 4 + 8 + 1
+
+
+class Gather:
+    def __init__(self, spot, shard, whole_ref, mine, theirs, block, sems, local_sems):
+        self.spot, self.shard, self.whole = spot, shard, whole_ref
+        self.mine, self.theirs, self.block = mine, theirs, block
+        self.sems, self.local = sems, local_sems
+        self.rows = block.shape[0]
+        self.half = block.shape[1]
+        self.sent = []
+        self.here = None
+
+    def columns(self, core):
+        return pl.ds(pl.multiple_of(core * self.half, 128), self.half)
+
+    def area(self, chip, core):
+        return self.whole.at[pl.ds(pl.multiple_of(chip * self.rows, 16), self.rows), self.columns(core)]
+
+    def go(self, source, target, number, device):
+        copy = send(source, target, self.sems, number, device)
+        copy.start()
+        self.sent.append(copy)
+        return copy
+
+    def join_start(self):
+        core = self.spot.core
+        self.first = self.go(
+            self.shard.at[:, self.columns(1 - core)], self.theirs, 0, self.spot.partner(core=1)
+        )
+        self.load = pltpu.make_async_copy(
+            self.shard.at[:, self.columns(core)], self.mine, self.local.at[0]
+        )
+        self.load.start()
+
+    def join_end(self):
+        self.load.wait()
+        self.first.wait_recv()
+        part = self.rows // 2
+        low = self.spot.core == 0
+        mine = self.mine[...].astype(SINGLE)[:part]
+        theirs = self.theirs[...].astype(SINGLE)[:part]
+        self.block[:part, :] = jnp.where(low, mine, theirs).astype(BFLOAT)
+        self.block[part:, :] = jnp.where(low, theirs, mine).astype(BFLOAT)
+
+    def z_start(self):
+        own = self.area(self.spot.chip(), self.spot.core)
+        self.here = pltpu.make_async_copy(self.block, own, self.local.at[1])
+        self.here.start()
+        self.z_copies = [self.go(self.block, own, k, self.spot.partner(z=k)) for k in (1, 2, 3)]
+
+    def y_own(self):
+        spot = self.spot
+        own = self.area(spot.chip(), spot.core)
+        self.y_copies = [self.go(self.block, own, 4, spot.partner(y=1))]
+        self.x_copies = [self.go(self.block, own, 8, spot.partner(x=1))]
+
+    def y_more(self, k):
+        spot = self.spot
+        self.z_copies[k - 1].wait_recv()
+        area = self.area(spot.chip(z=k), spot.core)
+        self.y_copies.append(self.go(area, area, 4 + k, spot.partner(y=1)))
+        self.x_copies.append(self.go(area, area, 8 + k, spot.partner(x=1)))
+
+    def x_more(self, k):
+        spot = self.spot
+        self.y_copies[k].wait_recv()
+        area = self.area(spot.chip(z=k, y=1), spot.core)
+        self.x_copies.append(self.go(area, area, 12 + k, spot.partner(x=1)))
+
+    def core_start(self):
+        for copy in self.x_copies:
+            copy.wait_recv()
+        self.here.wait()
+        area = self.whole.at[:, self.columns(self.spot.core)]
+        self.last = self.go(area, area, 16, self.spot.partner(core=1))
+
+    def finish(self):
+        self.last.wait_recv()
+        for copy in self.sent:
+            copy.wait_send()
+
+
+def arrive_kernel(
+    docs_ref, qkv_ref, x_ref, w_ref, mine, theirs, block, sems, local_sems, doc_sems, doc_local
+):
+    spot = Spot()
+    greet(
+        [
+            spot.partner(core=1),
+            spot.partner(z=1),
+            spot.partner(z=2),
+            spot.partner(z=3),
+            spot.partner(x=1),
+            spot.partner(y=1),
+            spot.partner(y=1, core=1),
+        ]
+    )
+    gather = Gather(spot, qkv_ref, w_ref, mine, theirs, block, sems, local_sems)
+    gather.join_start()
+    rows = docs_ref.shape[1]
+    space = x_ref.at[pl.ds(pl.multiple_of(spot.seq * rows, 16), rows), :]
+    own = pltpu.make_async_copy(docs_ref.at[spot.seq], space, doc_local.at[0])
+    own.start()
+    moves = []
+    gather.join_end()
+    gather.z_start()
+    gather.y_own()
+
+    def move_document(number, y, core):
+        device = spot.partner(y=y, core=core)
+        moves.append(send(docs_ref.at[device[1]], space, doc_sems, number, device))
+        moves[-1].start()
+
+    move_document(0, 1, 0)
+    for k in (1, 2, 3):
+        gather.y_more(k)
+    move_document(1, 1, 1)
+    move_document(2, 0, 1)
+    for k in (0, 1, 2, 3):
+        gather.x_more(k)
+    gather.core_start()
+    gather.finish()
+    own.wait()
+    for move in moves:
+        move.wait()
+
+
+def arrive(docs, qkv_shard):
+    n_docs, rows, width = docs.shape
+    shard_rows, columns = qkv_shard.shape
+    half = columns // 2
+    padded = -(-shard_rows // 16) * 16
+    qkv_shard = jnp.pad(qkv_shard, ((0, padded - shard_rows), (0, 0)))
+    anywhere = pl.BlockSpec(memory_space=pl.ANY)
+    return pl.pallas_call(
+        arrive_kernel,
+        in_specs=[anywhere, anywhere],
+        out_specs=[anywhere, anywhere],
+        out_shape=[
+            jax.ShapeDtypeStruct((n_docs * rows, width), BFLOAT),
+            jax.ShapeDtypeStruct((shard_rows * 32, columns), BFLOAT),
+        ],
+        scratch_shapes=[
+            pltpu.VMEM((padded, half), BFLOAT),
+            pltpu.VMEM((padded, half), BFLOAT),
+            pltpu.VMEM((2 * shard_rows, half), BFLOAT),
+            pltpu.SemaphoreType.DMA((2, GATHER_COPIES)),
+            pltpu.SemaphoreType.DMA((2,)),
+            pltpu.SemaphoreType.DMA((2, 3)),
+            pltpu.SemaphoreType.DMA((1,)),
+        ],
+        compiler_params=pltpu.CompilerParams(
+            collective_id=0, has_side_effects=True, vmem_limit_bytes=VMEM_LIMIT
+        ),
+        cost_estimate=cost(0, 100 << 20),
+    )(docs, qkv_shard)
+
+
+class Scatter:
+    def __init__(self, spot, grad, out, held, core_in, x_in, y_in, z_in, tail, tail_in, sems, local):
+        self.spot, self.grad, self.out = spot, grad, out
+        self.held, self.core_in, self.x_in, self.y_in, self.z_in = held, core_in, x_in, y_in, z_in
+        self.tail, self.tail_in, self.sems, self.local = tail, tail_in, sems, local
+        self.half = held.shape[1]
+        self.rows = held.shape[0] // 16
+        self.sent = []
+
+    def go(self, source, target, number, device):
+        copy = send(source, target, self.sems, number, device)
+        copy.start()
+        self.sent.append(copy)
+        return copy
+
+    def columns(self, core):
+        return pl.ds(pl.multiple_of(core * self.half, 128), self.half)
+
+    def span(self, chip):
+        return pl.ds(pl.multiple_of(chip * self.rows, 16), self.rows)
+
+    def core_start(self):
+        core = self.spot.core
+        self.first = self.go(
+            self.grad.at[:, self.columns(1 - core)], self.core_in, 0, self.spot.partner(core=1)
+        )
+        self.load = pltpu.make_async_copy(
+            self.grad.at[:, self.columns(core)], self.held, self.local.at[0]
+        )
+        self.load.start()
+
+    def core_end(self):
+        self.load.wait()
+        self.first.wait_recv()
+
+    def add(self, chip, others):
+        span = self.span(chip)
+        total = self.held[span, :].astype(SINGLE)
+        for ref, place in others:
+            total = total + ref[place, :].astype(SINGLE)
+        return span, total
+
+    def x_start(self):
+        spot = self.spot
+        self.x_copies = []
+        for number, (z, y) in enumerate((z, y) for z in (3, 2, 1, 0) for y in (1, 0)):
+            chip = spot.chip(z=z, x=1, y=y)
+            span, total = self.add(chip, [(self.core_in, self.span(chip))])
+            self.held[span, :] = total.astype(BFLOAT)
+            slot = self.x_in.at[pl.ds(number * self.rows, self.rows), :]
+            self.x_copies.append(
+                self.go(self.held.at[span, :], slot, 1 + number, spot.partner(x=1))
+            )
+
+    def y_start(self):
+        spot = self.spot
+        self.y_copies = []
+        for number, z in enumerate((3, 2, 1, 0)):
+            chip = spot.chip(z=z, y=1)
+            self.x_copies[2 * number].wait_recv()
+            place = pl.ds(2 * number * self.rows, self.rows)
+            span, total = self.add(chip, [(self.core_in, self.span(chip)), (self.x_in, place)])
+            self.held[span, :] = total.astype(BFLOAT)
+            slot = self.y_in.at[pl.ds(number * self.rows, self.rows), :]
+            self.y_copies.append(
+                self.go(self.held.at[span, :], slot, 9 + number, spot.partner(y=1))
+            )
+
+    def sum_here(self, number, z):
+        chip = self.spot.chip(z=z)
+        self.x_copies[2 * number + 1].wait_recv()
+        self.y_copies[number].wait_recv()
+        return self.add(
+            chip,
+            [
+                (self.core_in, self.span(chip)),
+                (self.x_in, pl.ds((2 * number + 1) * self.rows, self.rows)),
+                (self.y_in, pl.ds(number * self.rows, self.rows)),
+            ],
+        )
+
+    def z_start(self):
+        self.z_copies = []
+        for number, z in enumerate((3, 2, 1)):
+            span, total = self.sum_here(number, z)
+            self.held[span, :] = total.astype(BFLOAT)
+            slot = self.z_in.at[pl.ds(number * self.rows, self.rows), :]
+            self.z_copies.append(
+                self.go(self.held.at[span, :], slot, 13 + number, self.spot.partner(z=z))
+            )
+
+    def tail_start(self):
+        _, total = self.sum_here(3, 0)
+        for number in range(3):
+            self.z_copies[number].wait_recv()
+            total = total + self.z_in[pl.ds(number * self.rows, self.rows), :].astype(SINGLE)
+        self.tail[...] = total
+        part = self.rows // 2
+        core = self.spot.core
+        theirs = pl.ds(pl.multiple_of((1 - core) * part, 8), part)
+        self.last = self.go(self.tail.at[theirs, :], self.tail_in, 16, self.spot.partner(core=1))
+
+    def finish(self):
+        part = self.rows // 2
+        low = self.spot.core == 0
+        mine = jnp.where(low, self.tail[:part, :], self.tail[part:, :])
+        self.last.wait_recv()
+        other = self.tail_in[...]
+        self.out[:, : self.half] = jnp.where(low, mine, other)
+        self.out[:, self.half :] = jnp.where(low, other, mine)
+        for copy in self.sent:
+            copy.wait_send()
+
+
+def leave_kernel(
+    grad_ref,
+    dx_ref,
+    out_ref,
+    docs_ref,
+    held,
+    core_in,
+    x_in,
+    y_in,
+    z_in,
+    tail,
+    tail_in,
+    sems,
+    local_sems,
+    doc_sems,
+    doc_local,
+):
+    spot = Spot()
+    greet(
+        [
+            spot.partner(core=1),
+            spot.partner(z=1),
+            spot.partner(z=2),
+            spot.partner(z=3),
+            spot.partner(x=1),
+            spot.partner(y=1),
+            spot.partner(y=1, core=1),
+        ]
+    )
+    scatter = Scatter(
+        spot, grad_ref, out_ref, held, core_in, x_in, y_in, z_in, tail, tail_in, sems, local_sems
+    )
+    scatter.core_start()
+    rows = docs_ref.shape[1]
+    own = pltpu.make_async_copy(
+        dx_ref.at[pl.ds(pl.multiple_of(spot.seq * rows, 16), rows), :],
+        docs_ref.at[spot.seq],
+        doc_local.at[0],
+    )
+    own.start()
+    scatter.core_end()
+    scatter.x_start()
+    moves = []
+    for number, (y, core) in enumerate(((1, 0), (1, 1), (0, 1))):
+        device = spot.partner(y=y, core=core)
+        piece = dx_ref.at[pl.ds(pl.multiple_of(device[1] * rows, 16), rows), :]
+        moves.append(send(piece, docs_ref.at[spot.seq], doc_sems, number, device))
+        moves[-1].start()
+    scatter.y_start()
+    scatter.z_start()
+    scatter.tail_start()
+    scatter.finish()
+    own.wait()
+    for move in moves:
+        move.wait()
+
+
+def leave(grad, dx_docs, n_docs):
+    total_rows, columns = grad.shape
+    half = columns // 2
+    rows = total_rows // 16
+    width = dx_docs.shape[1]
+    anywhere = pl.BlockSpec(memory_space=pl.ANY)
+    return pl.pallas_call(
+        leave_kernel,
+        in_specs=[anywhere, anywhere],
+        out_specs=[pl.BlockSpec(memory_space=pltpu.VMEM), anywhere],
+        out_shape=[
+            jax.ShapeDtypeStruct((rows // 2, columns), SINGLE),
+            jax.ShapeDtypeStruct((n_docs, dx_docs.shape[0] // n_docs, width), BFLOAT),
+        ],
+        scratch_shapes=[
+            pltpu.VMEM((total_rows, half), BFLOAT),
+            pltpu.VMEM((total_rows, half), BFLOAT),
+            pltpu.VMEM((8 * rows, half), BFLOAT),
+            pltpu.VMEM((4 * rows, half), BFLOAT),
+            pltpu.VMEM((3 * rows, half), BFLOAT),
+            pltpu.VMEM((rows, half), SINGLE),
+            pltpu.VMEM((rows // 2, half), SINGLE),
+            pltpu.SemaphoreType.DMA((2, GATHER_COPIES)),
+            pltpu.SemaphoreType.DMA((1,)),
+            pltpu.SemaphoreType.DMA((2, 3)),
+            pltpu.SemaphoreType.DMA((1,)),
+        ],
+        compiler_params=pltpu.CompilerParams(
+            collective_id=1, has_side_effects=True, vmem_limit_bytes=VMEM_LIMIT
+        ),
+        cost_estimate=cost(0, 100 << 20),
+    )(grad, dx_docs)
 
 
 def on_device(
@@ -795,15 +1183,15 @@
     group = max(1, seq_size // n_docs)
     local_docs = max(1, n_docs // seq_size)
     local_rows = doc_len // group
-    orders = gather_orders()
-
-    tokens = jnp.concatenate(
-        [own_document(doc_tokens), queries.reshape(query_total, width)], 0
-    )
-    w_query, w_key, w_value = gather_weights(
-        [q_weight, kv_weight[:, :width], kv_weight[:, width:]], [orders[0], orders[1], orders[0]]
-    )
-    w_keyval = jnp.concatenate([w_key, w_value], 1)
+    dp_size = lax.axis_size("dp")
+    small = (dp_size, seq_size, n_docs) == (8, 4, 4) and width % 256 == 0 and shard_rows % 16 == 0
+
+    qkv_shard = jnp.concatenate([q_weight, kv_weight], 1)
+    if small:
+        own_doc, w_qkv = arrive(doc_tokens, qkv_shard)
+    else:
+        own_doc, w_qkv = own_document(doc_tokens), gather_rows(qkv_shard, gather_orders()[0])
+    tokens = jnp.concatenate([own_doc, queries.reshape(query_total, width)], 0)
     buckets = gather_positions(doc_buckets.astype(jnp.int16))
     if group > 1:
         part = lax.axis_index("seq") % group
@@ -818,7 +1206,7 @@
     same = jnp.kron(jnp.eye(repeats, dtype=jnp.int32), jnp.ones_like(query_buckets))
     tiled = jnp.where(same == 1, jnp.tile(query_buckets, (repeats, repeats)), bucket_count)
 
-    q_rows, kv_rows = project(tokens, attn_gain, w_query, w_keyval)
+    q_rows, kv_rows = project(tokens, attn_gain, w_qkv)
     if group > 1:
         teams = [list(range(t * group, (t + 1) * group)) for t in range(seq_size // group)]
         kv_docs = lax.all_gather(
@@ -833,31 +1221,24 @@
         q_rows, kv_rows, query_table, tiled, doc_rows, query_total, heads
     )
     mixture = jnp.concatenate([doc_mix, query_mix], 0)
-    half = out_weight.shape[1] // 2
-    half_up = up_weight.shape[1] // 2
-    o1, o2, u1, u2, d1, d2 = gather_weights(
-        [
-            out_weight[:, :half],
-            out_weight[:, half:],
-            up_weight[:, :half_up],
-            up_weight[:, half_up:],
-            down_weight[:, :half],
-            down_weight[:, half:],
-        ],
-        [orders[0], orders[1]] * 3,
-    )
-    w_out = jnp.concatenate([o1, o2], 1)
-    w_up = jnp.concatenate([u1, u2], 1)
-    w_down = jnp.concatenate([d1, d2], 1)
+    w_out_up = lax.all_gather(
+        jnp.concatenate([out_weight, up_weight], 1), ("dp", "seq"), axis=0, tiled=True
+    )
+    w_down = lax.all_gather(down_weight, ("dp", "seq"), axis=0, tiled=True)
     cotangent = jnp.concatenate(
         [own_document(doc_cot), query_cot.reshape(query_total, width)], 0
     )
-    outputs, grad_res, grad_mix, grad_out, grad_up, grad_down, grad_ff = feed(
-        tokens, mixture, cotangent, ff_gain, w_out, w_up, w_down
-    )
-    grad_down_shard = scatter_columns(grad_down, 2)
-    grad_up_shard = scatter_columns(grad_up, 2)
-    grad_out_shard = scatter_columns(grad_out, 2)
+    outputs, grad_res, grad_mix, grad_out_up, grad_down, grad_ff = feed(
+        tokens, mixture, cotangent, ff_gain, w_out_up, w_down
+    )
+    grad_down_shard = lax.psum_scatter(
+        grad_down, ("dp", "seq"), scatter_dimension=0, tiled=True
+    ).astype(SINGLE)
+    grad_out_up_shard = lax.psum_scatter(
+        grad_out_up, ("dp", "seq"), scatter_dimension=0, tiled=True
+    ).astype(SINGLE)
+    grad_out_shard = grad_out_up_shard[:, :width]
+    grad_up_shard = grad_out_up_shard[:, width:]
     doc_out = spread_document(outputs[:doc_rows], doc_tokens)
     query_out = outputs[doc_rows:].reshape(queries.shape)
 
@@ -876,12 +1257,15 @@
     dq = jnp.concatenate([doc_dq, query_dq], 0)
     dk = jnp.concatenate([doc_dk, query_dkv[:, :width]], 0)
     dv = jnp.concatenate([doc_dv, query_dkv[:, width:]], 0)
-    grad_tokens, grad_q, grad_kv, grad_attn = unproject(
-        tokens, attn_gain, dq, dk, dv, grad_res, w_query, w_keyval
-    )
-    grad_q_shard = scatter_columns(grad_q, 2)
-    grad_kv_shard = scatter_columns(grad_kv, 2)
-    doc_dx = spread_document(grad_tokens[:doc_rows].astype(BFLOAT), doc_tokens).astype(SINGLE)
+    grad_tokens, grad_low, grad_qkv, grad_attn = unproject(
+        tokens, attn_gain, dq, dk, dv, grad_res, w_qkv
+    )
+    if small:
+        grad_qkv_shard, doc_dx = leave(grad_qkv, grad_low[:doc_rows], n_docs)
+    else:
+        grad_qkv_shard = scatter_columns(grad_qkv, 2)
+        doc_dx = spread_document(grad_low[:doc_rows], doc_tokens)
+    doc_dx = doc_dx.astype(SINGLE)
     query_dx = grad_tokens[doc_rows:].reshape(queries.shape)
 
     sums = (doc_sums + query_sums).reshape(16, bucket_count, heads, 16)
@@ -902,8 +1286,8 @@
         query_out,
         doc_dx,
         query_dx,
-        grad_q_shard,
-        grad_kv_shard,
+        grad_qkv_shard[:, :width],
+        grad_qkv_shard[:, width:],
         grad_out_shard,
         grad_up_shard,
         grad_down_shard,

time: 741 us -> 492 us (0.66); the launches traced: 730 us -> 490 us
  waiting for transfers between devices: 233 us -> 43.5 us
  Pallas kernels: 246 us -> 358 us
  starting transfers between devices: 115 us -> 16.5 us
  other arithmetic: 68 us -> 26 us
  local copies, waits for them, and re-layouts: 62.3 us -> 29.4 us
  between operations: 5.74 us -> 16.7 us
    ppermute x102 -> x7, waiting for transfers between devices: 196 us -> 20.5 us  [swap(): return lax.ppermute(values, name, [(i, i ^ bit) for i in range(count)])]
    pallas_call x0 -> x2, Pallas kernels: none -> 113 us  [the longest x1 57.8 us: arrive(): pl.pallas_call(arrive_kernel, in_specs=[anywhere, anywhere], out_specs=[a...]
    ppermute x102 -> x7, starting transfers between devices: 109 us -> 10.9 us  [swap(): return lax.ppermute(values, name, [(i, i ^ bit) for i in range(count)])]
    ppermute x6 -> x3, waiting for transfers between devices: 25.8 us -> 0.01 us  [spread_document(): piece = lax.ppermute(piece, 'seq', route)]
    select_n x78 -> x0, other arithmetic: 23.1 us -> none  [gather_rows(): jnp.where(high, jnp.stack([other, held], place), jnp.stack([held, other],...]
    reduce_scatter x0 -> x2, waiting for transfers between devices: none -> 22.2 us  [the longest x1 22.2 us: on_device(): lax.psum_scatter(grad_out_up, ('dp', 'seq'), scatter_dimension=0, tiled=T...]
    dynamic_slice x15 -> x0, local copies, waits for them, and re-layouts: 14.6 us -> none  [the longest x10 9.46 us: scatter_rows(): away = lax.dynamic_index_in_dim(held, 1 - mine, place, keepdims=False)]
    ppermute x6 -> x3, waiting for transfers between devices: 10.9 us -> 0.01 us  [own_document(): piece = lax.ppermute(piece, 'seq', route)]
  transfers between devices with their start and end apart: 114 -> 17, of which waited for: 65 -> 4; matrix products, arithmetic and copies ran while one was open for 14% -> 10% of each run, Pallas kernels for 9% -> 59%
where the time goes in v2:
time: 492 us; the launch traced here: 490 us
  Pallas kernels  358 us (73%)
  waiting for transfers between devices  43.5 us (9%)
  local copies, waits for them, and re-layouts  29.4 us (6%)
  other arithmetic  26 us (5%)
  between operations  16.7 us (3%)
  starting transfers between devices  16.5 us (3%)
    pallas_call x1, Pallas kernels, doc_backward(): pl.pallas_call(functools.partial(doc_backward_kernel, labels), grid=(n_do...  70.1 us
    pallas_call x1, Pallas kernels, feed(): pl.pallas_call(functools.partial(feed_kernel, math.gcd(hidden, 768)), gri...  68.4 us
    pallas_call x1, Pallas kernels, arrive(): pl.pallas_call(arrive_kernel, in_specs=[anywhere, anywhere], out_specs=[a...  57.8 us
    pallas_call x1, Pallas kernels, leave(): pl.pallas_call(leave_kernel, in_specs=[anywhere, anywhere], out_specs=[pl...  55.1 us
    pallas_call x1, Pallas kernels, doc_forward(): pl.pallas_call(doc_forward_kernel, grid=(n_docs, steps), in_specs=[pl.Blo...  47.2 us
    reduce_scatter x1, waiting for transfers between devices, on_device(): lax.psum_scatter(grad_out_up, ('dp', 'seq'), scatter_dimension=0, tiled=T...  22.2 us
    pallas_call x1, Pallas kernels, unproject(): pl.pallas_call(unproject_kernel, grid=(rows // block,), in_specs=[along,...  20.5 us
    ppermute x7, waiting for transfers between devices, swap(): return lax.ppermute(values, name, [(i, i ^ bit) for i in range(count)])  20.5 us
  transfers between devices with their start and end apart: 17, of which 4 were waited for; matrix products, arithmetic and copies ran while one was open for 10% of the time, Pallas kernels for 59%

profile of v2, /device:TPU:0, one launch (start us, length us, event | category | flops | bytes accessed | tf_op | source)
XLA Modules:
  0.0 490.4 jit_solution(6084200328172789319)
XLA Ops:
  7.2 0.7 all-gather.5.cloned.1.call-update
  8.0 1.6 pad_maximum_fusion.8
  9.7 2.4 dynamic-slice_bitcast_fusion.11
  12.1 3.0 collective-permute-start.3
  15.3 2.1 collective-permute-start
  17.5 1.6 fusion.3.qkv_ref
  19.1 0.8 broadcast_select_fusion
  20.0 1.3 reshape.261.gain_ref
  21.2 0.6 scatter.10.table_ref
  21.8 0.8 select_n.107.bucket_ref
  22.6 1.3 reshape.264.gain_ref
  23.9 57.8 %shard_map.264 = (bf16[1024,768]{1,0:T(8,128)(2,1)}, bf16[768,2304]{1,0:T(8,128)(2,1)}) custom-call(bf16[4,256,768]{2,1,0:T(8,128)(2,1)} %docs_ref.1, bf16[32,2304]{1,0:T(8,128)(2,1)} %fusion.3.qkv_ref), custom_call_target="tpu_custom_call" | custom-call | bytes 104857600 | tf_op jit(solution)/shard_map/pallas_call | solution.py:928
  81.7 0.6 compare_reduce_fusion
  83.2 1.4 pad_maximum_fusion.5
  84.9 1.2 add_select_fusion.1
  86.2 0.5 collective-permute-start.1
  87.0 2.5 pad_maximum_fusion
  89.5 10.5 %shard_map.265 = (bf16[1536,768]{1,0:T(8,128)(2,1)}, bf16[1536,1536]{1,0:T(8,128)(2,1)}) custom-call(bf16[1536,768]{1,0:T(8,128)(2,1)} %get-tuple-element.162.x_ref, f32[1,768]{1,0:T(1,128)} %reshape.261.gain_ref, bf16[768,2304]{1,0:T(8,128)(2,1)} %get-tuple-element.77.w_ref), custom_call_target="tpu_custom_call" | custom-call | flops 5435817984 | bytes 14155776 | tf_op jit(solution)/shard_map/pallas_call | solution.py:69
  100.0 11.8 %shard_map.267 = (bf16[512,768]{1,0:T(8,128)(2,1)}, bf16[12,512,128]{2,1,0:T(8,128)(2,1)}) custom-call(bf16[1536,768]{1,0:T(8,128)(2,1)} %get-tuple-element.78.q_ref, bf16[1536,1536]{1,0:T(8,128)(2,1)} %get-tuple-element.79.k_ref.v_ref.kv_ref, f32[16,128]{1,0:T(8,128)} %copy-done.17, s32[128,128]{1,0:T(8,128)} %select_n.107.bucket_ref), custom_call_target="tpu_custom_call" | custom-call | flops 805306368 | bytes 3932160 | tf_op jit(solution)/shard_map/pallas_call | solution.py:335
  112.0 1.9 add_select_fusion
  113.9 47.2 %shard_map.266 = (bf16[1024,768]{1,0:T(8,128)(2,1)}, bf16[12,1024,1024]{2,1,0:T(8,128)(2,1)}) custom-call(bf16[1536,768]{1,0:T(8,128)(2,1)} %get-tuple-element.78.q_ref, bf16[1536,1536]{1,0:T(8,128)(2,1)} %get-tuple-element.79.k_ref.v_ref.kv_ref, bf16[1536,1536]{1,0:T(8,128)(2,1)} %get-tuple-element.79.k_ref.v_ref.kv_ref, s32[8,128]{1,0:T(8,128)} %scatter.10.table_ref, ...), custom_call_target="tpu_custom_call" | custom-call | flops 24159191040 | bytes 25165824 | tf_op jit(solution)/shard_map/pallas_call | solution.py:140
  161.1 1.7 constant_dynamic-update-slice_fusion.1
  162.9 1.4 copy-done.1
  164.3 68.4 %shard_map.268 = (bf16[1536,768]{1,0:T(8,128)(2,1)}, f32[1536,768]{1,0:T(8,128)}, bf16[1536,768]{1,0:T(8,128)(2,1)}, bf16[768,3840]{1,0:T(8,128)(2,1)}, bf16[3072,768]{1,0:T(8,128)(2,1)}, /*index=5*/f32[1,768]{1,0:T(1,128)}) custom-call(bf16[1536,768]{1,0:T(8,128)(2,1)} %get-tuple-element.162.x_ref, bf16[1536,768]{1,0:T(8,128)(2,1)} %copy-done.1, ...), custom_call_target="tpu_custom_call" | custom-call | flops 48922361856 | bytes 16515072 | tf_op jit(solution)/shard_map/pallas_call | solution.py:515
  232.8 0.7 copy-done.15
  233.6 0.8 select_reduce_fusion
  234.4 16.8 %shard_map.270 = (bf16[512,768]{1,0:T(8,128)(2,1)}, bf16[512,1536]{1,0:T(8,128)(2,1)}, f32[512,192]{1,0:T(8,128)}) custom-call(bf16[1536,768]{1,0:T(8,128)(2,1)} %get-tuple-element.78.q_ref, bf16[1536,1536]{1,0:T(8,128)(2,1)} %get-tuple-element.79.k_ref.v_ref.kv_ref, bf16[1536,768]{1,0:T(8,128)(2,1)} %get-tuple-element.83.da_ref, ...), custom_call_target="tpu_custom_call" | custom-call | flops 1610612736 | bytes 5505024 | tf_op jit(solution)/shard_map/pallas_call | solution.py:400
  251.2 70.1 %shard_map.269 = (bf16[1024,768]{1,0:T(8,128)(2,1)}, bf16[1024,768]{1,0:T(8,128)(2,1)}, bf16[1024,768]{1,0:T(8,128)(2,1)}, f32[512,192]{1,0:T(8,128)}) custom-call(bf16[1536,768]{1,0:T(8,128)(2,1)} %get-tuple-element.78.q_ref, bf16[1536,1536]{1,0:T(8,128)(2,1)} %get-tuple-element.79.k_ref.v_ref.kv_ref, ...), custom_call_target="tpu_custom_call" | custom-call | flops 56371445760 | bytes 25165824 | tf_op jit(solution)/shard_map/pallas_call | solution.py:276
  321.3 1.1 add.89
  322.6 0.4 reshape.268
  324.0 0.9 copy-done.7
  324.8 1.6 pad_maximum_fusion.4.dv_ref
  326.4 0.6 copy-done.6
  327.0 1.6 pad_maximum_fusion.3.dk_ref
  328.6 0.6 copy-done.5
  329.5 1.6 pad_maximum_fusion.2.dq_ref
  331.0 20.5 %shard_map.271 = (f32[1536,768]{1,0:T(8,128)}, bf16[1536,768]{1,0:T(8,128)(2,1)}, bf16[768,2304]{1,0:T(8,128)(2,1)}, f32[1,768]{1,0:T(1,128)}) custom-call(bf16[1536,768]{1,0:T(8,128)(2,1)} %get-tuple-element.162.x_ref, f32[1,768]{1,0:T(1,128)} %reshape.261.gain_ref, bf16[1536,768]{1,0:T(8,128)(2,1)} %pad_maximum_fusion.2.dq_ref, ...), custom_call_target="tpu_custom_call" | custom-call | flops 10871635968 | bytes 21233664 | tf_op jit(solution)/shard_map/pallas_call | solution.py:581
  351.6 0.7 reduce.11
  352.3 0.6 broadcast_in_dim.36
  353.5 1.0 constant_dynamic-slice_fusion
  354.7 2.0 collective-permute-start.6
  356.9 1.8 collective-permute-start.9
  358.7 16.7 %collective-permute-done.9 = f32[2048]{0:T(1024)S(1)} collective-permute-done((f32[2048]{0:T(1024)S(1)}, f32[2048]{0:T(1024)S(1)}, u32[]{:S(2)}, u32[]{:S(2)}) %collective-permute-start.9) | collective-permute-done | bytes 8224 | tf_op jit(solution)/shard_map/ppermute | solution.py:618
  375.3 1.7 collective-permute-start.10
  377.1 1.9 collective-permute-done.10
  379.0 1.7 collective-permute-start.11
  380.7 1.9 collective-permute-done.11
  382.7 2.8 collective-permute-start.12
  385.4 1.2 slice.109.dx_ref
  386.7 55.1 %shard_map.272 = (f32[24,2304]{1,0:T(8,128)}, bf16[4,256,768]{2,1,0:T(8,128)(2,1)}) custom-call(bf16[768,2304]{1,0:T(8,128)(2,1)} %get-tuple-element.92.grad_ref, bf16[1024,768]{1,0:T(8,128)(2,1)} %slice.109.dx_ref), custom_call_target="tpu_custom_call" | custom-call | bytes 104857600 | tf_op jit(solution)/shard_map/pallas_call | solution.py:1129
  441.8 1.7 slice.112
  443.5 1.5 slice.111
  445.1 0.9 slice.106
  446.0 1.9 convert_element_type.38
  447.9 2.7 slice.110
  450.6 0.6 slice.124
  451.3 0.7 copy.40
  452.6 0.6 fusion.6
  453.2 1.2 pad_maximum_fusion.6
  454.5 1.3 pad_maximum_fusion.7
  455.9 1.6 convert_element_type.40
  457.5 22.2 %reduce-scatter.3.cloned.1.call-done = bf16[24,3840]{1,0:T(8,128)(2,1)} async-done(((bf16[768,3840]{1,0:T(8,128)(2,1)}), bf16[24,3840]{1,0:T(8,128)(2,1)}) %reduce-scatter.3.cloned.1.call-update) | async-done | bytes 184336 | tf_op jit(solution)/shard_map/reduce_scatter | solution.py:1237
  479.7 1.6 slice.120
  481.3 1.4 slice.119
  (96 shorter events, 4.3 us)
Async XLA Ops:
  7.2 8.0 %copy-start = (s32[256,1024]{1,0:T(8,128)S(1)}, s32[256,1024]{1,0:T(8,128)}, u32[]{:S(2)}) copy-start(s32[256,1024]{1,0:T(8,128)} %param.35) | copy-start | bytes 3145732
  7.2 155.7 %all-gather.5.cloned.1.call-start = ((), (), s32[]{:S(2)}) async-start(), calls=%async_computation.3 | async-start | bytes 4866048 | tf_op jit(solution)/shard_map/all_gather | solution.py:1227
  7.9 155.0 %all-gather.3.cloned.1.call-start = ((), (), s32[]{:S(2)}) async-start(), calls=%async_computation.2 | async-start | bytes 6082560 | tf_op jit(solution)/shard_map/all_gather | solution.py:1224
  9.6 446.3 %reduce-scatter.5.cloned.1.call-start = ((), (), s32[]{:S(2)}) async-start(), calls=%async_computation.5 | async-start | bytes 4866048 | tf_op jit(solution)/shard_map/reduce_scatter | solution.py:1234
  9.7 7.7 %copy-start.16 = (f32[32,12]{0,1:T(8,128)S(1)}, f32[32,12]{0,1:T(8,128)}, u32[]{:S(2)}) copy-start(f32[32,12]{0,1:T(8,128)} %param.34) | copy-start | bytes 4612
  12.1 71.1 %collective-permute-start.3 = (bf16[1,256,768]{2,1,0:T(8,128)(2,1)}, bf16[1,256,768]{2,1,0:T(8,128)(2,1)}, u32[]{:S(2)}, u32[]{:S(2)}) collective-permute-start(bf16[1,256,768]{2,1,0:T(8,128)(2,1)} %get-tuple-element.159), channel_id=1, source_target_pairs={{0,2},{1,3},{2,0},{3,1},{4,6},{5,7},{6,4},{7,5},{8,10},{9,11},{10,... | collective-permute-start | bytes 1179656 | tf_op jit(solution)/shard_map/ppermute | solution.py:696
  15.0 68.1 %collective-permute-start.4 = (bf16[1,256,768]{2,1,0:T(8,128)(2,1)}, bf16[1,256,768]{2,1,0:T(8,128)(2,1)}, u32[]{:S(2)}, u32[]{:S(2)}) collective-permute-start(bf16[1,256,768]{2,1,0:T(8,128)(2,1)} %get-tuple-element.158), channel_id=1, source_target_pairs={{0,3},{1,2},{2,1},{3,0},{4,7},{5,6},{6,5},{7,4},{8,11},{9,10},{10,... | collective-permute-start | bytes 1179656 | tf_op jit(solution)/shard_map/ppermute | solution.py:696
  15.1 68.1 %collective-permute-start.2 = (bf16[1,256,768]{2,1,0:T(8,128)(2,1)}, bf16[1,256,768]{2,1,0:T(8,128)(2,1)}, u32[]{:S(2)}, u32[]{:S(2)}) collective-permute-start(bf16[1,256,768]{2,1,0:T(8,128)(2,1)} %get-tuple-element.157), channel_id=1, source_target_pairs={{0,1},{1,0},{2,3},{3,2},{4,5},{5,4},{6,7},{7,6},{8,9},{9,8},{10,11... | collective-permute-start | bytes 1179656 | tf_op jit(solution)/shard_map/ppermute | solution.py:696
  15.3 69.6 %collective-permute-start = (s16[256,1024]{1,0:T(8,128)(2,1)S(1)}, s16[256,1024]{1,0:T(8,128)(2,1)S(1)}, u32[]{:S(2)}, u32[]{:S(2)}) collective-permute-start(s16[256,1024]{1,0:T(8,128)(2,1)S(1)} %convert_element_type.36), channel_id=1, source_target_pairs={{0,2},{1,3},{2,0},{3,1},{4,6},{5,7},{6,4},{7,5},{8,10},{9,11},{10,... | collective-permute-start | bytes 1572872 | tf_op jit(solution)/shard_map/ppermute | solution.py:618
  83.2 1.6 copy-start.17
  84.8 1.8 copy-start.3
  84.8 2.0 copy-start.10
  84.8 2.2 copy-start.11
  86.2 25.9 %collective-permute-start.1 = (s16[2,256,1024]{2,1,0:T(8,128)(2,1)}, s16[2,256,1024]{2,1,0:T(8,128)(2,1)S(1)}, u32[]{:S(2)}, u32[]{:S(2)}) collective-permute-start(s16[2,256,1024]{2,1,0:T(8,128)(2,1)} %add_select_fusion.1), channel_id=1, source_target_pairs={{0,1},{1,0},{2,3},{3,2},{4,5},{5,4},{6,7},{7,6},{8,9},{9,8},{10,11... | collective-permute-start | bytes 3145736 | tf_op jit(solution)/shard_map/ppermute | solution.py:618
  161.1 1.7 copy-start.13
  162.9 1.4 copy-start.1
  232.7 0.8 copy-start.15
  232.7 0.8 copy-start.20
  232.7 0.9 copy-start.19
  232.8 246.9 %reduce-scatter.3.cloned.1.call-start = ((), (), s32[]{:S(2)}) async-start(), calls=%async_computation.4 | async-start | bytes 6082560 | tf_op jit(solution)/shard_map/reduce_scatter | solution.py:1237
  251.2 70.2 %copy-start.14 = (f32[512,192]{1,0:T(8,128)S(1)}, f32[512,192]{1,0:T(8,128)}, u32[]{:S(2)}) copy-start(f32[512,192]{1,0:T(8,128)} %get-tuple-element.102) | copy-start | bytes 1179652
  322.4 1.4 copy-start.4
  323.3 1.5 copy-start.7
  324.8 2.2 copy-start.6
  327.0 2.2 copy-start.5
  327.0 2.5 copy-start.12
  331.0 21.3 %copy-start.18 = (f32[1,768]{1,0:T(1,128)S(1)}, f32[1,768]{1,0:T(1,128)}, u32[]{:S(2)}) copy-start(f32[1,768]{1,0:T(1,128)} %get-tuple-element.100) | copy-start | bytes 9220
  331.0 22.3 %copy-start.2 = (bf16[1536,768]{1,0:T(8,128)(2,1)S(1)}, bf16[1536,768]{1,0:T(8,128)(2,1)}, u32[]{:S(2)}) copy-start(bf16[1536,768]{1,0:T(8,128)(2,1)} %get-tuple-element.82) | copy-start | bytes 7077892
  353.0 3.9 collective-permute-start.8
  353.5 31.9 %copy-start.9 = (bf16[1536,768]{1,0:T(8,128)(2,1)S(1)}, bf16[1536,768]{1,0:T(8,128)(2,1)}, u32[]{:S(2)}) copy-start(bf16[1536,768]{1,0:T(8,128)(2,1)} %get-tuple-element.93) | copy-start | bytes 7077892
  354.6 98.7 %collective-permute-start.5 = (bf16[1,256,768]{2,1,0:T(8,128)(2,1)}, bf16[1,256,768]{2,1,0:T(8,128)(2,1)S(1)}, u32[]{:S(2)}, u32[]{:S(2)}) collective-permute-start(bf16[1,256,768]{2,1,0:T(8,128)(2,1)} %get-tuple-element.151), channel_id=1, source_target_pairs={{1,0},{0,1},{3,2},{2,3},{5,4},{4,5},{7,6},{6,7},{9,8},{8,9},{11,10... | collective-permute-start | bytes 1179656 | tf_op jit(solution)/shard_map/ppermute | solution.py:723
  354.7 98.5 %collective-permute-start.6 = (bf16[1,256,768]{2,1,0:T(8,128)(2,1)}, bf16[1,256,768]{2,1,0:T(8,128)(2,1)S(1)}, u32[]{:S(2)}, u32[]{:S(2)}) collective-permute-start(bf16[1,256,768]{2,1,0:T(8,128)(2,1)} %get-tuple-element.150), channel_id=1, source_target_pairs={{2,0},{3,1},{0,2},{1,3},{6,4},{7,5},{4,6},{5,7},{10,8},{11,9},{8,1... | collective-permute-start | bytes 1179656 | tf_op jit(solution)/shard_map/ppermute | solution.py:723
  356.8 96.4 %collective-permute-start.7 = (bf16[1,256,768]{2,1,0:T(8,128)(2,1)}, bf16[1,256,768]{2,1,0:T(8,128)(2,1)}, u32[]{:S(2)}, u32[]{:S(2)}) collective-permute-start(bf16[1,256,768]{2,1,0:T(8,128)(2,1)} %get-tuple-element.149), channel_id=1, source_target_pairs={{3,0},{2,1},{1,2},{0,3},{7,4},{6,5},{5,6},{4,7},{11,8},{10,9},{9,1... | collective-permute-start | bytes 1179656 | tf_op jit(solution)/shard_map/ppermute | solution.py:723
  356.9 18.4 %collective-permute-start.9 = (f32[2048]{0:T(1024)S(1)}, f32[2048]{0:T(1024)S(1)}, u32[]{:S(2)}, u32[]{:S(2)}) collective-permute-start(f32[2048]{0:T(1024)S(1)} %fusion.7), channel_id=1, source_target_pairs={{0,2},{1,3},{2,0},{3,1},{4,6},{5,7},{6,4},{7,5},{8,10},{9,11},{10,... | collective-permute-start | bytes 24584 | tf_op jit(solution)/shard_map/ppermute | solution.py:618
  375.3 3.7 collective-permute-start.10
  379.0 3.7 collective-permute-start.11
  382.7 67.9 %collective-permute-start.12 = (f32[2048]{0:T(1024)S(1)}, f32[2048]{0:T(1024)S(1)}, u32[]{:S(2)}, u32[]{:S(2)}) collective-permute-start(f32[2048]{0:T(1024)S(1)} %add.93), channel_id=1, source_target_pairs={{0,16},{4,20},{8,24},{12,28},{16,0},{20,4},{24,8},{28,12},{1,17},{... | collective-permute-start | bytes 24584 | tf_op jit(solution)/shard_map/ppermute | solution.py:618
  441.8 4.2 copy-start.8
Sparse Core Ops, SparseCore 0:
  10.9 80.3 all-gather.4
  94.8 67.8 all-gather.2
  232.9 108.5 reduce-scatter.4
  347.9 131.7 reduce-scatter.2

commit v3 on v1

--- a/solution.py
+++ b/solution.py
@@ -55,14 +55,15 @@
     return lax.broadcasted_iota(jnp.int32, shape, 1) < head_dim
 
 
-def project_kernel(x_ref, gain_ref, wq_ref, wkv_ref, q_ref, kv_ref):
+def project_kernel(x_ref, gain_ref, w_ref, q_ref, kv_ref):
     values = x_ref[...].astype(SINGLE)
     normed = (values * scale_of(values) * gain_ref[...]).astype(BFLOAT)
-    q_ref[...] = nn(normed, wq_ref[...]).astype(BFLOAT)
-    kv_ref[...] = nn(normed, wkv_ref[...]).astype(BFLOAT)
-
-
-def project(tokens, gain, w_query, w_keyval):
+    width = values.shape[1]
+    q_ref[...] = nn(normed, w_ref[:, :width]).astype(BFLOAT)
+    kv_ref[...] = nn(normed, w_ref[:, width:]).astype(BFLOAT)
+
+
+def project(tokens, gain, w_qkv):
     rows, width = tokens.shape
     block = math.gcd(rows, 256)
     return pl.pallas_call(
@@ -71,8 +72,7 @@
         in_specs=[
             pl.BlockSpec((block, width), lambda i: (i, 0)),
             whole((1, width)),
-            whole(w_query.shape),
-            whole(w_keyval.shape),
+            whole(w_qkv.shape),
         ],
         out_specs=[
             pl.BlockSpec((block, width), lambda i: (i, 0)),
@@ -84,49 +84,64 @@
         ],
         compiler_params=params(),
         cost_estimate=cost(6 * rows * width * width, 12 * rows * width),
-    )(tokens, gain.reshape(1, width), w_query, w_keyval)
+    )(tokens, gain.reshape(1, width), w_qkv)
+
+
+def attend_pair(q_pair, k_pair, v_pair, table_row, bucket_ref, start, prob_ref, step, head_dim):
+    rows, keys = q_pair.shape[0], k_pair.shape[0]
+    wide = first_lanes(q_pair.shape, head_dim)
+    tall = first_lanes(v_pair.shape, head_dim)
+    table = jnp.broadcast_to(table_row, (rows, 128))
+    span = pl.ds(start, rows)
+    packed = jnp.concatenate(
+        [
+            jnp.take_along_axis(
+                table,
+                bucket_ref[span, part * 128 : part * 128 + 128].astype(jnp.int32),
+                axis=1,
+                mode="promise_in_bounds",
+            )
+            for part in range(keys // 128)
+        ],
+        1,
+    )
+    total = None
+    for side in range(2):
+        mine = wide if side == 0 else ~wide
+        mine_tall = tall if side == 0 else ~tall
+        coded = (packed >> 16) if side == 0 else ((packed << 16) >> 16)
+        scores = nt(jnp.where(mine, q_pair, 0), k_pair)
+        scores = scores + coded.astype(SINGLE) * (1.0 / FIXED)
+        shifted = jnp.exp(scores - jnp.max(scores, axis=-1, keepdims=True))
+        inverse = 1.0 / jnp.sum(shifted, axis=-1, keepdims=True)
+        soft = (shifted * inverse).astype(BFLOAT)
+        prob_ref[2 * step + side] = soft
+        term = nn(soft, jnp.where(mine_tall, v_pair, 0))
+        total = term if total is None else total + term
+    return total.astype(BFLOAT)
+
+
+def pair_lanes(step, head_dim, offset=0):
+    return pl.ds(pl.multiple_of(offset + step * 2 * head_dim, 128), 2 * head_dim)
 
 
 def doc_forward_kernel(q_ref, k_ref, v_ref, table_ref, bucket_ref, mix_ref, prob_ref):
-    rows, width = q_ref.shape
-    keys = k_ref.shape[0]
     heads = prob_ref.shape[0]
-    head_dim = width // heads
+    head_dim = q_ref.shape[1] // heads
 
     def pair(step, carry):
-        lanes = pl.ds(pl.multiple_of(step * 2 * head_dim, 128), 2 * head_dim)
-        q_pair = q_ref[:, lanes]
-        k_pair = k_ref[:, lanes]
-        v_pair = v_ref[:, lanes]
-        wide = first_lanes(q_pair.shape, head_dim)
-        tall = first_lanes(v_pair.shape, head_dim)
-        table = jnp.broadcast_to(table_ref[pl.ds(step, 1), :], (rows, 128))
-        packed = jnp.concatenate(
-            [
-                jnp.take_along_axis(
-                    table,
-                    bucket_ref[:, part * 128 : part * 128 + 128].astype(jnp.int32),
-                    axis=1,
-                    mode="promise_in_bounds",
-                )
-                for part in range(keys // 128)
-            ],
-            1,
-        )
-        total = None
-        for side in range(2):
-            mine = wide if side == 0 else ~wide
-            mine_tall = tall if side == 0 else ~tall
-            coded = (packed >> 16) if side == 0 else ((packed << 16) >> 16)
-            scores = nt(jnp.where(mine, q_pair, 0), k_pair)
-            scores = scores + coded.astype(SINGLE) * (1.0 / FIXED)
-            shifted = jnp.exp(scores - jnp.max(scores, axis=-1, keepdims=True))
-            inverse = 1.0 / jnp.sum(shifted, axis=-1, keepdims=True)
-            soft = (shifted * inverse).astype(BFLOAT)
-            prob_ref[2 * step + side] = soft
-            term = nn(soft, jnp.where(mine_tall, v_pair, 0))
-            total = term if total is None else total + term
-        mix_ref[:, lanes] = total.astype(BFLOAT)
+        lanes = pair_lanes(step, head_dim)
+        mix_ref[:, lanes] = attend_pair(
+            q_ref[:, lanes],
+            k_ref[:, lanes],
+            v_ref[:, lanes],
+            table_ref[pl.ds(step, 1), :],
+            bucket_ref,
+            0,
+            prob_ref,
+            step,
+            head_dim,
+        )
         return carry
 
     lax.fori_loop(0, heads // 2, pair, 0)
@@ -302,16 +317,13 @@
     )(q_rows, kv_rows, kv_rows, da_rows, mixture, probs, buckets)
 
 
-def query_forward_kernel(q_ref, kv_ref, table_ref, bucket_ref, mix_ref, prob_ref):
-    rows, width = q_ref.shape
-    heads = prob_ref.shape[0]
+def query_block(q_rows, k_rows, v_rows, table_ref, index, heads):
+    rows, width = q_rows.shape
     head_dim = width // heads
-    index = bucket_ref[...]
+    softs, outs = [], []
     for step in range(heads // 2):
         lanes = slice(step * 2 * head_dim, (step + 1) * 2 * head_dim)
-        q_pair = q_ref[:, lanes]
-        k_pair = kv_ref[:, lanes]
-        v_pair = kv_ref[:, width + lanes.start : width + lanes.stop]
+        q_pair, k_pair, v_pair = q_rows[:, lanes], k_rows[:, lanes], v_rows[:, lanes]
         wide = first_lanes(q_pair.shape, head_dim)
         total = None
         for side in range(2):
@@ -323,10 +335,20 @@
             shifted = jnp.exp(scores - jnp.max(scores, axis=-1, keepdims=True))
             inverse = 1.0 / jnp.sum(shifted, axis=-1, keepdims=True)
             soft = (shifted * inverse).astype(BFLOAT)
-            prob_ref[head] = soft
+            softs.append(soft)
             term = nn(soft, jnp.where(mine, v_pair, 0))
             total = term if total is None else total + term
-        mix_ref[:, lanes] = total.astype(BFLOAT)
+        outs.append(total.astype(BFLOAT))
+    return softs, jnp.concatenate(outs, 1)
+
+
+def query_forward_kernel(q_ref, kv_ref, table_ref, bucket_ref, mix_ref, prob_ref):
+    width = q_ref.shape[1]
+    softs, mix_ref[...] = query_block(
+        q_ref[...], kv_ref[:, :width], kv_ref[:, width:], table_ref, bucket_ref[...], prob_ref.shape[0]
+    )
+    for head, soft in enumerate(softs):
+        prob_ref[head] = soft
 
 
 def query_forward(q_rows, kv_rows, table, buckets, start, count, heads):
@@ -430,44 +452,40 @@
     mix_ref,
     dy_ref,
     gain_ref,
-    wo_ref,
-    wu_ref,
+    wou_ref,
     wd_ref,
     y_ref,
     dh_ref,
     da_ref,
-    go_ref,
-    gu_ref,
+    gou_ref,
     gd_ref,
     gg_ref,
-    go_acc,
-    gu_acc,
+    gou_acc,
     gd_acc,
     stage,
     sems,
 ):
     step = pl.program_id(0)
-    hidden = wu_ref.shape[1]
-    width = wu_ref.shape[0]
+    hidden, width = wd_ref.shape
 
     @pl.when(step == 0)
     def _():
-        go_acc[...] = jnp.zeros_like(go_acc)
-        gu_acc[...] = jnp.zeros_like(gu_acc)
+        gou_acc[...] = jnp.zeros_like(gou_acc)
         gd_acc[...] = jnp.zeros_like(gd_acc)
         gg_ref[...] = jnp.zeros_like(gg_ref)
 
     mixture = mix_ref[...]
     dy = dy_ref[...]
     gain = gain_ref[...]
-    residual = x_ref[...].astype(SINGLE) + nn(mixture, wo_ref[...])
+    residual = x_ref[...].astype(SINGLE) + nn(mixture, wou_ref[:, :width])
     scale = scale_of(residual)
     second = (residual * scale * gain).astype(BFLOAT)
     y = residual
     grad_second = jnp.zeros_like(residual)
     for part in range(hidden // chunk):
         span = slice(part * chunk, (part + 1) * chunk)
-        pre = nn(second, wu_ref[:, span])
+        past = slice(width + part * chunk, width + (part + 1) * chunk)
+        pre = nn(second, wou_ref[:, past])
         grad_hidden = nt(dy, wd_ref[span, :])
         square = pre * pre
         tanh = jnp.tanh(pre * (GELU_A + (GELU_A * GELU_B) * square))
@@ -477,22 +495,22 @@
         act_low = act.astype(BFLOAT)
         grad_pre = (grad_hidden * slope).astype(BFLOAT)
         y = y + nn(act_low, wd_ref[span, :])
-        grad_second = grad_second + nt(grad_pre, wu_ref[:, span])
+        grad_second = grad_second + nt(grad_pre, wou_ref[:, past])
         gd_acc[span, :] += tn(act_low, dy)
-        gu_acc[:, span] += tn(second, grad_pre)
+        gou_acc[:, past] += tn(second, grad_pre)
     y_ref[...] = y.astype(BFLOAT)
     gg_ref[...] += jnp.sum(grad_second * residual * scale, axis=0, keepdims=True)
     grad_res = dy.astype(SINGLE) + norm_back(residual, scale, grad_second * gain)
     dh_ref[...] = grad_res
     grad_low = grad_res.astype(BFLOAT)
-    da_ref[...] = nt(grad_low, wo_ref[...]).astype(BFLOAT)
-    go_acc[...] += tn(mixture, grad_low)
+    da_ref[...] = nt(grad_low, wou_ref[:, :width]).astype(BFLOAT)
+    gou_acc[:, :width] += tn(mixture, grad_low)
 
     @pl.when(step == pl.num_programs(0) - 1)
     def _():
         pieces = []
         rows, columns = stage.shape[1:]
-        for acc, out in ((gd_acc, gd_ref), (gu_acc, gu_ref), (go_acc, go_ref)):
+        for acc, out in ((gd_acc, gd_ref), (gou_acc, gou_ref)):
             for r in range(acc.shape[0] // rows):
                 for c in range(acc.shape[1] // columns):
                     spot = (pl.ds(r * rows, rows), pl.ds(c * columns, columns))
@@ -510,9 +528,9 @@
                 copy.wait()
 
 
-def feed(tokens, mixture, cotangent, gain, w_out, w_up, w_down):
+def feed(tokens, mixture, cotangent, gain, w_out_up, w_down):
     rows, width = tokens.shape
-    hidden = w_up.shape[1]
+    hidden = w_down.shape[0]
     block = math.gcd(rows, 256)
     along = pl.BlockSpec((block, width), lambda i: (i, 0))
     anywhere = pl.BlockSpec(memory_space=pl.ANY)
@@ -524,90 +542,79 @@
             along,
             along,
             whole((1, width)),
-            whole(w_out.shape),
-            whole(w_up.shape),
+            whole(w_out_up.shape),
             whole(w_down.shape),
         ],
-        out_specs=[along, along, along, anywhere, anywhere, anywhere, whole((1, width))],
+        out_specs=[along, along, along, anywhere, anywhere, whole((1, width))],
         out_shape=[
             jax.ShapeDtypeStruct((rows, width), BFLOAT),
             jax.ShapeDtypeStruct((rows, width), SINGLE),
             jax.ShapeDtypeStruct((rows, width), BFLOAT),
-            jax.ShapeDtypeStruct(w_out.shape, BFLOAT),
-            jax.ShapeDtypeStruct(w_up.shape, BFLOAT),
+            jax.ShapeDtypeStruct(w_out_up.shape, BFLOAT),
             jax.ShapeDtypeStruct(w_down.shape, BFLOAT),
             jax.ShapeDtypeStruct((1, width), SINGLE),
         ],
         scratch_shapes=[
-            pltpu.VMEM(w_out.shape, SINGLE),
-            pltpu.VMEM(w_up.shape, SINGLE),
+            pltpu.VMEM(w_out_up.shape, SINGLE),
             pltpu.VMEM(w_down.shape, SINGLE),
             pltpu.VMEM((2, width, width), BFLOAT),
             pltpu.SemaphoreType.DMA((2,)),
         ],
         compiler_params=params(),
         cost_estimate=cost(2 * rows * width * (6 * hidden + 3 * width), 14 * rows * width),
-    )(tokens, mixture, cotangent, gain.reshape(1, width), w_out, w_up, w_down)
+    )(tokens, mixture, cotangent, gain.reshape(1, width), w_out_up, w_down)
 
 
 def unproject_kernel(
-    x_ref, gain_ref, dq_ref, dk_ref, dv_ref, dh_ref, wq_ref, wkv_ref, dx_ref, gq_ref, gkv_ref, gg_ref, gq_acc, gkv_acc
+    x_ref, gain_ref, dq_ref, dk_ref, dv_ref, dh_ref, w_ref, dx_ref, low_ref, gw_ref, gg_ref, acc
 ):
     step = pl.program_id(0)
-    width = wq_ref.shape[0]
+    width = w_ref.shape[0]
 
     @pl.when(step == 0)
     def _():
-        gq_acc[...] = jnp.zeros_like(gq_acc)
-        gkv_acc[...] = jnp.zeros_like(gkv_acc)
+        acc[...] = jnp.zeros_like(acc)
         gg_ref[...] = jnp.zeros_like(gg_ref)
 
     values = x_ref[...].astype(SINGLE)
     gain = gain_ref[...]
     scale = scale_of(values)
     normed = (values * scale * gain).astype(BFLOAT)
-    dq, dk, dv = dq_ref[...], dk_ref[...], dv_ref[...]
-    gq_acc[...] += tn(normed, dq)
-    gkv_acc[:, :width] += tn(normed, dk)
-    gkv_acc[:, width:] += tn(normed, dv)
-    grad = nt(dq, wq_ref[...]) + nt(dk, wkv_ref[:, :width]) + nt(dv, wkv_ref[:, width:])
+    grad = jnp.zeros_like(values)
+    for number, ref in enumerate((dq_ref, dk_ref, dv_ref)):
+        span = slice(number * width, (number + 1) * width)
+        part = ref[...]
+        acc[:, span] += tn(normed, part)
+        grad = grad + nt(part, w_ref[:, span])
     gg_ref[...] += jnp.sum(grad * values * scale, axis=0, keepdims=True)
-    dx_ref[...] = dh_ref[...] + norm_back(values, scale, grad * gain)
+    dx = dh_ref[...] + norm_back(values, scale, grad * gain)
+    dx_ref[...] = dx
+    low_ref[...] = dx.astype(BFLOAT)
 
     @pl.when(step == pl.num_programs(0) - 1)
     def _():
-        gq_ref[...] = gq_acc[...].astype(BFLOAT)
-        gkv_ref[...] = gkv_acc[...].astype(BFLOAT)
-
-
-def unproject(tokens, gain, dq, dk, dv, grad_res, w_query, w_keyval):
+        gw_ref[...] = acc[...].astype(BFLOAT)
+
+
+def unproject(tokens, gain, dq, dk, dv, grad_res, w_qkv):
     rows, width = tokens.shape
     block = math.gcd(rows, 256)
     along = pl.BlockSpec((block, width), lambda i: (i, 0))
     return pl.pallas_call(
         unproject_kernel,
         grid=(rows // block,),
-        in_specs=[
-            along,
-            whole((1, width)),
-            along,
-            along,
-            along,
-            along,
-            whole(w_query.shape),
-            whole(w_keyval.shape),
-        ],
-        out_specs=[along, whole(w_query.shape), whole(w_keyval.shape), whole((1, width))],
+        in_specs=[along, whole((1, width)), along, along, along, along, whole(w_qkv.shape)],
+        out_specs=[along, along, whole(w_qkv.shape), whole((1, width))],
         out_shape=[
             jax.ShapeDtypeStruct((rows, width), SINGLE),
-            jax.ShapeDtypeStruct(w_query.shape, BFLOAT),
-            jax.ShapeDtypeStruct(w_keyval.shape, BFLOAT),
+            jax.ShapeDtypeStruct((rows, width), BFLOAT),
+            jax.ShapeDtypeStruct(w_qkv.shape, BFLOAT),
             jax.ShapeDtypeStruct((1, width), SINGLE),
         ],
-        scratch_shapes=[pltpu.VMEM(w_query.shape, SINGLE), pltpu.VMEM(w_keyval.shape, SINGLE)],
+        scratch_shapes=[pltpu.VMEM(w_qkv.shape, SINGLE)],
         compiler_params=params(),
         cost_estimate=cost(12 * rows * width * width, 18 * rows * width),
-    )(tokens, gain.reshape(1, width), dq, dk, dv, grad_res, w_query, w_keyval)
+    )(tokens, gain.reshape(1, width), dq, dk, dv, grad_res, w_qkv)
 
 
 def bits_of(count):
@@ -651,13 +658,6 @@
             high, jnp.stack([other, held], place), jnp.stack([held, other], place)
         )
     return held.reshape(-1, shard.shape[1])
-
-
-def gather_weights(shards, orders):
-    pieces = []
-    for shard, order in zip(shards, orders):
-        pieces.append(gather_rows(shard, order))
-    return pieces
 
 
 def scatter_rows(values, order):
@@ -764,6 +764,1126 @@
         )
         done.append(item)
     return held.reshape(-1, shard.shape[1])
+
+
+class Spot:
+    def __init__(self):
+        self.dp = lax.axis_index("dp")
+        self.seq = lax.axis_index("seq")
+        self.core = self.seq % 2
+        self.y = self.seq // 2
+        self.x = self.dp % 2
+        self.z = self.dp // 2
+
+    def partner(self, z=0, x=0, y=0, core=0):
+        dp = self.flip(self.z, z) * 2 + self.flip(self.x, x)
+        seq = self.flip(self.y, y) * 2 + self.flip(self.core, core)
+        return (dp, seq)
+
+    @staticmethod
+    def flip(value, bits):
+        if bits == 0:
+            return value
+        if bits == 1:
+            return value + 1 - 2 * (value % 2)
+        if bits == 2:
+            return (value + 2) % 4
+        return 3 - value
+
+    def chip(self, z=0, x=0, y=0):
+        return (self.flip(self.z, z) * 2 + self.flip(self.x, x)) * 2 + self.flip(self.y, y)
+
+
+def send(source, target, sems, number, device):
+    return pltpu.make_async_remote_copy(
+        src_ref=source,
+        dst_ref=target,
+        send_sem=sems.at[0, number],
+        recv_sem=sems.at[1, number],
+        device_id=device,
+        device_id_type=pl.DeviceIdType.MESH,
+    )
+
+
+def greet(partners):
+    barrier = pltpu.get_barrier_semaphore()
+    for device in partners:
+        pl.semaphore_signal(barrier, inc=1, device_id=device, device_id_type=pl.DeviceIdType.MESH)
+    pl.semaphore_wait(barrier, len(partners))
+
+
+COPIES = 17
+
+
+class Gather:
+    def __init__(self, spot, shard, whole_ref, mine, theirs, block, sems, local):
+        self.spot, self.shard, self.whole = spot, shard, whole_ref
+        self.mine, self.theirs, self.block = mine, theirs, block
+        self.sems, self.local = sems, local
+        self.rows, self.half = block.shape
+
+    def columns(self, core):
+        return pl.ds(pl.multiple_of(core * self.half, 128), self.half)
+
+    def area(self, **bits):
+        row = pl.multiple_of(self.spot.chip(**bits) * self.rows, 16)
+        return self.whole.at[pl.ds(row, self.rows), self.columns(self.spot.core)]
+
+    def copy(self, number):
+        spot = self.spot
+        if number == 0:
+            source, target = self.shard.at[:, self.columns(1 - spot.core)], self.theirs
+            device = spot.partner(core=1)
+        elif number < 4:
+            source, target, device = self.block, self.area(), spot.partner(z=number)
+        elif number < 8:
+            target, device = self.area(z=number - 4), spot.partner(y=1)
+            source = self.block if number == 4 else target
+        elif number < 16:
+            target = self.area(z=(number - 8) % 4, y=(number - 8) // 4)
+            source, device = self.block if number == 8 else target, spot.partner(x=1)
+        else:
+            source = target = self.whole.at[:, self.columns(spot.core)]
+            device = spot.partner(core=1)
+        return send(source, target, self.sems, number, device)
+
+    def load(self):
+        return pltpu.make_async_copy(
+            self.shard.at[:, self.columns(self.spot.core)], self.mine, self.local.at[0]
+        )
+
+    def here(self):
+        return pltpu.make_async_copy(self.block, self.area(), self.local.at[1])
+
+    def join_start(self):
+        self.copy(0).start()
+        self.load().start()
+
+    def join_end(self):
+        self.load().wait()
+        self.copy(0).wait_recv()
+        part = self.rows // 2
+        low = self.spot.core == 0
+        mine = self.mine[...].astype(SINGLE)[:part]
+        theirs = self.theirs[...].astype(SINGLE)[:part]
+        self.block[:part, :] = jnp.where(low, mine, theirs).astype(BFLOAT)
+        self.block[part:, :] = jnp.where(low, theirs, mine).astype(BFLOAT)
+        self.here().start()
+
+    def z_start(self):
+        for number in (1, 2, 3):
+            self.copy(number).start()
+
+    def y_own(self):
+        self.copy(4).start()
+        self.copy(8).start()
+
+    def y_more(self):
+        for k in (1, 2, 3):
+            self.copy(k).wait_recv()
+            self.copy(4 + k).start()
+            self.copy(8 + k).start()
+
+    def x_more(self):
+        for k in (0, 1, 2, 3):
+            self.copy(4 + k).wait_recv()
+            self.copy(12 + k).start()
+
+    def swap_start(self):
+        for number in range(8, 16):
+            self.copy(number).wait_recv()
+        self.here().wait()
+        self.copy(16).start()
+
+    def finish(self):
+        self.copy(16).wait_recv()
+        for number in range(COPIES):
+            self.copy(number).wait_send()
+
+
+class Move:
+    PARTNERS = ((1, 0), (1, 1), (0, 1))
+
+    def __init__(self, spot, source, target, own_target, sems, local):
+        self.spot, self.source, self.target = spot, source, target
+        self.own_target, self.sems, self.local = own_target, sems, local
+
+    def own(self):
+        return pltpu.make_async_copy(
+            self.source(self.spot.seq), self.own_target(self.spot.seq), self.local
+        )
+
+    def copy(self, number):
+        y, core = self.PARTNERS[number]
+        device = self.spot.partner(y=y, core=core)
+        return send(self.source(device[1]), self.target(self.spot.seq), self.sems, number, device)
+
+    def start(self):
+        self.own().start()
+        for number in range(3):
+            self.copy(number).start()
+
+    def finish(self):
+        self.own().wait()
+        for number in range(3):
+            self.copy(number).wait()
+
+
+def all_partners(spot):
+    return [
+        spot.partner(core=1),
+        spot.partner(z=1),
+        spot.partner(z=2),
+        spot.partner(z=3),
+        spot.partner(x=1),
+        spot.partner(y=1),
+        spot.partner(y=1, core=1),
+    ]
+
+
+def row_block(ref, rows):
+    return lambda number: ref.at[pl.ds(pl.multiple_of(number * rows, 16), rows), :]
+
+
+def front_kernel(
+    docs_ref,
+    queries_ref,
+    doc_cot_ref,
+    query_cot_ref,
+    qkv_shard,
+    ou_shard,
+    down_shard,
+    bucket_shard,
+    gain_ref,
+    doc_table_ref,
+    query_table_ref,
+    query_bucket_ref,
+    tokens_out,
+    cots_out,
+    w_out,
+    ou_out,
+    down_out,
+    bucket_out,
+    qkv_out,
+    mix_ref,
+    prob_ref,
+    query_prob_ref,
+    x_v,
+    w_v,
+    qkv_v,
+    bucket_v,
+    qkv_mine,
+    qkv_theirs,
+    qkv_block,
+    ou_mine,
+    ou_theirs,
+    ou_block,
+    down_mine,
+    down_theirs,
+    down_block,
+    gather_sems,
+    move_sems,
+    local,
+):
+    step = pl.program_id(0)
+    last = pl.num_programs(0) - 1
+    spot = Spot()
+    n_docs, shard_rows, width = docs_ref.shape
+    doc_rows = n_docs * shard_rows
+    query_rows = queries_ref.shape[0]
+    heads = prob_ref.shape[0]
+    head_dim = width // heads
+    block = prob_ref.shape[1]
+
+    gathers = []
+    for number, parts in enumerate(
+        (
+            (qkv_shard, w_v, qkv_mine, qkv_theirs, qkv_block),
+            (ou_shard, ou_out, ou_mine, ou_theirs, ou_block),
+            (down_shard, down_out, down_mine, down_theirs, down_block),
+        )
+    ):
+        gathers.append(
+            Gather(spot, *parts, gather_sems.at[number], local.at[pl.ds(2 * number, 2)])
+        )
+    g_qkv, g_ou, g_down = gathers
+    token_move = Move(
+        spot,
+        lambda number: docs_ref.at[number],
+        row_block(x_v, shard_rows),
+        row_block(x_v, shard_rows),
+        move_sems.at[0],
+        local.at[6],
+    )
+    cot_move = Move(
+        spot,
+        lambda number: doc_cot_ref.at[number],
+        row_block(cots_out, shard_rows),
+        row_block(cots_out, shard_rows),
+        move_sems.at[1],
+        local.at[7],
+    )
+    query_load = pltpu.make_async_copy(
+        queries_ref, x_v.at[pl.ds(doc_rows, query_rows), :], local.at[8]
+    )
+    cot_copy = pltpu.make_async_copy(
+        query_cot_ref, cots_out.at[pl.ds(doc_rows, query_rows), :], local.at[9]
+    )
+    bucket_rows = row_block(bucket_v, shard_rows)
+    bucket_load = pltpu.make_async_copy(bucket_shard, bucket_rows(spot.seq), local.at[10])
+    bucket_y = send(
+        bucket_shard, bucket_rows(spot.seq), move_sems.at[2], 0, spot.partner(y=1)
+    )
+    near = bucket_rows(spot.seq)
+    far = bucket_rows(spot.partner(y=1)[1])
+    bucket_near = send(near, near, move_sems.at[2], 1, spot.partner(core=1))
+    bucket_far = send(far, far, move_sems.at[2], 2, spot.partner(core=1))
+    saves = [
+        pltpu.make_async_copy(x_v, tokens_out, local.at[11]),
+        pltpu.make_async_copy(w_v, w_out, local.at[12]),
+        pltpu.make_async_copy(qkv_v, qkv_out, local.at[13]),
+        pltpu.make_async_copy(bucket_v, bucket_out, local.at[14]),
+    ]
+
+    @pl.when(step == 0)
+    def _():
+        greet(all_partners(spot))
+        g_qkv.join_start()
+        query_load.start()
+        bucket_load.start()
+        token_move.own().start()
+        g_ou.join_start()
+        g_down.join_start()
+        g_qkv.join_end()
+        g_qkv.z_start()
+        g_qkv.y_own()
+        token_move.copy(0).start()
+        token_move.copy(2).start()
+        g_ou.join_end()
+        g_down.join_end()
+        g_qkv.y_more()
+        token_move.copy(1).start()
+        g_ou.z_start()
+        g_down.z_start()
+        g_qkv.x_more()
+        bucket_y.start()
+        bucket_load.wait()
+        bucket_near.start()
+        g_qkv.swap_start()
+        g_ou.y_own()
+        g_down.y_own()
+        query_load.wait()
+        token_move.finish()
+        g_qkv.finish()
+        saves[0].start()
+        saves[1].start()
+
+        def project_block(number, carry):
+            span = pl.ds(pl.multiple_of(number * block, 16), block)
+            values = x_v[span, :].astype(SINGLE)
+            normed = (values * scale_of(values) * gain_ref[...]).astype(BFLOAT)
+            for part in range(3):
+                lanes = slice(part * width, (part + 1) * width)
+                qkv_v[span, lanes] = nn(normed, w_v[:, lanes]).astype(BFLOAT)
+            return carry
+
+        blocks = (doc_rows + query_rows) // block
+        lax.fori_loop(0, blocks // 2, project_block, 0)
+        g_ou.y_more()
+        g_down.y_more()
+        lax.fori_loop(blocks // 2, blocks, project_block, 0)
+        saves[2].start()
+        cot_move.start()
+        cot_copy.start()
+        bucket_y.wait_recv()
+        bucket_far.start()
+
+        def query_step(number, carry):
+            span = pl.ds(pl.multiple_of(doc_rows + number * 128, 16), 128)
+            softs, mixed = query_block(
+                qkv_v[span, :width],
+                qkv_v[span, width : 2 * width],
+                qkv_v[span, 2 * width :],
+                query_table_ref,
+                query_bucket_ref[...],
+                heads,
+            )
+            mix_ref[span, :] = mixed
+            for head, soft in enumerate(softs):
+                query_prob_ref[head, pl.ds(pl.multiple_of(number * 128, 16), 128), :] = soft
+            return carry
+
+        lax.fori_loop(0, query_rows // 128, query_step, 0)
+        bucket_near.wait()
+        bucket_far.wait()
+        bucket_y.wait_send()
+        saves[3].start()
+
+    @pl.when(step == 1)
+    def _():
+        g_ou.x_more()
+        g_down.x_more()
+
+    @pl.when(step == last - 1)
+    def _():
+        g_ou.swap_start()
+
+    @pl.when(step == last)
+    def _():
+        g_down.swap_start()
+
+    @pl.when(step > 0)
+    def _():
+        span = pl.ds(pl.multiple_of((step - 1) * block, 16), block)
+
+        def pair(number, carry):
+            lanes = pair_lanes(number, head_dim)
+            mix_ref[span, lanes] = attend_pair(
+                qkv_v[span, lanes],
+                qkv_v[:doc_rows, pair_lanes(number, head_dim, width)],
+                qkv_v[:doc_rows, pair_lanes(number, head_dim, 2 * width)],
+                doc_table_ref[pl.ds(number, 1), :],
+                bucket_v,
+                pl.multiple_of((step - 1) * block, 16),
+                prob_ref,
+                number,
+                head_dim,
+            )
+            return carry
+
+        lax.fori_loop(0, heads // 2, pair, 0)
+
+    @pl.when(step == last)
+    def _():
+        g_ou.finish()
+        g_down.finish()
+        cot_move.finish()
+        cot_copy.wait()
+        for save in saves:
+            save.wait()
+
+
+def gather_scratch(shard):
+    rows, columns = shard.shape
+    padded = -(-rows // 16) * 16
+    half = columns // 2
+    return [
+        pltpu.VMEM((padded, half), BFLOAT),
+        pltpu.VMEM((padded, half), BFLOAT),
+        pltpu.VMEM((2 * rows, half), BFLOAT),
+    ]
+
+
+def pad_rows(shard):
+    rows = shard.shape[0]
+    return jnp.pad(shard, ((0, -rows % 16), (0, 0)))
+
+
+def front(
+    docs,
+    queries,
+    doc_cot,
+    query_cot,
+    shards,
+    buckets,
+    gain,
+    doc_table,
+    query_table,
+    query_buckets,
+    heads,
+):
+    n_docs, shard_rows, width = docs.shape
+    doc_rows = n_docs * shard_rows
+    query_rows = queries.shape[0]
+    rows = doc_rows + query_rows
+    keys = buckets.shape[1]
+    block = 256
+    steps = doc_rows // block
+    anywhere = pl.BlockSpec(memory_space=pl.ANY)
+    wholes = [jax.ShapeDtypeStruct((shard.shape[0] * 32, shard.shape[1]), BFLOAT) for shard in shards]
+    scratch = []
+    for shard in shards:
+        scratch += gather_scratch(shard)
+    return pl.pallas_call(
+        front_kernel,
+        grid=(steps + 1,),
+        in_specs=[anywhere] * 8
+        + [
+            whole((1, width)),
+            whole(doc_table.shape),
+            whole(query_table.shape),
+            whole(query_buckets.shape),
+        ],
+        out_specs=[anywhere] * 7
+        + [
+            whole((rows, width)),
+            pl.BlockSpec((heads, block, keys), lambda i: (0, jnp.maximum(i - 1, 0), 0)),
+            whole((heads, query_rows, 128)),
+        ],
+        out_shape=[
+            jax.ShapeDtypeStruct((rows, width), BFLOAT),
+            jax.ShapeDtypeStruct((rows, width), BFLOAT),
+            *wholes,
+            jax.ShapeDtypeStruct((keys, keys), jnp.int16),
+            jax.ShapeDtypeStruct((rows, 3 * width), BFLOAT),
+            jax.ShapeDtypeStruct((rows, width), BFLOAT),
+            jax.ShapeDtypeStruct((heads, doc_rows, keys), BFLOAT),
+            jax.ShapeDtypeStruct((heads, query_rows, 128), BFLOAT),
+        ],
+        scratch_shapes=[
+            pltpu.VMEM((rows, width), BFLOAT),
+            pltpu.VMEM((width, 3 * width), BFLOAT),
+            pltpu.VMEM((rows, 3 * width), BFLOAT),
+            pltpu.VMEM((keys, keys), jnp.int16),
+            *scratch,
+            pltpu.SemaphoreType.DMA((3, 2, COPIES)),
+            pltpu.SemaphoreType.DMA((3, 2, 3)),
+            pltpu.SemaphoreType.DMA((15,)),
+        ],
+        compiler_params=pltpu.CompilerParams(
+            collective_id=0, has_side_effects=True, vmem_limit_bytes=VMEM_LIMIT
+        ),
+        cost_estimate=cost(6 * rows * width * width, 100 << 20),
+    )(
+        docs,
+        queries,
+        doc_cot,
+        query_cot,
+        *[pad_rows(shard) for shard in shards],
+        buckets,
+        gain.reshape(1, width),
+        doc_table,
+        query_table,
+        query_buckets,
+    )
+
+
+class Scatter:
+    Z_ORDER = (3, 2, 1, 0)
+
+    def __init__(self, spot, away, buffers, sems):
+        self.spot, self.away, self.sems = spot, away, sems
+        self.held, self.core_in, self.x_in, self.y_in, self.z_in, self.tail, self.tail_in = buffers
+        self.half = self.held.shape[1]
+        self.rows = self.held.shape[0] // 16
+
+    def span(self, **bits):
+        return pl.ds(pl.multiple_of(self.spot.chip(**bits) * self.rows, 16), self.rows)
+
+    def slot(self, number):
+        return pl.ds(number * self.rows, self.rows)
+
+    def copy(self, number):
+        spot = self.spot
+        if number == 0:
+            source, target, device = self.away, self.core_in, spot.partner(core=1)
+        elif number < 9:
+            index = number - 1
+            source = self.held.at[self.span(z=self.Z_ORDER[index // 2], x=1, y=1 - index % 2), :]
+            target, device = self.x_in.at[self.slot(index), :], spot.partner(x=1)
+        elif number < 13:
+            index = number - 9
+            source = self.held.at[self.span(z=self.Z_ORDER[index], y=1), :]
+            target, device = self.y_in.at[self.slot(index), :], spot.partner(y=1)
+        elif number < 16:
+            index = number - 13
+            source = self.held.at[self.span(z=self.Z_ORDER[index]), :]
+            target = self.z_in.at[self.slot(index), :]
+            device = spot.partner(z=self.Z_ORDER[index])
+        else:
+            part = self.rows // 2
+            theirs = pl.ds(pl.multiple_of((1 - spot.core) * part, 8), part)
+            source, target, device = self.tail.at[theirs, :], self.tail_in, spot.partner(core=1)
+        return send(source, target, self.sems, number, device)
+
+    def add(self, span, others):
+        total = self.held[span, :].astype(SINGLE) + self.core_in[span, :].astype(SINGLE)
+        for ref, place in others:
+            total = total + ref[place, :].astype(SINGLE)
+        return total
+
+    def core_end(self):
+        self.copy(0).wait_recv()
+
+    def x_step(self, index):
+        span = self.span(z=self.Z_ORDER[index // 2], x=1, y=1 - index % 2)
+        self.held[span, :] = self.add(span, []).astype(BFLOAT)
+        self.copy(1 + index).start()
+
+    def y_step(self, index):
+        self.copy(1 + 2 * index).wait_recv()
+        span = self.span(z=self.Z_ORDER[index], y=1)
+        total = self.add(span, [(self.x_in, self.slot(2 * index))])
+        self.held[span, :] = total.astype(BFLOAT)
+        self.copy(9 + index).start()
+
+    def here(self, index):
+        self.copy(2 + 2 * index).wait_recv()
+        self.copy(9 + index).wait_recv()
+        span = self.span(z=self.Z_ORDER[index])
+        others = [(self.x_in, self.slot(2 * index + 1)), (self.y_in, self.slot(index))]
+        return span, self.add(span, others)
+
+    def z_step(self, index):
+        span, total = self.here(index)
+        self.held[span, :] = total.astype(BFLOAT)
+        self.copy(13 + index).start()
+
+    def tail_start(self):
+        _, total = self.here(3)
+        for index in range(3):
+            self.copy(13 + index).wait_recv()
+            total = total + self.z_in[self.slot(index), :].astype(SINGLE)
+        self.tail[...] = total
+        self.copy(16).start()
+
+    def finish(self):
+        part = self.rows // 2
+        low = self.spot.core == 0
+        mine = jnp.where(low, self.tail[:part, :], self.tail[part:, :])
+        self.copy(16).wait_recv()
+        other = self.tail_in[...]
+        for number in range(COPIES):
+            self.copy(number).wait_send()
+        return jnp.where(low, mine, other), jnp.where(low, other, mine)
+
+
+def scatter_scratch(rows, columns):
+    half, part = columns // 2, rows // 16
+    return [
+        pltpu.VMEM((rows, half), BFLOAT),
+        pltpu.VMEM((rows, half), BFLOAT),
+        pltpu.VMEM((8 * part, half), BFLOAT),
+        pltpu.VMEM((4 * part, half), BFLOAT),
+        pltpu.VMEM((3 * part, half), BFLOAT),
+        pltpu.VMEM((part, half), SINGLE),
+        pltpu.VMEM((part // 2, half), SINGLE),
+    ]
+
+
+def half_of(ref, core):
+    half = ref.shape[1] // 2
+    return ref.at[:, pl.ds(pl.multiple_of(core * half, 128), half)]
+
+
+def back_kernel(
+    labels,
+    doc_steps,
+    q_ref,
+    k_ref,
+    v_ref,
+    query_k_ref,
+    query_v_ref,
+    da_ref,
+    mix_ref,
+    prob_ref,
+    query_prob_ref,
+    query_bucket_ref,
+    grad_ou_ref,
+    grad_down_ref,
+    y_ref,
+    dq_ref,
+    dkv_ref,
+    ds_ref,
+    sums_ref,
+    ou_ref,
+    down_ref,
+    docs_ref,
+    dk_acc,
+    dv_acc,
+    ds_keep,
+    *rest,
+):
+    ou_buffers, down_buffers, (sems, move_sems, local) = rest[:7], rest[7:14], rest[14:]
+    step = pl.program_id(0)
+    last = pl.num_programs(0) - 1
+    spot = Spot()
+    rows, width = q_ref.shape
+    pairs = prob_ref.shape[0] // 2
+    keys = k_ref.shape[0]
+    heads = query_prob_ref.shape[0]
+    head_dim = width // heads
+    ou = Scatter(spot, half_of(grad_ou_ref, 1 - spot.core), ou_buffers, sems.at[0])
+    down = Scatter(spot, half_of(grad_down_ref, 1 - spot.core), down_buffers, sems.at[1])
+    both = (ou, down)
+    loads = [
+        pltpu.make_async_copy(half_of(grad_ou_ref, spot.core), ou.held, local.at[0]),
+        pltpu.make_async_copy(half_of(grad_down_ref, spot.core), down.held, local.at[1]),
+    ]
+    move = Move(
+        spot,
+        row_block(y_ref, docs_ref.shape[1]),
+        lambda number: docs_ref.at[number],
+        lambda number: docs_ref.at[number],
+        move_sems,
+        local.at[2],
+    )
+
+    @pl.when(step == 0)
+    def _():
+        greet(all_partners(spot))
+        for scatter, load in zip(both, loads):
+            scatter.copy(0).start()
+            load.start()
+        move.start()
+        dk_acc[...] = jnp.zeros_like(dk_acc)
+        dv_acc[...] = jnp.zeros_like(dv_acc)
+        sums_ref[...] = jnp.zeros_like(sums_ref)
+
+    @pl.when(step == 1)
+    def _():
+        for scatter, load in zip(both, loads):
+            load.wait()
+            scatter.core_end()
+        for index in range(8):
+            for scatter in both:
+                scatter.x_step(index)
+
+    def at(when, *actions):
+        @pl.when(step == when)
+        def _():
+            for name, index in actions:
+                for scatter in both:
+                    getattr(scatter, name)(index)
+
+    at(3, ("y_step", 0))
+    at(5, ("z_step", 0), ("y_step", 1))
+    at(7, ("z_step", 1), ("y_step", 2))
+    at(9, ("z_step", 2), ("y_step", 3))
+
+    @pl.when(step < doc_steps)
+    def _():
+        def pair(number, carry):
+            spread = (step % 2) * pairs + number
+            lanes = pair_lanes(spread, head_dim)
+            dq, dk, dv, kept = attend_back(
+                q_ref[:, lanes],
+                k_ref[:, lanes],
+                v_ref[:, lanes],
+                da_ref[:, lanes],
+                mix_ref[:, lanes],
+                [prob_ref[2 * number], prob_ref[2 * number + 1]],
+                head_dim,
+            )
+            ds_ref[2 * number] = kept[0]
+            ds_ref[2 * number + 1] = kept[1]
+            dq_ref[:, lanes] = dq.astype(BFLOAT)
+            dk_acc[:, lanes] += dk
+            dv_acc[:, lanes] += dv
+            return carry
+
+        lax.fori_loop(0, pairs, pair, 0)
+
+    @pl.when(step == doc_steps - 1)
+    def _():
+        dkv_ref[:keys, :width] = dk_acc[...].astype(BFLOAT)
+        dkv_ref[:keys, width:] = dv_acc[...].astype(BFLOAT)
+
+    @pl.when(step >= doc_steps)
+    def _():
+        def part(number, carry):
+            span = pl.ds(pl.multiple_of(number * 128, 128), 128)
+            place = pl.ds(pl.multiple_of(keys + (step - doc_steps) * rows + number * 128, 16), 128)
+            for pair in range(heads // 2):
+                lanes = slice(pair * 2 * head_dim, (pair + 1) * 2 * head_dim)
+                dq, dk, dv, kept = attend_back(
+                    q_ref[span, lanes],
+                    query_k_ref[span, lanes],
+                    query_v_ref[span, lanes],
+                    da_ref[span, lanes],
+                    mix_ref[span, lanes],
+                    [query_prob_ref[2 * pair, span, :], query_prob_ref[2 * pair + 1, span, :]],
+                    head_dim,
+                )
+                ds_keep[2 * pair] = kept[0]
+                ds_keep[2 * pair + 1] = kept[1]
+                dq_ref[span, lanes] = dq.astype(BFLOAT)
+                dkv_ref[place, lanes] = dk.astype(BFLOAT)
+                dkv_ref[place, width + lanes.start : width + lanes.stop] = dv.astype(BFLOAT)
+
+            def group(index, carry):
+                some = pl.ds(pl.multiple_of(index * 16, 16), 16)
+                sums_ref[...] += bucket_products(
+                    query_bucket_ref[some, :], ds_keep[:, some, :].reshape(heads * 16, 128), labels
+                )
+                return carry
+
+            lax.fori_loop(0, 8, group, 0)
+            return carry
+
+        lax.fori_loop(0, rows // 128, part, 0)
+
+    @pl.when(step == last)
+    def _():
+        for scatter in both:
+            scatter.tail_start()
+        for scatter, out in ((ou, ou_ref), (down, down_ref)):
+            left, right = scatter.finish()
+            out[:, : scatter.half] = left
+            out[:, scatter.half :] = right
+        move.finish()
+
+
+def back(qkv, da_rows, mixture, probs, query_probs, query_buckets, grad_ou, grad_down, outputs, n_docs, labels):
+    rows, width = da_rows.shape
+    heads, doc_rows, keys = probs.shape
+    block = 256
+    doc_steps = 2 * doc_rows // block
+    doc_blocks = doc_rows // block
+    steps = doc_steps + (rows - doc_rows) // block
+    half = heads // 2
+
+    def row(i):
+        return jnp.where(i < doc_steps, i // 2, i - doc_steps + doc_blocks)
+
+    def doc(i):
+        clipped = jnp.minimum(i, doc_steps - 1)
+        return (clipped % 2, clipped // 2, 0)
+
+    def query(i):
+        return jnp.maximum(i, doc_steps) - doc_steps
+
+    anywhere = pl.BlockSpec(memory_space=pl.ANY)
+    along = pl.BlockSpec((block, width), lambda i: (row(i), 0))
+    once = pl.Buffered(1)
+    return pl.pallas_call(
+        functools.partial(back_kernel, labels, doc_steps),
+        grid=(steps,),
+        in_specs=[
+            along,
+            pl.BlockSpec((keys, width), lambda i: (0, 1), pipeline_mode=once),
+            pl.BlockSpec((keys, width), lambda i: (0, 2), pipeline_mode=once),
+            pl.BlockSpec((block, width), lambda i: (query(i) + doc_blocks, 1)),
+            pl.BlockSpec((block, width), lambda i: (query(i) + doc_blocks, 2)),
+            along,
+            along,
+            pl.BlockSpec((half, block, keys), doc),
+            pl.BlockSpec((heads, block, 128), lambda i: (0, query(i), 0)),
+            whole(query_buckets.shape),
+            anywhere,
+            anywhere,
+            anywhere,
+        ],
+        out_specs=[
+            along,
+            whole((rows, 2 * width)),
+            pl.BlockSpec((half, block, keys), doc),
+            whole((16 * labels, heads * 16)),
+            whole((grad_ou.shape[0] // 32, grad_ou.shape[1])),
+            whole((grad_down.shape[0] // 32, grad_down.shape[1])),
+            anywhere,
+        ],
+        out_shape=[
+            jax.ShapeDtypeStruct((rows, width), BFLOAT),
+            jax.ShapeDtypeStruct((rows, 2 * width), BFLOAT),
+            jax.ShapeDtypeStruct(probs.shape, BFLOAT),
+            jax.ShapeDtypeStruct((16 * labels, heads * 16), SINGLE),
+            jax.ShapeDtypeStruct((grad_ou.shape[0] // 32, grad_ou.shape[1]), SINGLE),
+            jax.ShapeDtypeStruct((grad_down.shape[0] // 32, grad_down.shape[1]), SINGLE),
+            jax.ShapeDtypeStruct((n_docs, doc_rows // n_docs, width), BFLOAT),
+        ],
+        scratch_shapes=[
+            pltpu.VMEM((keys, width), SINGLE),
+            pltpu.VMEM((keys, width), SINGLE),
+            pltpu.VMEM((heads, 128, 128), BFLOAT),
+            *scatter_scratch(*grad_ou.shape),
+            *scatter_scratch(*grad_down.shape),
+            pltpu.SemaphoreType.DMA((2, 2, COPIES)),
+            pltpu.SemaphoreType.DMA((2, 3)),
+            pltpu.SemaphoreType.DMA((3,)),
+        ],
+        compiler_params=pltpu.CompilerParams(
+            collective_id=1, has_side_effects=True, vmem_limit_bytes=VMEM_LIMIT
+        ),
+        cost_estimate=cost(70 * doc_rows * keys * width, 100 << 20),
+    )(
+        qkv,
+        qkv,
+        qkv,
+        qkv,
+        qkv,
+        da_rows,
+        mixture,
+        probs,
+        query_probs,
+        query_buckets,
+        grad_ou,
+        grad_down,
+        outputs,
+    )
+
+
+class Total:
+    def __init__(self, spot, slots, sems):
+        self.spot, self.slots, self.sems = spot, slots, sems
+
+    def rounds(self):
+        spot = self.spot
+        return (
+            (spot.core, 2, [(1, spot.partner(core=1))]),
+            (
+                spot.x * 2 + spot.y,
+                4,
+                [(1, spot.partner(y=1)), (2, spot.partner(x=1)), (3, spot.partner(x=1, y=1))],
+            ),
+            (spot.z, 4, [(k, spot.partner(z=k)) for k in (1, 2, 3)]),
+        )
+
+    def run(self, values):
+        base = 0
+        for index, (place, count, partners) in enumerate(self.rounds()):
+            mine = self.slots.at[base + place]
+            mine[...] = values
+            copies = [send(mine, mine, self.sems.at[index], k - 1, device) for k, device in partners]
+            for copy in copies:
+                copy.start()
+            for copy in copies:
+                copy.wait_recv()
+            values = self.slots[base]
+            for other in range(1, count):
+                values = values + self.slots[base + other]
+            for copy in copies:
+                copy.wait_send()
+            base += count
+        return values
+
+
+def leave_kernel(
+    labels,
+    x_ref,
+    gain_ref,
+    dq_ref,
+    dkv_ref,
+    dh_ref,
+    w_ref,
+    ds_ref,
+    bucket_ref,
+    query_sums_ref,
+    ff_ref,
+    found_ref,
+    out_ref,
+    docs_ref,
+    query_dx_ref,
+    total_ref,
+    normed,
+    away,
+    low,
+    high,
+    sums,
+    gain_sum,
+    slots,
+    *rest,
+):
+    buffers, (sems, move_sems, total_sems, local) = rest[:7], rest[7:]
+    step = pl.program_id(0)
+    last = pl.num_programs(0) - 1
+    spot = Spot()
+    rows, width = x_ref.shape
+    heads = ds_ref.shape[0]
+    doc_rows = low.shape[0]
+    block = doc_rows // 4
+    scatter = Scatter(spot, away, buffers, sems)
+    half = scatter.half
+    move = Move(
+        spot,
+        row_block(low, block),
+        lambda number: docs_ref.at[number],
+        lambda number: docs_ref.at[number],
+        move_sems,
+        local.at[0],
+    )
+    query_copy = pltpu.make_async_copy(high, query_dx_ref, local.at[1])
+
+    @pl.when(step == 0)
+    def _():
+        greet(all_partners(spot) + [spot.partner(x=1, y=1)])
+        gain = gain_ref[...]
+        sums[...] = query_sums_ref[...]
+        gain_sum[...] = jnp.zeros_like(gain_sum)
+
+        def norm_block(number, carry):
+            span = pl.ds(pl.multiple_of(number * block, 16), block)
+            values = x_ref[span, :].astype(SINGLE)
+            normed[span, :] = (values * scale_of(values) * gain).astype(BFLOAT)
+            return carry
+
+        lax.fori_loop(0, rows // block, norm_block, 0)
+
+        def product(core, into):
+            part = half // 3
+
+            for number in range(3):
+                spot_out = slice(number * part, (number + 1) * part)
+                start = core * half + number * part
+
+                def from_q():
+                    lanes = pl.ds(pl.multiple_of(start, 128), part)
+                    into[:, spot_out] = tn(normed[...], dq_ref[:, lanes]).astype(BFLOAT)
+
+                def from_kv():
+                    lanes = pl.ds(pl.multiple_of(start - width, 128), part)
+                    into[:, spot_out] = tn(normed[...], dkv_ref[:, lanes]).astype(BFLOAT)
+
+                pl.when(start < width)(from_q)
+                pl.when(start >= width)(from_kv)
+
+        product(1 - spot.core, away)
+        scatter.copy(0).start()
+        product(spot.core, scatter.held)
+        scatter.core_end()
+        for index in range(8):
+            scatter.x_step(index)
+
+        def grad_block(start, into, place):
+            span = pl.ds(pl.multiple_of(start, 16), block)
+            values = x_ref[span, :].astype(SINGLE)
+            scale = scale_of(values)
+            grad = nt(dq_ref[span, :], w_ref[:, :width])
+            grad = grad + nt(dkv_ref[span, :width], w_ref[:, width : 2 * width])
+            grad = grad + nt(dkv_ref[span, width:], w_ref[:, 2 * width :])
+            gain_sum[...] += jnp.sum(grad * values * scale, axis=0, keepdims=True)
+            dx = dh_ref[span, :] + norm_back(values, scale, grad * gain)
+            into[place, :] = dx.astype(into.dtype)
+
+        for number in range(3):
+            y, core = Move.PARTNERS[number]
+            start = spot.partner(y=y, core=core)[1] * block
+            grad_block(start, low, pl.ds(pl.multiple_of(start, 16), block))
+            move.copy(number).start()
+        start = spot.seq * block
+        grad_block(start, low, pl.ds(pl.multiple_of(start, 16), block))
+        move.own().start()
+        for number in range((rows - doc_rows) // block):
+            grad_block(
+                doc_rows + number * block, high, pl.ds(number * block, block)
+            )
+        query_copy.start()
+
+    def at(when, name, index):
+        @pl.when(step == when)
+        def _():
+            getattr(scatter, name)(index)
+
+    at(1, "y_step", 0)
+    at(2, "y_step", 1)
+    at(3, "z_step", 0)
+    at(3, "y_step", 2)
+    at(4, "z_step", 1)
+    at(4, "y_step", 3)
+    at(5, "z_step", 2)
+
+    @pl.when(step == 7)
+    def _():
+        scatter.tail_start()
+
+    @pl.when(step > 0)
+    def _():
+        def group(number, carry):
+            span = pl.ds(pl.multiple_of(number * 16, 16), 16)
+            sums[...] += bucket_products(
+                bucket_ref[span, :], ds_ref[:, span, :].reshape(heads * 16, ds_ref.shape[2]), labels
+            )
+            return carry
+
+        lax.fori_loop(0, ds_ref.shape[1] // 16, group, 0)
+
+    @pl.when(step == last)
+    def _():
+        shape = sums.shape
+        same = (
+            lax.broadcasted_iota(jnp.int32, shape, 0) // labels
+            == lax.broadcasted_iota(jnp.int32, shape, 1) % 16
+        )
+        kept = jnp.where(same, sums[...], 0.0)
+        folded = kept[:labels]
+        for index in range(1, 16):
+            folded = folded + kept[index * labels : (index + 1) * labels]
+        pick_shape = (heads * 16, 128)
+        pick = (
+            lax.broadcasted_iota(jnp.int32, pick_shape, 0) // 16
+            == lax.broadcasted_iota(jnp.int32, pick_shape, 1)
+        )
+        bias = jnp.dot(
+            folded,
+            jnp.where(pick, 1.0, 0.0),
+            preferred_element_type=SINGLE,
+            precision=lax.Precision.HIGHEST,
+        )
+        wide = width // 128
+        lines = [gain_sum[:, r * 128 : (r + 1) * 128] for r in range(wide)]
+        lines += [ff_ref[:, r * 128 : (r + 1) * 128] for r in range(wide)]
+        lines += [found_ref[...]] * (slots.shape[1] - labels - 2 * wide)
+        total_ref[...] = Total(spot, slots, total_sems).run(jnp.concatenate(lines + [bias], 0))
+        left, right = scatter.finish()
+        out_ref[:, :half] = left
+        out_ref[:, half:] = right
+        move.finish()
+        query_copy.wait()
+
+
+def leave(
+    tokens, gain, dq, dkv, grad_res, w_qkv, ds, buckets, query_sums, grad_ff, found, n_docs, labels
+):
+    rows, width = tokens.shape
+    heads, doc_rows, keys = ds.shape
+    columns = 3 * width
+    block = 128
+    lines = -(-(2 * width // 128 + 1) // 8) * 8 + labels
+    anywhere = pl.BlockSpec(memory_space=pl.ANY)
+    return pl.pallas_call(
+        functools.partial(leave_kernel, labels),
+        grid=(1 + doc_rows // block,),
+        in_specs=[
+            whole((rows, width)),
+            whole((1, width)),
+            whole((rows, width)),
+            whole((rows, 2 * width)),
+            whole((rows, width)),
+            whole(w_qkv.shape),
+            pl.BlockSpec((heads, block, keys), lambda i: (0, jnp.maximum(i - 1, 0), 0)),
+            pl.BlockSpec((block, keys), lambda i: (jnp.maximum(i - 1, 0), 0)),
+            whole(query_sums.shape),
+            whole((1, width)),
+            whole((1, 128)),
+        ],
+        out_specs=[whole((width // 32, columns)), anywhere, anywhere, whole((lines, 128))],
+        out_shape=[
+            jax.ShapeDtypeStruct((width // 32, columns), SINGLE),
+            jax.ShapeDtypeStruct((n_docs, doc_rows // n_docs, width), BFLOAT),
+            jax.ShapeDtypeStruct((rows - doc_rows, width), SINGLE),
+            jax.ShapeDtypeStruct((lines, 128), SINGLE),
+        ],
+        scratch_shapes=[
+            pltpu.VMEM((rows, width), BFLOAT),
+            pltpu.VMEM((width, columns // 2), BFLOAT),
+            pltpu.VMEM((doc_rows, width), BFLOAT),
+            pltpu.VMEM((rows - doc_rows, width), SINGLE),
+            pltpu.VMEM(query_sums.shape, SINGLE),
+            pltpu.VMEM((1, width), SINGLE),
+            pltpu.VMEM((10, lines, 128), SINGLE),
+            *scatter_scratch(width, columns),
+            pltpu.SemaphoreType.DMA((2, COPIES)),
+            pltpu.SemaphoreType.DMA((2, 3)),
+            pltpu.SemaphoreType.DMA((3, 2, 3)),
+            pltpu.SemaphoreType.DMA((2,)),
+        ],
+        compiler_params=pltpu.CompilerParams(
+            collective_id=2, has_side_effects=True, vmem_limit_bytes=VMEM_LIMIT
+        ),
+        cost_estimate=cost(12 * rows * width * width, 100 << 20),
+    )(
+        tokens,
+        gain.reshape(1, width),
+        dq,
+        dkv,
+        grad_res,
+        w_qkv,
+        ds,
+        buckets,
+        query_sums,
+        grad_ff,
+        found,
+    )
 
 
 def on_device(
@@ -795,19 +1915,14 @@
     group = max(1, seq_size // n_docs)
     local_docs = max(1, n_docs // seq_size)
     local_rows = doc_len // group
-    orders = gather_orders()
-
-    tokens = jnp.concatenate(
-        [own_document(doc_tokens), queries.reshape(query_total, width)], 0
-    )
-    w_query, w_key, w_value = gather_weights(
-        [q_weight, kv_weight[:, :width], kv_weight[:, width:]], [orders[0], orders[1], orders[0]]
-    )
-    w_keyval = jnp.concatenate([w_key, w_value], 1)
-    buckets = gather_positions(doc_buckets.astype(jnp.int16))
-    if group > 1:
-        part = lax.axis_index("seq") % group
-        buckets = lax.dynamic_slice_in_dim(buckets, part * local_rows, local_rows, 0)
+    dp_size = lax.axis_size("dp")
+    small = (dp_size, seq_size, n_docs) == (8, 4, 4) and width % 256 == 0 and shard_rows % 16 == 0
+
+    qkv_shard = jnp.concatenate([q_weight, kv_weight], 1)
+    out_up_shard = jnp.concatenate([out_weight, up_weight], 1)
+    low_buckets = doc_buckets.astype(jnp.int16)
+    flat_queries = queries.reshape(query_total, width)
+    flat_query_cot = query_cot.reshape(query_total, width)
 
     fixed = jnp.round(rel_bias.T * FIXED).astype(jnp.int32)
     packed = (fixed[0::2] << 16) | (fixed[1::2] & 0xFFFF)
@@ -818,99 +1933,152 @@
     same = jnp.kron(jnp.eye(repeats, dtype=jnp.int32), jnp.ones_like(query_buckets))
     tiled = jnp.where(same == 1, jnp.tile(query_buckets, (repeats, repeats)), bucket_count)
 
-    q_rows, kv_rows = project(tokens, attn_gain, w_query, w_keyval)
-    if group > 1:
-        teams = [list(range(t * group, (t + 1) * group)) for t in range(seq_size // group)]
-        kv_docs = lax.all_gather(
-            kv_rows[:doc_rows], "seq", axis=0, tiled=True, axis_index_groups=teams
+    if small:
+        tokens, cotangent, w_qkv, w_out_up, w_down, buckets, qkv, mixture, doc_probs, query_probs = front(
+            doc_tokens,
+            flat_queries,
+            doc_cot,
+            flat_query_cot,
+            (qkv_shard, out_up_shard, down_weight),
+            low_buckets,
+            attn_gain,
+            doc_table,
+            query_table,
+            tiled,
+            heads,
         )
     else:
+        order = gather_orders()[0]
+        w_qkv = gather_rows(qkv_shard, order)
+        w_out_up = gather_rows(out_up_shard, order)
+        w_down = gather_rows(down_weight, order)
+        tokens = jnp.concatenate([own_document(doc_tokens), flat_queries], 0)
+        cotangent = jnp.concatenate([own_document(doc_cot), flat_query_cot], 0)
+        buckets = gather_positions(low_buckets)
+        if group > 1:
+            part = lax.axis_index("seq") % group
+            buckets = lax.dynamic_slice_in_dim(buckets, part * local_rows, local_rows, 0)
+        q_rows, kv_rows = project(tokens, attn_gain, w_qkv)
         kv_docs = kv_rows
-    doc_mix, doc_probs = doc_forward(
-        q_rows, kv_docs, doc_table, buckets, local_docs, local_rows, heads
+        if group > 1:
+            teams = [list(range(t * group, (t + 1) * group)) for t in range(seq_size // group)]
+            kv_docs = lax.all_gather(
+                kv_rows[:doc_rows], "seq", axis=0, tiled=True, axis_index_groups=teams
+            )
+        doc_mix, doc_probs = doc_forward(
+            q_rows, kv_docs, doc_table, buckets, local_docs, local_rows, heads
+        )
+        query_mix, query_probs = query_forward(
+            q_rows, kv_rows, query_table, tiled, doc_rows, query_total, heads
+        )
+        mixture = jnp.concatenate([doc_mix, query_mix], 0)
+    outputs, grad_res, grad_mix, grad_out_up, grad_down, grad_ff = feed(
+        tokens, mixture, cotangent, ff_gain, w_out_up, w_down
     )
-    query_mix, query_probs = query_forward(
-        q_rows, kv_rows, query_table, tiled, doc_rows, query_total, heads
-    )
-    mixture = jnp.concatenate([doc_mix, query_mix], 0)
-    half = out_weight.shape[1] // 2
-    half_up = up_weight.shape[1] // 2
-    o1, o2, u1, u2, d1, d2 = gather_weights(
-        [
-            out_weight[:, :half],
-            out_weight[:, half:],
-            up_weight[:, :half_up],
-            up_weight[:, half_up:],
-            down_weight[:, :half],
-            down_weight[:, half:],
-        ],
-        [orders[0], orders[1]] * 3,
-    )
-    w_out = jnp.concatenate([o1, o2], 1)
-    w_up = jnp.concatenate([u1, u2], 1)
-    w_down = jnp.concatenate([d1, d2], 1)
-    cotangent = jnp.concatenate(
-        [own_document(doc_cot), query_cot.reshape(query_total, width)], 0
-    )
-    outputs, grad_res, grad_mix, grad_out, grad_up, grad_down, grad_ff = feed(
-        tokens, mixture, cotangent, ff_gain, w_out, w_up, w_down
-    )
-    grad_down_shard = scatter_columns(grad_down, 2)
-    grad_up_shard = scatter_columns(grad_up, 2)
-    grad_out_shard = scatter_columns(grad_out, 2)
-    doc_out = spread_document(outputs[:doc_rows], doc_tokens)
     query_out = outputs[doc_rows:].reshape(queries.shape)
-
-    doc_dq, doc_dk, doc_dv, doc_sums = doc_backward(
-        q_rows, kv_docs, grad_mix, doc_mix, doc_probs, buckets, local_docs, local_rows, bucket_count
-    )
-    if group > 1:
-        both = jnp.concatenate([doc_dk, doc_dv], 1)
-        both = lax.psum_scatter(
-            both, "seq", scatter_dimension=0, tiled=True, axis_index_groups=teams
-        )
-        doc_dk, doc_dv = both[:, :width], both[:, width:]
-    query_dq, query_dkv, query_sums = query_backward(
-        q_rows, kv_rows, grad_mix, mixture, query_probs, tiled, doc_rows, bucket_count
-    )
-    dq = jnp.concatenate([doc_dq, query_dq], 0)
-    dk = jnp.concatenate([doc_dk, query_dkv[:, :width]], 0)
-    dv = jnp.concatenate([doc_dv, query_dkv[:, width:]], 0)
-    grad_tokens, grad_q, grad_kv, grad_attn = unproject(
-        tokens, attn_gain, dq, dk, dv, grad_res, w_query, w_keyval
-    )
-    grad_q_shard = scatter_columns(grad_q, 2)
-    grad_kv_shard = scatter_columns(grad_kv, 2)
-    doc_dx = spread_document(grad_tokens[:doc_rows].astype(BFLOAT), doc_tokens).astype(SINGLE)
-    query_dx = grad_tokens[doc_rows:].reshape(queries.shape)
-
-    sums = (doc_sums + query_sums).reshape(16, bucket_count, heads, 16)
-    keep = jnp.eye(16, dtype=SINGLE)[:, None, None, :]
-    bias_local = jnp.sum(sums * keep, axis=(0, 3))
     matches = positives[:, :, None] == jnp.arange(doc_len, dtype=jnp.int32)[None, None, :]
     counted = jnp.arange(positives.shape[1], dtype=jnp.int32)[None, :] < pos_count[:, None]
     retrieved = jnp.sum(
         jnp.where(matches & counted[:, :, None], topk_mask[:, None, :].astype(SINGLE), 0.0)
     )
-    flat = jnp.concatenate(
-        [grad_attn[0], grad_ff[0], bias_local.reshape(-1), jnp.full((128,), retrieved)]
-    )
-    total = sum_all(flat)
-    slots = float(n_query * lax.axis_size("dp") * seq_size * positives.shape[1])
+
+    if small:
+        dq, dkv, ds, query_sums, grad_out_up_shard, grad_down_shard, doc_out = back(
+            qkv,
+            grad_mix,
+            mixture,
+            doc_probs,
+            query_probs,
+            tiled,
+            grad_out_up,
+            grad_down,
+            outputs,
+            n_docs,
+            bucket_count,
+        )
+        grad_qkv_shard, doc_dx, query_dx, total = leave(
+            tokens,
+            attn_gain,
+            dq,
+            dkv,
+            grad_res,
+            w_qkv,
+            ds,
+            buckets,
+            query_sums,
+            grad_ff,
+            jnp.full((1, 128), retrieved),
+            n_docs,
+            bucket_count,
+        )
+        lines = width // 128
+        total_attn = total[:lines].reshape(-1)
+        total_ff = total[lines : 2 * lines].reshape(-1)
+        total_found = total[2 * lines, 0]
+        total_bias = total[-bucket_count:, :heads]
+        query_dx = query_dx.reshape(queries.shape)
+    else:
+        grad_down_shard = scatter_columns(grad_down, 2)
+        grad_out_up_shard = scatter_columns(grad_out_up, 2)
+        doc_out = spread_document(outputs[:doc_rows], doc_tokens)
+        doc_dq, doc_dk, doc_dv, doc_sums = doc_backward(
+            q_rows,
+            kv_docs,
+            grad_mix,
+            doc_mix,
+            doc_probs,
+            buckets,
+            local_docs,
+            local_rows,
+            bucket_count,
+        )
+        if group > 1:
+            both = jnp.concatenate([doc_dk, doc_dv], 1)
+            both = lax.psum_scatter(
+                both, "seq", scatter_dimension=0, tiled=True, axis_index_groups=teams
+            )
+            doc_dk, doc_dv = both[:, :width], both[:, width:]
+        query_dq, query_dkv, query_sums = query_backward(
+            q_rows, kv_rows, grad_mix, mixture, query_probs, tiled, doc_rows, bucket_count
+        )
+        grad_tokens, grad_low, grad_qkv, grad_attn = unproject(
+            tokens,
+            attn_gain,
+            jnp.concatenate([doc_dq, query_dq], 0),
+            jnp.concatenate([doc_dk, query_dkv[:, :width]], 0),
+            jnp.concatenate([doc_dv, query_dkv[:, width:]], 0),
+            grad_res,
+            w_qkv,
+        )
+        grad_qkv_shard = scatter_columns(grad_qkv, 2)
+        doc_dx = spread_document(grad_low[:doc_rows], doc_tokens)
+        query_dx = grad_tokens[doc_rows:].reshape(queries.shape)
+        sums = (doc_sums + query_sums).reshape(16, bucket_count, heads, 16)
+        keep = jnp.eye(16, dtype=SINGLE)[:, None, None, :]
+        bias_local = jnp.sum(sums * keep, axis=(0, 3))
+        flat = jnp.concatenate(
+            [grad_attn[0], grad_ff[0], bias_local.reshape(-1), jnp.full((128,), retrieved)]
+        )
+        total = sum_all(flat)
+        total_attn, total_ff = total[:width], total[width : 2 * width]
+        total_bias = total[2 * width : 2 * width + bucket_count * heads]
+        total_bias = total_bias.reshape(bucket_count, heads)
+        total_found = total[-1]
+    slots = float(n_query * dp_size * seq_size * positives.shape[1])
     return (
         doc_out,
         query_out,
-        doc_dx,
+        doc_dx.astype(SINGLE),
         query_dx,
-        grad_q_shard,
-        grad_kv_shard,
-        grad_out_shard,
-        grad_up_shard,
+        grad_qkv_shard[:, :width],
+        grad_qkv_shard[:, width:],
+        grad_out_up_shard[:, :width],
+        grad_out_up_shard[:, width:],
         grad_down_shard,
-        total[:width],
-        total[width : 2 * width],
-        total[2 * width : 2 * width + bucket_count * heads].reshape(bucket_count, heads),
-        total[-1] / slots,
+        total_attn,
+        total_ff,
+        total_bias,
+        total_found / slots,
     )
 
 

time: 741 us -> 384 us (0.52)
  waiting for transfers between devices: 233 us -> 0 us
  starting transfers between devices: 115 us -> 0 us
  Pallas kernels: 246 us -> 350 us
  other arithmetic: 68 us -> 10.8 us
  local copies, waits for them, and re-layouts: 62.3 us -> 14.9 us
    ppermute x114 -> x0, waiting for transfers between devices: 233 us -> none  [the longest x102 196 us: swap(): return lax.ppermute(values, name, [(i, i ^ bit) for i in range(count)])]
    ppermute x114 -> x0, starting transfers between devices: 115 us -> none  [the longest x102 109 us: swap(): return lax.ppermute(values, name, [(i, i ^ bit) for i in range(count)])]
    pallas_call x6 -> x3, Pallas kernels: 177 us -> 281 us  [the longest x1 124 us: front(): pl.pallas_call(front_kernel, grid=(steps + 1,), in_specs=[anywhere] * 8 +...]
    select_n x81 -> x0, other arithmetic: 28.4 us -> none  [the longest x78 23.1 us: gather_rows(): jnp.where(high, jnp.stack([other, held], place), jnp.stack([held, other],...]
    dynamic_slice x19 -> x0, local copies, waits for them, and re-layouts: 21.9 us -> none  [the longest x10 9.46 us: scatter_rows(): away = lax.dynamic_index_in_dim(held, 1 - mine, place, keepdims=False)]
    concatenate x16 -> x2, other arithmetic: 20.5 us -> 2.29 us  [the longest x1 1.62 us: on_device(): out_up_shard = jnp.concatenate([out_weight, up_weight], 1)]
    unnamed x128 -> x32, local copies, waits for them, and re-layouts: 15.4 us -> 4.34 us
  transfers between devices with their start and end apart: 114 -> 0, of which waited for: 65 -> 0; matrix products, arithmetic and copies ran while one was open for 14% -> 0% of each run, Pallas kernels for 9% -> 0%
where the time goes in v3:
time: 384 us; the launch traced here: 379 us
  Pallas kernels  350 us (91%)
  local copies, waits for them, and re-layouts  14.9 us (4%)
  other arithmetic  10.8 us (3%)
    pallas_call x1, Pallas kernels, front(): pl.pallas_call(front_kernel, grid=(steps + 1,), in_specs=[anywhere] * 8 +...  124 us
    pallas_call x1, Pallas kernels, back(): pl.pallas_call(functools.partial(back_kernel, labels, doc_steps), grid=(s...  79.8 us
    pallas_call x1, Pallas kernels, leave(): pl.pallas_call(functools.partial(leave_kernel, labels), grid=(1 + doc_row...  77 us
    pallas_call x1, Pallas kernels, feed(): pl.pallas_call(functools.partial(feed_kernel, math.gcd(hidden, 768)), gri...  68.5 us

profile of v3, /device:TPU:0, one launch (start us, length us, event | category | flops | bytes accessed | tf_op | source)
XLA Modules:
  0.0 378.6 jit_solution(6335804363442190270)
XLA Ops:
  0.6 0.0 copy-start.8
  0.7 0.0 copy-start.7
  0.7 0.0 copy-start.5
  0.7 0.7 round-nearest-even_convert_fusion
  1.5 0.6 scatter.10.doc_table_ref
  2.1 0.8 broadcast_select_fusion
  2.9 0.8 select_n.11.query_bucket_ref
  3.7 1.3 reshape.173.gain_ref
  5.0 2.1 convert_element_type.24.bucket_shard
  7.0 1.6 fusion.5.ou_shard
  8.7 0.0 copy-done.7
  8.7 0.0 copy-done.5
  8.7 0.7 fusion.6.qkv_shard
  9.3 0.6 compare_reduce_fusion
  10.6 0.0 copy-done.8
  10.7 0.1 scatter.14.query_table_ref
  10.8 0.0 copy-start.10
  10.8 0.6 copy-done.10
  11.4 0.0 copy-start.11
  11.4 124.2 %shard_map.264 = (bf16[1536,768]{1,0:T(8,128)(2,1)}, bf16[1536,768]{1,0:T(8,128)(2,1)}, bf16[768,2304]{1,0:T(8,128)(2,1)}, bf16[768,3840]{1,0:T(8,128)(2,1)}, bf...) custom-call(bf16[4,256,768]{2,1,0:T(8,128)(2,1)} %docs_ref.1, ...), custom_call_target="tpu_custom_call" | custom-call | flops 5435817984 | bytes 104857600 | tf_op jit(solution)/shard_map/pallas_call | solution.py:1207
  135.6 0.0 copy-done.11
  135.6 0.6 reshape.174.gain_ref
  136.2 68.5 %shard_map.265 = (bf16[1536,768]{1,0:T(8,128)(2,1)}, f32[1536,768]{1,0:T(8,128)}, bf16[1536,768]{1,0:T(8,128)(2,1)}, bf16[768,3840]{1,0:T(8,128)(2,1)}, bf16[3072,768]{1,0:T(8,128)(2,1)}, /*index=5*/f32[1,768]{1,0:T(1,128)}) custom-call(bf16[1536,768]{1,0:T(8,128)(2,1)} %get-tuple-element.77.x_ref, bf16[1536,768]{1,0:T(8,128)(2,1)} %get-tuple-element.78.mix_ref, ...), custom_call_target="tpu_custom_call" | custom-call | flops 48922361856 | bytes 16515072 | tf_op jit(solution)/shard_map/pallas_call | solution.py:537
  204.7 0.0 copy-start.6
  204.7 0.0 copy-start.13
  204.7 0.0 copy-start.12
  204.7 79.8 %shard_map.266 = (bf16[1536,768]{1,0:T(8,128)(2,1)}, bf16[1536,1536]{1,0:T(8,128)(2,1)}, bf16[12,1024,1024]{2,1,0:T(8,128)(2,1)}, f32[512,192]{1,0:T(8,128)}, f3...) custom-call(bf16[1536,2304]{1,0:T(8,128)(2,1)} %get-tuple-element.76.q_ref.k_ref.v_ref.query_k_ref.query_v_ref, ...), custom_call_target="tpu_custom_call" | custom-call | flops 56371445760 | bytes 104857600 | tf_op jit(solution)/shard_map/pallas_call | solution.py:1549
  284.5 0.0 copy-done.6
  284.6 0.0 copy-done.13
  284.6 0.0 copy-done.12
  284.6 0.8 select_reduce_fusion
  285.4 1.2 broadcast_in_dim.35.found_ref
  286.5 77.0 %shard_map.267 = (f32[24,2304]{1,0:T(8,128)}, bf16[4,256,768]{2,1,0:T(8,128)(2,1)}, f32[512,768]{1,0:T(8,128)}, f32[48,128]{1,0:T(8,128)}) custom-call(bf16[1536,768]{1,0:T(8,128)(2,1)} %get-tuple-element.77.x_ref, f32[1,768]{1,0:T(1,128)} %reshape.173.gain_ref, bf16[1536,768]{1,0:T(8,128)(2,1)} %get-tuple-element.89.dq_ref, ...), custom_call_target="tpu_custom_call" | custom-call | flops 10871635968 | bytes 104857600 | tf_op jit(solution)/shard_map/pallas_call | solution.py:1833
  363.6 0.0 copy-start.4
  363.6 0.0 copy-start.9
  363.6 0.0 copy-start.2
  363.6 3.4 convert_element_type.28
  367.0 0.0 copy-start
  367.0 0.0 copy-done.4
  367.0 0.7 slice.92
  367.7 0.6 slice.91
  368.3 0.0 copy-done.9
  368.3 0.7 copy.32
  369.0 0.6 slice_bitcast_fusion
  369.6 0.5 slice.98
  370.8 0.0 copy-done.2
  370.8 0.7 slice.94
  371.5 0.6 slice.93
  372.1 0.0 copy-start.1
  372.1 2.2 slice.90
  374.3 0.0 copy-done
  374.3 1.1 copy.37
  375.5 0.0 copy-done.1
  375.5 0.0 copy-start.3
  375.5 1.1 copy.38
  376.6 0.0 copy-done.3
  376.6 0.7 copy.39
  (9 shorter events, 0.1 us)
Async XLA Ops:
  0.6 10.0 %copy-start.8 = (f32[32,12]{0,1:T(8,128)S(1)}, f32[32,12]{0,1:T(8,128)}, u32[]{:S(2)}) copy-start(f32[32,12]{0,1:T(8,128)} %param.34) | copy-start | bytes 4612
  0.7 8.0 %copy-start.7 = (bf16[24,768]{1,0:T(8,128)(2,1)S(1)}, bf16[24,768]{1,0:T(8,128)(2,1)}, u32[]{:S(2)}) copy-start(bf16[24,768]{1,0:T(8,128)(2,1)} %param.27) | copy-start | bytes 110596
  0.7 8.0 %copy-start.5 = (bf16[24,1536]{1,0:T(8,128)(2,1)S(1)}, bf16[24,1536]{1,0:T(8,128)(2,1)}, u32[]{:S(2)}) copy-start(bf16[24,1536]{1,0:T(8,128)(2,1)} %param.28) | copy-start | bytes 221188
  10.8 0.6 copy-start.10
  11.4 124.2 %copy-start.11 = (f32[768]{0:T(1024)S(1)}, f32[768]{0:T(1024)}, u32[]{:S(2)}) copy-start(f32[768]{0:T(1024)} %param.33) | copy-start | bytes 9220
  204.7 79.9 %copy-start.6 = (s32[16,1024]{1,0:T(8,128)S(1)}, s32[16,1024]{1,0:T(8,128)}, u32[]{:S(2)}) copy-start(s32[16,1024]{1,0:T(8,128)} %param.37) | copy-start | bytes 196612
  204.7 79.9 %copy-start.13 = (s32[16]{0:T(128)S(1)}, s32[16]{0:T(128)}, u32[]{:S(2)}) copy-start(s32[16]{0:T(128)} %param.39) | copy-start | bytes 196
  204.7 79.9 %copy-start.12 = (s32[16,4]{0,1:T(4,128)S(1)}, s32[16,4]{0,1:T(4,128)}, u32[]{:S(2)}) copy-start(s32[16,4]{0,1:T(4,128)} %param.38) | copy-start | bytes 772
  363.6 3.4 copy-start.4
  363.6 4.7 %copy-start.9 = (f32[48,128]{1,0:T(8,128)S(1)}, f32[48,128]{1,0:T(8,128)}, u32[]{:S(2)}) copy-start(f32[48,128]{1,0:T(8,128)} %get-tuple-element.102) | copy-start | bytes 73732
  363.6 7.2 %copy-start.2 = (f32[24,3840]{1,0:T(8,128)S(1)}, f32[24,3840]{1,0:T(8,128)}, u32[]{:S(2)}) copy-start(f32[24,3840]{1,0:T(8,128)} %get-tuple-element.100) | copy-start | bytes 1105924
  367.0 7.3 %copy-start = (bf16[4,256,768]{2,1,0:T(8,128)(2,1)S(1)}, bf16[4,256,768]{2,1,0:T(8,128)(2,1)}, u32[]{:S(2)}) copy-start(bf16[4,256,768]{2,1,0:T(8,128)(2,1)} %get-tuple-element.144) | copy-start | bytes 4718596
  372.1 3.3 copy-start.1
  375.5 1.1 copy-start.3
